TPU v7x, 256 devices: a whole 4x4x8 slice. The times are simulated.
256 devices in a mesh: wide: 32 (over x, z_hi, core), narrow: 8 (over y, z_lo).
Axes of the slice: x: 4, y: 4, z: 8 (z_hi: 4, z_lo: 2; z = z_hi * 2 + z_lo), core: 2. Of those that a mesh axis runs over, the one named last changes fastest.
Arguments:
- acts: float32 [2048, 6144], P(None, 'narrow'), may hold values from -6 to 6
- grads: float32 [2048, 6144], P(None, 'wide'), may hold values from -0.375 to 0.375
- basis_in: float32 [6144, 6144], P('narrow', 'wide'), may hold values from -0.078125 to 0.078125
- basis_out: float32 [6144, 6144], P('wide', 'narrow'), may hold values from -0.078125 to 0.078125
Outputs:
- moments: float32 [6144, 6144], P('narrow', 'wide')
All inputs are finite; a program needn't handle non-finite values.
Results may differ from a plain program's by a relative error of at most 0.00012.
Values sent between devices are 32-bit elements; how exact they have to be, the bound alone decides.
No kernel may reach another device: no remote copies, remote signals or barrier semaphores. Data moves between devices by JAX's collectives and lax.ppermute only.
A program may use at most 64 MiB of HBM per device.

v0:
```python
import jax
import jax.numpy as jnp
from jax import lax
from jax.sharding import PartitionSpec as P

TOK_IMG = 256
IMAGES = 8


def local(acts, grads, basis_in, basis_out):
    highest = lax.Precision.HIGHEST
    cols_in = basis_in.shape[1]
    cols_out = basis_out.shape[1]
    partial_in = jnp.dot(acts, basis_in, precision=highest, preferred_element_type=jnp.float32)
    rotated_in = lax.psum(partial_in, "narrow")
    partial_out = jnp.dot(grads, basis_out, precision=highest, preferred_element_type=jnp.float32)
    rotated_out = lax.psum(partial_out, "wide")
    tiles = jnp.einsum(
        "nti,ntj->nij",
        rotated_out.reshape(IMAGES, TOK_IMG, cols_out),
        rotated_in.reshape(IMAGES, TOK_IMG, cols_in),
        precision=highest,
    )
    return jnp.mean(tiles * tiles, axis=0)


def solution(mesh):
    placed = (P(None, "narrow"), P(None, "wide"), P("narrow", "wide"), P("wide", "narrow"))
    return jax.shard_map(
        local, mesh=mesh, in_specs=placed, out_specs=P("narrow", "wide"), check_vma=False
    )
```

profile of v0, /device:TPU:1, one launch (start us, length us, event | category | flops | bytes accessed | tf_op | source)
XLA Modules:
  0.0 441.4 jit_solution(18357483582483100756)
XLA Ops:
  6.5 0.0 copy-start
  6.5 0.0 copy-start.1
  6.5 0.0 all-reduce.5.cloned.1.call-start
  6.5 9.0 %fusion.1 = f32[2048,192]{0,1:T(8,128)S(1)} fusion(f32[2048,768]{1,0:T(8,128)} %param.4, f32[768,192]{0,1:T(8,128)} %param.6), kind=kOutput, calls=%fused_computation.4 | convolution fusion | flops 3623878656 | bytes 8454144 | tf_op jit(solution)/shard_map/dot_general | solution.py:14
  15.5 1.3 copy.8
  16.8 0.0 all-reduce.5.cloned.1.call-update
  16.8 0.0 all-reduce.3.cloned.1.call-start
  16.9 0.0 copy-done
  16.9 0.0 copy-done.1
  16.9 7.1 %fusion = f32[2048,768]{1,0:T(8,128)} fusion(f32[2048,192]{0,1:T(8,128)S(1)} %copy-done, f32[192,768]{1,0:T(8,128)S(1)} %copy-done.1), kind=kOutput, calls=%fused_computation.3 | convolution fusion | flops 3623878656 | bytes 8454144 | tf_op jit(solution)/shard_map/dot_general | solution.py:16
  24.0 0.0 all-reduce.3.cloned.1.call-update
  24.0 86.8 %all-reduce.5.cloned.1.call-done = f32[8,256,192]{1,2,0:T(8,128)} async-done(((f32[8,256,192]{1,2,0:T(8,128)}), f32[8,256,192]{1,2,0:T(8,128)}) %all-reduce.5.cloned.1.call-update) | async-done | bytes 1572880 | tf_op jit(solution)/shard_map/psum | solution.py:15
  110.8 314.5 %all-reduce.3.cloned.1.call-done = f32[8,256,768]{2,1,0:T(8,128)} async-done(((f32[8,256,768]{2,1,0:T(8,128)}), f32[8,256,768]{2,1,0:T(8,128)}) %all-reduce.3.cloned.1.call-update) | async-done | bytes 6291472 | tf_op jit(solution)/shard_map/psum | solution.py:17
  425.2 8.4 %multiply_reduce_fusion = f32[768,192]{0,1:T(8,128)S(1)} fusion(f32[8,256,768]{2,1,0:T(8,128)} %all-reduce.3.cloned.1.call-done, f32[8,256,192]{1,2,0:T(8,128)} %all-reduce.5.cloned.1.call-done), kind=kOutput, calls=%fused_computation | convolution fusion | flops 3626090496 | bytes 8454144 | tf_op jit(solution)/shard_map/nti,ntj->nij/dot_general | solution.py:18
  433.7 0.9 broadcast_multiply_fusion
Async XLA Ops:
  6.5 10.3 %copy-start = (f32[2048,192]{0,1:T(8,128)S(1)}, f32[2048,192]{0,1:T(8,128)}, u32[]{:S(2)}) copy-start(f32[2048,192]{0,1:T(8,128)} %param.5) | copy-start | bytes 4718596
  6.5 10.3 %copy-start.1 = (f32[192,768]{1,0:T(8,128)S(1)}, f32[192,768]{1,0:T(8,128)}, u32[]{:S(2)}) copy-start(f32[192,768]{1,0:T(8,128)} %param.7) | copy-start | bytes 1769476
  6.5 104.2 %all-reduce.5.cloned.1.call-start = ((), (), s32[]{:S(2)}) async-start(), calls=%async_computation.1 | async-start | bytes 3145728 | tf_op jit(solution)/shard_map/psum | solution.py:15
  16.8 408.4 %all-reduce.3.cloned.1.call-start = ((), (), s32[]{:S(2)}) async-start(), calls=%async_computation | async-start | bytes 12582912 | tf_op jit(solution)/shard_map/psum | solution.py:17
Sparse Core Ops, SparseCore 0:
  16.9 93.7 all-reduce.4
  113.4 311.7 all-reduce.2
where the time goes:
time: 442 us; the launch traced here: 441 us
  waiting for transfers between devices  401 us (91%)
  matrix products  24.5 us (6%)
  between operations  13.4 us (3%)
    psum x1, waiting for transfers between devices, local(): rotated_out = lax.psum(partial_out, 'wide')  314 us
    psum x1, waiting for transfers between devices, local(): rotated_in = lax.psum(partial_in, 'narrow')  86.8 us
    dot_general x1, matrix products, local(): jnp.dot(acts, basis_in, precision=highest, preferred_element_type=jnp.flo...  8.96 us
  transfers between devices with their start and end apart: 2, of which 2 were waited for; matrix products, arithmetic and copies ran while one was open for 2% of the time, Pallas kernels for 0%

commit v1 on v0

v1 whole, which is shorter than its diff:
```python
import functools

import jax
import jax.numpy as jnp
from jax import lax
from jax.experimental import pallas as pl
from jax.experimental.pallas import tpu as pltpu
from jax.sharding import Mesh, PartitionSpec as P

IMAGES = 8
TOK = 256
HALF, QUARTER, PIECE = 128, 64, 16
VMEM_LIMIT = 48 * 1024 * 1024

EVEN = [(0, 1), (1, 0), (2, 3), (3, 2)]
ODD = [(0, 3), (3, 0), (1, 2), (2, 1)]
SWAP = [(0, 1), (1, 0)]


def ring(k):
    return [(i, (i + k) % 4) for i in range(4)]


def split(a):
    hi = a.astype(jnp.bfloat16)
    return hi, (a - hi.astype(jnp.float32)).astype(jnp.bfloat16)


def dot3(a, b, dims):
    a_hi, a_lo = split(a)
    b_hi, b_lo = split(b)
    dot = functools.partial(
        lax.dot_general, dimension_numbers=(dims, ((), ())), preferred_element_type=jnp.float32
    )
    return dot(a_hi, b_hi) + (dot(a_hi, b_lo) + dot(a_lo, b_hi))


def place(half, quarter, zh, at):
    row = (half ^ (at // 8)) * HALF + (quarter ^ (at // 4 % 2)) * QUARTER + ((zh + at % 4) % 4) * PIECE
    return pl.multiple_of(row, PIECE)


def out_kernel(flip, pos, g_own, g_other, b_own, b_other, keep, send, whole):
    h, b, zh = pos[1], pos[2], pos[3]
    half, quarter = (b, h) if flip else (h, b)
    g = jnp.concatenate([g_own[...], g_other[...]], axis=0).T
    basis = jnp.concatenate([b_own[...], b_other[...]], axis=0)
    whole[...] = dot3(g, basis, ((1,), (0,)))
    for at in range(16):
        to = keep if at < 8 else send
        to[pl.ds(at % 8 * PIECE, PIECE), :] = whole[pl.ds(place(half, quarter, zh, at), PIECE), :]


def rotate_out(pos, image, g_own, g_other, b_own, b_other):
    feat, cols = b_own.shape
    spec = lambda: pl.BlockSpec((feat, cols), lambda i, pos: (0, 0))
    out = lambda: pl.BlockSpec((HALF, cols), lambda i, pos: (0, 0))
    return pl.pallas_call(
        functools.partial(out_kernel, image % 2 == 1),
        grid_spec=pltpu.PrefetchScalarGridSpec(
            num_scalar_prefetch=1,
            grid=(1,),
            in_specs=[
                pl.BlockSpec((feat, TOK), lambda i, pos: (0, pos[0] * 4 + image)),
                pl.BlockSpec((feat, TOK), lambda i, pos: (0, image)),
                spec(),
                spec(),
            ],
            out_specs=[out(), out()],
            scratch_shapes=[pltpu.VMEM((TOK, cols), jnp.float32)],
        ),
        out_shape=[jax.ShapeDtypeStruct((HALF, cols), jnp.float32)] * 2,
        compiler_params=pltpu.CompilerParams(vmem_limit_bytes=VMEM_LIMIT),
        cost_estimate=pl.CostEstimate(flops=6 * TOK * 2 * feat * cols, bytes_accessed=4000000, transcendentals=0),
    )(pos, g_own, g_other, b_own, b_other)


def in_kernel(pos, acts, b_own, b_other, o0, o1, o2, o3, whole):
    y = pos[4]
    basis = jnp.concatenate([b_own[...], b_other[...]], axis=0)
    whole[...] = dot3(acts[...], basis, ((1,), (1,)))
    for k, to in enumerate((o0, o1, o2, o3)):
        to[...] = whole[pl.ds(pl.multiple_of((y + k) % 4 * QUARTER, QUARTER), QUARTER), :]


def rotate_in(pos, acts, b_own, b_other):
    cols, feat = b_own.shape
    spec = lambda: pl.BlockSpec((cols, feat), lambda i, pos: (0, 0))
    return pl.pallas_call(
        in_kernel,
        grid_spec=pltpu.PrefetchScalarGridSpec(
            num_scalar_prefetch=1,
            grid=(4,),
            in_specs=[pl.BlockSpec((TOK, feat), lambda i, pos: (pos[0] * 4 + i, 0)), spec(), spec()],
            out_specs=[pl.BlockSpec((QUARTER, 2 * cols), lambda i, pos: (i, 0)) for _ in range(4)],
            scratch_shapes=[pltpu.VMEM((TOK, 2 * cols), jnp.float32)],
        ),
        out_shape=[jax.ShapeDtypeStruct((4 * QUARTER, 2 * cols), jnp.float32)] * 4,
        compiler_params=pltpu.CompilerParams(vmem_limit_bytes=VMEM_LIMIT),
        cost_estimate=pl.CostEstimate(flops=24 * TOK * 2 * feat * cols, bytes_accessed=6000000, transcendentals=0),
    )(pos, acts, b_own, b_other)


def tile_kernel(first, pos, w_a, v_a, w_b, v_b, q0, q1, q2, q3, *rest):
    if first:
        own, other, left, right = rest
    else:
        own_in, other_in, own, other, left, right = rest
    h, b, zh, y = pos[1], pos[2], pos[3], pos[4]
    total = None
    for image, (w, v) in enumerate(((w_a, v_a), (w_b, v_b))):
        half, quarter = (b, h) if image else (h, b)
        for at in range(16):
            src = w if at < 8 else v
            right[pl.ds(place(half, quarter, zh, at), PIECE), :] = src[pl.ds(at % 8 * PIECE, PIECE), :]
        for k, q in enumerate((q0, q1, q2, q3)):
            left[pl.ds(pl.multiple_of((y + k) % 4 * QUARTER, QUARTER), QUARTER), :] = q[
                pl.ds(image * QUARTER, QUARTER), :
            ]
        tile = dot3(left[...].T, right[...], ((1,), (0,)))
        total = tile * tile if total is None else total + tile * tile
    cols = own.shape[0]
    if first:
        own[...] = total[:cols]
        other[...] = total[cols:]
    else:
        own[...] = own_in[...] + total[:cols]
        other[...] = other_in[...] + total[cols:]


def tiles(pos, pair, halves, quarters, running):
    rows, cols = halves[0].shape[1], quarters[0].shape[1] // 2
    full = lambda shape: pl.BlockSpec(shape, lambda i, pos: (0, 0))
    first = running is None
    return pl.pallas_call(
        functools.partial(tile_kernel, first),
        grid_spec=pltpu.PrefetchScalarGridSpec(
            num_scalar_prefetch=1,
            grid=(1,),
            in_specs=[full((HALF, rows))] * 4
            + [pl.BlockSpec((2 * QUARTER, 2 * cols), lambda i, pos: (pair, 0))] * 4
            + ([] if first else [full((cols, rows))] * 2),
            out_specs=[full((cols, rows))] * 2,
            scratch_shapes=[pltpu.VMEM((TOK, 2 * cols), jnp.float32), pltpu.VMEM((TOK, rows), jnp.float32)],
        ),
        out_shape=[jax.ShapeDtypeStruct((cols, rows), jnp.float32)] * 2,
        compiler_params=pltpu.CompilerParams(vmem_limit_bytes=VMEM_LIMIT),
        cost_estimate=pl.CostEstimate(flops=24 * TOK * rows * cols, bytes_accessed=6000000, transcendentals=0),
    )(pos, *halves, *quarters, *(() if first else running))


def local(acts, grads, basis_in, basis_out):
    send = lax.ppermute
    x, zh, c, y = (lax.axis_index(a) for a in ("x", "zh", "c", "y"))
    h = ((x == 1) | (x == 2)).astype(jnp.int32)
    b = (x >= 2).astype(jnp.int32)
    pos = jnp.stack([c.astype(jnp.int32), h, b, zh.astype(jnp.int32), y.astype(jnp.int32)])

    grads_t, basis_in_t = grads.T, basis_in.T
    rows = grads.shape[0] // 2
    theirs = lax.dynamic_slice(grads_t, (0, (1 - c) * rows), (grads_t.shape[0], rows))
    grads_other = send(theirs, "c", SWAP)
    basis_out_other = send(basis_out, "c", SWAP)
    basis_in_other = send(basis_in_t, "c", SWAP)

    done = []
    for pair in range(2):
        steps = (EVEN, ODD), (ODD, EVEN)
        sums = []
        for image, (near, far) in zip((2 * pair, 2 * pair + 1), steps):
            keep, give = rotate_out(pos, image, grads_t, grads_other, basis_out, basis_out_other)
            s = keep + send(give, "x", near)
            s = s[:QUARTER] + send(s[QUARTER:], "x", far)
            sums.append(s)
        pieces = [
            jnp.concatenate([s[k * PIECE : (k + 1) * PIECE] for s in sums], axis=0) for k in range(4)
        ]
        total = pieces[0]
        for k in (1, 3, 2):
            total = total + send(pieces[k], "zh", ring(k))
        back = [total] + [send(total, "zh", ring(-k)) for k in (1, 2, 3)]
        halves = []
        for image, (near, far) in enumerate(steps):
            mine = jnp.concatenate([p[image * PIECE : (image + 1) * PIECE] for p in back], axis=0)
            w = jnp.concatenate([mine, send(mine, "x", far)], axis=0)
            halves += [w, send(w, "x", near)]
        done.append(halves)

    parts = rotate_in(pos, acts, basis_in_t, basis_in_other)
    total = parts[0]
    for k in (1, 3, 2):
        total = total + send(parts[k], "y", ring(k))
    total = total + send(total, "zl", SWAP)
    quarters = [total] + [send(total, "y", ring(-k)) for k in (1, 2, 3)]

    running = None
    for pair in range(2):
        running = tiles(pos, pair, done[pair], quarters, running)
    own, other = running
    return ((own + send(other, "c", SWAP)) * (1.0 / IMAGES)).T


def solution(mesh):
    axes = Mesh(mesh.devices.reshape(4, 4, 2, 4, 2), ("x", "zh", "c", "y", "zl"))
    wide, narrow = ("x", "zh", "c"), ("y", "zl")
    placed = (P(None, narrow), P(None, wide), P(narrow, wide), P(wide, narrow))
    return jax.shard_map(
        local, mesh=axes, in_specs=placed, out_specs=P(narrow, wide), check_vma=False
    )
```

time: 442 us -> 141 us (0.32)
  waiting for transfers between devices: 401 us -> 45.3 us
  starting transfers between devices: 0.04 us -> 75.9 us
  matrix products: 24.5 us -> 0 us
  Pallas kernels: 0 us -> 15.1 us
  between operations: 13.4 us -> 0.43 us
    psum x2 -> x0, waiting for transfers between devices: 401 us -> none  [the longest x1 314 us: local(): rotated_out = lax.psum(partial_out, 'wide')]
    ppermute x0 -> x39, starting transfers between devices: none -> 75.9 us  [the longest x6 20.3 us: local(): back = [total] + [send(total, 'zh', ring(-k)) for k in (1, 2, 3)]]
    ppermute x0 -> x39, waiting for transfers between devices: none -> 45.3 us  [the longest x6 8.59 us: local(): back = [total] + [send(total, 'zh', ring(-k)) for k in (1, 2, 3)]]
    dot_general x3 -> x0, matrix products: 24.5 us -> none  [the longest x1 8.96 us: local(): jnp.dot(acts, basis_in, precision=highest, preferred_element_type=jnp.flo...]
    pallas_call x0 -> x7, Pallas kernels: none -> 15.1 us  [the longest x4 5.73 us: rotate_out(): pl.pallas_call(functools.partial(out_kernel, image % 2 == 1), grid_spec=p...]
  transfers between devices with their start and end apart: 2 -> 39, of which waited for: 2 -> 21; matrix products, arithmetic and copies ran while one was open for 2% -> 2% of each run, Pallas kernels for 0% -> 9%
where the time goes in v1:
time: 141 us
  starting transfers between devices  75.9 us (54%)
  waiting for transfers between devices  45.3 us (32%)
  Pallas kernels  15.1 us (11%)
  local copies, waits for them, and re-layouts  2.5 us (2%)
  other arithmetic  1.51 us (1%)
    ppermute x6, starting transfers between devices, local(): back = [total] + [send(total, 'zh', ring(-k)) for k in (1, 2, 3)]  20.3 us
    ppermute x1, starting transfers between devices, local(): return ((own + send(other, 'c', SWAP)) * (1.0 / IMAGES)).T  15.1 us
    ppermute x6, starting transfers between devices, local(): total = total + send(pieces[k], 'zh', ring(k))  12.4 us
    ppermute x6, waiting for transfers between devices, local(): back = [total] + [send(total, 'zh', ring(-k)) for k in (1, 2, 3)]  8.59 us
    ppermute x4, waiting for transfers between devices, local(): halves += [w, send(w, 'x', near)]  8.54 us
    ppermute x3, waiting for transfers between devices, local(): total = total + send(parts[k], 'y', ring(k))  8.26 us
    ppermute x4, waiting for transfers between devices, local(): w = jnp.concatenate([mine, send(mine, 'x', far)], axis=0)  7.09 us
    ppermute x3, starting transfers between devices, local(): quarters = [total] + [send(total, 'y', ring(-k)) for k in (1, 2, 3)]  6.23 us
  transfers between devices with their start and end apart: 39, of which 21 were waited for; matrix products, arithmetic and copies ran while one was open for 2% of the time, Pallas kernels for 9%

profile of v1, /device:TPU:1, one launch (start us, length us, event | category | flops | bytes accessed | tf_op | source)
XLA Modules:
  0.0 140.8 jit_solution(5923721967054087137)
XLA Ops:
  0.0 3.2 %collective-permute-start.16 = (f32[192,768]{1,0:T(8,128)}, f32[192,768]{1,0:T(8,128)S(1)}, u32[]{:S(2)}, u32[]{:S(2)}) collective-permute-start(f32[192,768]{1,0:T(8,128)} %bitcast.15), channel_id=1, source_target_pairs={{0,8},{8,0},{1,9},{9,1},{2,10},{10,2},{3,11},{11,3},{4,12},{12,4},... | collective-permute-start | bytes 1769480 | tf_op jit(solution)/shard_map/ppermute | solution.py:164
  3.2 2.1 %dynamic-slice_bitcast_fusion = f32[192,1024]{1,0:T(8,128)} fusion(f32[2048,192]{0,1:T(8,128)} %param.5, s32[]{:T(128)S(6)} %select_n.3), kind=kLoop, calls=%fused_computation | loop fusion | bytes 1572868 | tf_op jit(solution)/shard_map/dynamic_slice | solution.py:161
  5.4 0.1 collective-permute-start
  5.5 0.4 collective-permute-start.1
  5.9 0.1 stack.31.pos
  6.0 5.4 %shard_map.48 = (f32[256,384]{1,0:T(8,128)S(1)}, f32[256,384]{1,0:T(8,128)S(1)}, f32[256,384]{1,0:T(8,128)S(1)}, f32[256,384]{1,0:T(8,128)S(1)}) custom-call(s32[5]{0:T(128)S(1)} %stack.31.pos, f32[2048,768]{1,0:T(8,128)} %acts.1, f32[192,768]{1,0:T(8,128)S(1)} %bitcast.16, f32[192,768]{1,0:T(8,128)S(1)} %collective-permute-done.16.b_other), custom_call_target="tpu_custom_call" | custom-call | flops 1811939328 | bytes 6000000 | tf_op jit(solution)/shard_map/pallas_call | solution.py:89
  11.5 2.7 %collective-permute-start.18 = (f32[256,384]{1,0:T(8,128)S(1)}, f32[256,384]{1,0:T(8,128)S(1)}, u32[]{:S(2)}, u32[]{:S(2)}) collective-permute-start(f32[256,384]{1,0:T(8,128)S(1)} %get-tuple-element.27), channel_id=1, source_target_pairs={{0,6},{2,0},{4,2},{6,4},{1,7},{3,1},{5,3},{7,5},{8,14},{10,8},{12,... | collective-permute-start | bytes 1179656 | tf_op jit(solution)/shard_map/ppermute | solution.py:192
  14.2 1.4 %shard_map.49 = (f32[128,768]{1,0:T(8,128)S(1)}, f32[128,768]{1,0:T(8,128)S(1)}) custom-call(s32[5]{0:T(128)S(1)} %stack.31.pos, f32[192,2048]{1,0:T(8,128)S(1)} %bitcast.11, f32[192,1024]{1,0:T(8,128)S(1)} %collective-permute-done.g_other, f32[192,768]{1,0:T(8,128)S(1)} %copy-done.1, f32[192,768]{1,0:T(8,128)S(1)} %collective-permute-done.1.b_other), custom_call_target="tpu_custom_call" | custom-call | flops 452984832 | bytes 4000000 | tf_op jit(solution)/shard_map/pallas_call | solution.py:58
  15.6 1.3 collective-permute-start.24
  16.9 1.4 %shard_map.50 = (f32[128,768]{1,0:T(8,128)S(1)}, f32[128,768]{1,0:T(8,128)S(1)}) custom-call(s32[5]{0:T(128)S(1)} %stack.31.pos, f32[192,2048]{1,0:T(8,128)S(1)} %bitcast.12, f32[192,1024]{1,0:T(8,128)S(1)} %collective-permute-done.g_other, f32[192,768]{1,0:T(8,128)S(1)} %copy-done.1, f32[192,768]{1,0:T(8,128)S(1)} %collective-permute-done.1.b_other), custom_call_target="tpu_custom_call" | custom-call | flops 452984832 | bytes 4000000 | tf_op jit(solution)/shard_map/pallas_call | solution.py:58
  18.3 1.9 %collective-permute-start.26 = (f32[128,768]{1,0:T(8,128)S(1)}, f32[128,768]{1,0:T(8,128)S(1)}, u32[]{:S(2)}, u32[]{:S(2)}) collective-permute-start(f32[128,768]{1,0:T(8,128)S(1)} %get-tuple-element.32), channel_id=1, source_target_pairs={{0,192},{192,0},{64,128},{128,64},{1,193},{193,1},{65,129},{129,65... | collective-permute-start | bytes 1179656 | tf_op jit(solution)/shard_map/ppermute | solution.py:172
  20.2 1.4 %shard_map.46 = (f32[128,768]{1,0:T(8,128)S(1)}, f32[128,768]{1,0:T(8,128)S(1)}) custom-call(s32[5]{0:T(128)S(1)} %stack.31.pos, f32[192,2048]{1,0:T(8,128)S(1)} %bitcast.13, f32[192,1024]{1,0:T(8,128)S(1)} %collective-permute-done.g_other, f32[192,768]{1,0:T(8,128)S(1)} %copy-done.1, f32[192,768]{1,0:T(8,128)S(1)} %collective-permute-done.1.b_other), custom_call_target="tpu_custom_call" | custom-call | flops 452984832 | bytes 4000000 | tf_op jit(solution)/shard_map/pallas_call | solution.py:58
  21.6 1.4 %shard_map.47 = (f32[128,768]{1,0:T(8,128)S(1)}, f32[128,768]{1,0:T(8,128)S(1)}) custom-call(s32[5]{0:T(128)S(1)} %stack.31.pos, f32[192,2048]{1,0:T(8,128)S(1)} %bitcast.14, f32[192,1024]{1,0:T(8,128)S(1)} %collective-permute-done.g_other, f32[192,768]{1,0:T(8,128)S(1)} %copy-done.1, f32[192,768]{1,0:T(8,128)S(1)} %collective-permute-done.1.b_other), custom_call_target="tpu_custom_call" | custom-call | flops 452984832 | bytes 4000000 | tf_op jit(solution)/shard_map/pallas_call | solution.py:58
  23.1 0.8 collective-permute-done.17
  23.8 6.7 %collective-permute-done.18 = f32[256,384]{1,0:T(8,128)S(1)} collective-permute-done((f32[256,384]{1,0:T(8,128)S(1)}, f32[256,384]{1,0:T(8,128)S(1)}, u32[]{:S(2)}, u32[]{:S(2)}) %collective-permute-start.18) | collective-permute-done | bytes 393248 | tf_op jit(solution)/shard_map/ppermute | solution.py:192
  30.6 0.8 collective-permute-done.19
  31.3 0.1 add_add_fusion
  31.4 1.6 %collective-permute-start.20 = (f32[256,384]{1,0:T(8,128)S(1)}, f32[256,384]{1,0:T(8,128)S(1)}, u32[]{:S(2)}, u32[]{:S(2)}) collective-permute-start(f32[256,384]{1,0:T(8,128)S(1)} %add_add_fusion), channel_id=1, source_target_pairs={{0,1},{1,0},{2,3},{3,2},{4,5},{5,4},{6,7},{7,6},{8,9},{9,8},{10,11... | collective-permute-start | bytes 1179656 | tf_op jit(solution)/shard_map/ppermute | solution.py:193
  33.1 2.7 %collective-permute-start.25 = (f32[64,768]{1,0:T(8,128)S(1)}, f32[64,768]{1,0:T(8,128)S(1)}, u32[]{:S(2)}, u32[]{:S(2)}) collective-permute-start(f32[64,768]{1,0:T(8,128)S(1)} %slice.181), channel_id=1, source_target_pairs={{0,192},{192,0},{64,128},{128,64},{1,193},{193,1},{65,129},{129,65... | collective-permute-start | bytes 589832 | tf_op jit(solution)/shard_map/ppermute | solution.py:173
  35.8 0.1 collective-permute-start.27
  36.0 1.0 collective-permute-start.3
  37.1 3.3 %collective-permute-done.4 = f32[128,768]{1,0:T(8,128)S(1)} collective-permute-done((f32[128,768]{1,0:T(8,128)S(1)}, f32[128,768]{1,0:T(8,128)S(1)}, u32[]{:S(2)}, u32[]{:S(2)}) %collective-permute-start.4) | collective-permute-done | bytes 393248 | tf_op jit(solution)/shard_map/ppermute | solution.py:172
  40.4 0.1 collective-permute-start.5
  40.6 4.5 %collective-permute-start.21 = (f32[256,384]{1,0:T(8,128)S(1)}, f32[256,384]{1,0:T(8,128)S(1)}, u32[]{:S(2)}, u32[]{:S(2)}) collective-permute-start(f32[256,384]{1,0:T(8,128)S(1)} %add.71.q0), channel_id=1, source_target_pairs={{0,6},{2,0},{4,2},{6,4},{1,7},{3,1},{5,3},{7,5},{8,14},{10,8},{12,... | collective-permute-start | bytes 1179656 | tf_op jit(solution)/shard_map/ppermute | solution.py:194
  45.2 1.5 %collective-permute-start.28 = (f32[32,768]{1,0:T(8,128)S(1)}, f32[32,768]{1,0:T(8,128)S(1)}, u32[]{:S(2)}, u32[]{:S(2)}) collective-permute-start(f32[32,768]{1,0:T(8,128)S(1)} %pad_maximum_fusion.7), channel_id=1, source_target_pairs={{0,16},{16,32},{32,48},{48,0},{1,17},{17,33},{33,49},{49,1},{2,18}... | collective-permute-start | bytes 294920 | tf_op jit(solution)/shard_map/ppermute | solution.py:180
  46.7 2.0 %collective-permute-done.3 = f32[64,768]{1,0:T(8,128)S(1)} collective-permute-done((f32[64,768]{1,0:T(8,128)S(1)}, f32[64,768]{1,0:T(8,128)S(1)}, u32[]{:S(2)}, u32[]{:S(2)}) %collective-permute-start.3) | collective-permute-done | bytes 196640 | tf_op jit(solution)/shard_map/ppermute | solution.py:173
  48.8 2.0 %collective-permute-start.29 = (f32[32,768]{1,0:T(8,128)S(1)}, f32[32,768]{1,0:T(8,128)S(1)}, u32[]{:S(2)}, u32[]{:S(2)}) collective-permute-start(f32[32,768]{1,0:T(8,128)S(1)} %pad_maximum_fusion.8), channel_id=1, source_target_pairs={{0,48},{16,0},{32,16},{48,32},{1,49},{17,1},{33,17},{49,33},{2,50}... | collective-permute-start | bytes 294920 | tf_op jit(solution)/shard_map/ppermute | solution.py:180
  50.9 3.3 %collective-permute-start.30 = (f32[32,768]{1,0:T(8,128)S(1)}, f32[32,768]{1,0:T(8,128)S(1)}, u32[]{:S(2)}, u32[]{:S(2)}) collective-permute-start(f32[32,768]{1,0:T(8,128)S(1)} %pad_maximum_fusion.9), channel_id=1, source_target_pairs={{0,32},{16,48},{32,0},{48,16},{1,33},{17,49},{33,1},{49,17},{2,34}... | collective-permute-start | bytes 294920 | tf_op jit(solution)/shard_map/ppermute | solution.py:180
  54.3 0.2 collective-permute-start.6
  54.5 3.4 %collective-permute-start.7 = (f32[32,768]{1,0:T(8,128)S(1)}, f32[32,768]{1,0:T(8,128)S(1)}, u32[]{:S(2)}, u32[]{:S(2)}) collective-permute-start(f32[32,768]{1,0:T(8,128)S(1)} %pad_maximum_fusion.5), channel_id=1, source_target_pairs={{0,48},{16,0},{32,16},{48,32},{1,49},{17,1},{33,17},{49,33},{2,50}... | collective-permute-start | bytes 294920 | tf_op jit(solution)/shard_map/ppermute | solution.py:180
  57.9 2.8 %collective-permute-done.30 = f32[32,768]{1,0:T(8,128)S(1)} collective-permute-done((f32[32,768]{1,0:T(8,128)S(1)}, f32[32,768]{1,0:T(8,128)S(1)}, u32[]{:S(2)}, u32[]{:S(2)}) %collective-permute-start.30) | collective-permute-done | bytes 98336 | tf_op jit(solution)/shard_map/ppermute | solution.py:180
  60.7 1.9 %collective-permute-start.8 = (f32[32,768]{1,0:T(8,128)S(1)}, f32[32,768]{1,0:T(8,128)S(1)}, u32[]{:S(2)}, u32[]{:S(2)}) collective-permute-start(f32[32,768]{1,0:T(8,128)S(1)} %pad_maximum_fusion.6), channel_id=1, source_target_pairs={{0,32},{16,48},{32,0},{48,16},{1,33},{17,49},{33,1},{49,17},{2,34}... | collective-permute-start | bytes 294920 | tf_op jit(solution)/shard_map/ppermute | solution.py:180
  62.7 1.7 %collective-permute-start.23 = (f32[256,384]{1,0:T(8,128)S(1)}, f32[256,384]{1,0:T(8,128)S(1)}, u32[]{:S(2)}, u32[]{:S(2)}) collective-permute-start(f32[256,384]{1,0:T(8,128)S(1)} %add.71.q0), channel_id=1, source_target_pairs={{0,2},{2,4},{4,6},{6,0},{1,3},{3,5},{5,7},{7,1},{8,10},{10,12},{12... | collective-permute-start | bytes 1179656 | tf_op jit(solution)/shard_map/ppermute | solution.py:194
  64.4 0.3 collective-permute-done.7
  64.8 1.8 %collective-permute-start.31 = (f32[32,768]{1,0:T(8,128)S(1)}, f32[32,768]{1,0:T(8,128)S(1)}, u32[]{:S(2)}, u32[]{:S(2)}) collective-permute-start(f32[32,768]{1,0:T(8,128)S(1)} %fusion.3), channel_id=1, source_target_pairs={{0,48},{16,0},{32,16},{48,32},{1,49},{17,1},{33,17},{49,33},{2,50}... | collective-permute-start | bytes 294920 | tf_op jit(solution)/shard_map/ppermute | solution.py:181
  66.5 2.7 %collective-permute-done.8 = f32[32,768]{1,0:T(8,128)S(1)} collective-permute-done((f32[32,768]{1,0:T(8,128)S(1)}, f32[32,768]{1,0:T(8,128)S(1)}, u32[]{:S(2)}, u32[]{:S(2)}) %collective-permute-start.8) | collective-permute-done | bytes 98336 | tf_op jit(solution)/shard_map/ppermute | solution.py:180
  69.2 3.9 %collective-permute-start.32 = (f32[32,768]{1,0:T(8,128)S(1)}, f32[32,768]{1,0:T(8,128)S(1)}, u32[]{:S(2)}, u32[]{:S(2)}) collective-permute-start(f32[32,768]{1,0:T(8,128)S(1)} %fusion.3), channel_id=1, source_target_pairs={{0,32},{16,48},{32,0},{48,16},{1,33},{17,49},{33,1},{49,17},{2,34}... | collective-permute-start | bytes 294920 | tf_op jit(solution)/shard_map/ppermute | solution.py:181
  73.2 9.3 %collective-permute-start.33 = (f32[32,768]{1,0:T(8,128)S(1)}, f32[32,768]{1,0:T(8,128)S(1)}, u32[]{:S(2)}, u32[]{:S(2)}) collective-permute-start(f32[32,768]{1,0:T(8,128)S(1)} %fusion.3), channel_id=1, source_target_pairs={{0,16},{16,32},{32,48},{48,0},{1,17},{17,33},{33,49},{49,1},{2,18}... | collective-permute-start | bytes 294920 | tf_op jit(solution)/shard_map/ppermute | solution.py:181
  82.5 0.1 collective-permute-start.9
  82.6 1.5 %collective-permute-done.33 = f32[32,768]{1,0:T(8,128)S(1)} collective-permute-done((f32[32,768]{1,0:T(8,128)S(1)}, f32[32,768]{1,0:T(8,128)S(1)}, u32[]{:S(2)}, u32[]{:S(2)}) %collective-permute-start.33) | collective-permute-done | bytes 98336 | tf_op jit(solution)/shard_map/ppermute | solution.py:181
  84.1 3.7 %collective-permute-start.10 = (f32[32,768]{1,0:T(8,128)S(1)}, f32[32,768]{1,0:T(8,128)S(1)}, u32[]{:S(2)}, u32[]{:S(2)}) collective-permute-start(f32[32,768]{1,0:T(8,128)S(1)} %fusion.1), channel_id=1, source_target_pairs={{0,32},{16,48},{32,0},{48,16},{1,33},{17,49},{33,1},{49,17},{2,34}... | collective-permute-start | bytes 294920 | tf_op jit(solution)/shard_map/ppermute | solution.py:181
  87.8 1.1 collective-permute-done.9
  88.9 1.6 %collective-permute-start.11 = (f32[32,768]{1,0:T(8,128)S(1)}, f32[32,768]{1,0:T(8,128)S(1)}, u32[]{:S(2)}, u32[]{:S(2)}) collective-permute-start(f32[32,768]{1,0:T(8,128)S(1)} %fusion.1), channel_id=1, source_target_pairs={{0,16},{16,32},{32,48},{48,0},{1,17},{17,33},{33,49},{49,1},{2,18}... | collective-permute-start | bytes 294920 | tf_op jit(solution)/shard_map/ppermute | solution.py:181
  90.6 4.7 %collective-permute-done.10 = f32[32,768]{1,0:T(8,128)S(1)} collective-permute-done((f32[32,768]{1,0:T(8,128)S(1)}, f32[32,768]{1,0:T(8,128)S(1)}, u32[]{:S(2)}, u32[]{:S(2)}) %collective-permute-start.10) | collective-permute-done | bytes 98336 | tf_op jit(solution)/shard_map/ppermute | solution.py:181
  95.3 1.3 collective-permute-done.11
  96.6 1.5 %collective-permute-start.34 = (f32[64,768]{1,0:T(8,128)S(1)}, f32[64,768]{1,0:T(8,128)S(1)}, u32[]{:S(2)}, u32[]{:S(2)}) collective-permute-start(f32[64,768]{1,0:T(8,128)S(1)} %pad_maximum_fusion.2), channel_id=1, source_target_pairs={{0,192},{192,0},{64,128},{128,64},{1,193},{193,1},{65,129},{129,65... | collective-permute-start | bytes 589832 | tf_op jit(solution)/shard_map/ppermute | solution.py:185
  98.1 1.7 %collective-permute-done.36 = f32[64,768]{1,0:T(8,128)S(1)} collective-permute-done((f32[64,768]{1,0:T(8,128)S(1)}, f32[64,768]{1,0:T(8,128)S(1)}, u32[]{:S(2)}, u32[]{:S(2)}) %collective-permute-start.36) | collective-permute-done | bytes 196640 | tf_op jit(solution)/shard_map/ppermute | solution.py:185
  99.8 0.3 collective-permute-start.14
  100.1 2.2 %collective-permute-done.34 = f32[64,768]{1,0:T(8,128)S(1)} collective-permute-done((f32[64,768]{1,0:T(8,128)S(1)}, f32[64,768]{1,0:T(8,128)S(1)}, u32[]{:S(2)}, u32[]{:S(2)}) %collective-permute-start.34) | collective-permute-done | bytes 196640 | tf_op jit(solution)/shard_map/ppermute | solution.py:185
  102.3 1.5 %collective-permute-start.12 = (f32[64,768]{1,0:T(8,128)S(1)}, f32[64,768]{1,0:T(8,128)S(1)}, u32[]{:S(2)}, u32[]{:S(2)}) collective-permute-start(f32[64,768]{1,0:T(8,128)S(1)} %pad_maximum_fusion), channel_id=1, source_target_pairs={{0,192},{192,0},{64,128},{128,64},{1,193},{193,1},{65,129},{129,65... | collective-permute-start | bytes 589832 | tf_op jit(solution)/shard_map/ppermute | solution.py:185
  103.8 0.8 collective-permute-done.14
  104.6 1.0 collective-permute-start.37
  105.7 2.4 %collective-permute-done.12 = f32[64,768]{1,0:T(8,128)S(1)} collective-permute-done((f32[64,768]{1,0:T(8,128)S(1)}, f32[64,768]{1,0:T(8,128)S(1)}, u32[]{:S(2)}, u32[]{:S(2)}) %collective-permute-start.12) | collective-permute-done | bytes 196640 | tf_op jit(solution)/shard_map/ppermute | solution.py:185
  108.1 1.7 %collective-permute-start.15 = (f32[128,768]{1,0:T(8,128)S(1)}, f32[128,768]{1,0:T(8,128)S(1)}, u32[]{:S(2)}, u32[]{:S(2)}) collective-permute-start(f32[128,768]{1,0:T(8,128)S(1)} %constant_dynamic-update-slice_fusion.5.w_b), channel_id=1, source_target_pairs={{0,192},{192,0},{64,128},{128,64},{1,193},{193,1},{65,129},{129,65... | collective-permute-start | bytes 1179656 | tf_op jit(solution)/shard_map/ppermute | solution.py:186
  109.8 0.9 collective-permute-start.13
  110.6 2.1 %collective-permute-done.37.v_b = f32[128,768]{1,0:T(8,128)S(1)} collective-permute-done((f32[128,768]{1,0:T(8,128)S(1)}, f32[128,768]{1,0:T(8,128)S(1)}, u32[]{:S(2)}, u32[]{:S(2)}) %collective-permute-start.37) | collective-permute-done | bytes 393248 | tf_op jit(solution)/shard_map/ppermute | solution.py:186
  112.8 2.8 %collective-permute-done.35.v_a = f32[128,768]{1,0:T(8,128)S(1)} collective-permute-done((f32[128,768]{1,0:T(8,128)S(1)}, f32[128,768]{1,0:T(8,128)S(1)}, u32[]{:S(2)}, u32[]{:S(2)}) %collective-permute-start.35) | collective-permute-done | bytes 393248 | tf_op jit(solution)/shard_map/ppermute | solution.py:186
  115.6 2.0 %shard_map.51 = (f32[192,768]{1,0:T(8,128)S(1)}, f32[192,768]{1,0:T(8,128)S(1)}) custom-call(s32[5]{0:T(128)S(1)} %stack.31.pos, f32[128,768]{1,0:T(8,128)S(1)} %constant_dynamic-update-slice_fusion.10.w_a, f32[128,768]{1,0:T(8,128)S(1)} %collective-permute-done.35.v_a, f32[128,768]{1,0:T(8,128)S(1)} %constant_dynamic-update-slice_fusion.15.w_b, ...), custom_call_target="tpu_custom_call" | custom-call | flops 905969664 | bytes 6000000 | tf_op jit(solution)/shard_map/pallas_call | solution.py:135
  117.6 1.2 collective-permute-done.15.v_b
  118.8 2.4 %collective-permute-done.13.v_a = f32[128,768]{1,0:T(8,128)S(1)} collective-permute-done((f32[128,768]{1,0:T(8,128)S(1)}, f32[128,768]{1,0:T(8,128)S(1)}, u32[]{:S(2)}, u32[]{:S(2)}) %collective-permute-start.13) | collective-permute-done | bytes 393248 | tf_op jit(solution)/shard_map/ppermute | solution.py:186
  121.2 2.0 %shard_map.52 = (f32[192,768]{1,0:T(8,128)S(1)}, f32[192,768]{1,0:T(8,128)S(1)}) custom-call(s32[5]{0:T(128)S(1)} %stack.31.pos, f32[128,768]{1,0:T(8,128)S(1)} %constant_dynamic-update-slice_fusion.w_a, f32[128,768]{1,0:T(8,128)S(1)} %collective-permute-done.13.v_a, f32[128,768]{1,0:T(8,128)S(1)} %constant_dynamic-update-slice_fusion.5.w_b, ...), custom_call_target="tpu_custom_call" | custom-call | flops 905969664 | bytes 6000000 | tf_op jit(solution)/shard_map/pallas_call | solution.py:135
  123.2 15.1 %collective-permute-start.38 = (f32[192,768]{1,0:T(8,128)S(1)}, f32[192,768]{1,0:T(8,128)S(1)}, u32[]{:S(2)}, u32[]{:S(2)}) collective-permute-start(f32[192,768]{1,0:T(8,128)S(1)} %get-tuple-element.36), channel_id=1, source_target_pairs={{0,8},{8,0},{1,9},{9,1},{2,10},{10,2},{3,11},{11,3},{4,12},{12,4},... | collective-permute-start | bytes 1769480 | tf_op jit(solution)/shard_map/ppermute | solution.py:200
  138.2 1.6 %collective-permute-done.38 = f32[192,768]{1,0:T(8,128)S(1)} collective-permute-done((f32[192,768]{1,0:T(8,128)S(1)}, f32[192,768]{1,0:T(8,128)S(1)}, u32[]{:S(2)}, u32[]{:S(2)}) %collective-permute-start.38) | collective-permute-done | bytes 589856 | tf_op jit(solution)/shard_map/ppermute | solution.py:200
  139.9 0.9 multiply_bitcast_fusion
  (72 shorter events, 1.0 us)
Async XLA Ops:
  0.0 6.0 %copy-start.2 = (f32[768,192]{0,1:T(8,128)S(1)}, f32[768,192]{0,1:T(8,128)}, u32[]{:S(2)}) copy-start(f32[768,192]{0,1:T(8,128)} %param.6) | copy-start | bytes 1769476
  0.0 5.5 %copy-start.1 = (f32[192,768]{1,0:T(8,128)S(1)}, f32[192,768]{1,0:T(8,128)}, u32[]{:S(2)}) copy-start(f32[192,768]{1,0:T(8,128)} %b_own.7) | copy-start | bytes 1769476
  0.0 6.0 %collective-permute-start.16 = (f32[192,768]{1,0:T(8,128)}, f32[192,768]{1,0:T(8,128)S(1)}, u32[]{:S(2)}, u32[]{:S(2)}) collective-permute-start(f32[192,768]{1,0:T(8,128)} %bitcast.15), channel_id=1, source_target_pairs={{0,8},{8,0},{1,9},{9,1},{2,10},{10,2},{3,11},{11,3},{4,12},{12,4},... | collective-permute-start | bytes 1769480 | tf_op jit(solution)/shard_map/ppermute | solution.py:164
  5.4 8.8 %collective-permute-start = (f32[192,1024]{1,0:T(8,128)}, f32[192,1024]{1,0:T(8,128)S(1)}, u32[]{:S(2)}, u32[]{:S(2)}) collective-permute-start(f32[192,1024]{1,0:T(8,128)} %dynamic-slice_bitcast_fusion), channel_id=1, source_target_pairs={{0,8},{8,0},{1,9},{9,1},{2,10},{10,2},{3,11},{11,3},{4,12},{12,4},... | collective-permute-start | bytes 2359304 | tf_op jit(solution)/shard_map/ppermute | solution.py:162
  5.5 8.7 %collective-permute-start.1 = (f32[192,768]{1,0:T(8,128)S(1)}, f32[192,768]{1,0:T(8,128)S(1)}, u32[]{:S(2)}, u32[]{:S(2)}) collective-permute-start(f32[192,768]{1,0:T(8,128)S(1)} %copy-done.1), channel_id=1, source_target_pairs={{0,8},{8,0},{1,9},{9,1},{2,10},{10,2},{3,11},{11,3},{4,12},{12,4},... | collective-permute-start | bytes 1769480 | tf_op jit(solution)/shard_map/ppermute | solution.py:163
  6.0 8.2 %copy-start = (f32[2048,192]{0,1:T(8,128)S(1)}, f32[2048,192]{0,1:T(8,128)}, u32[]{:S(2)}) copy-start(f32[2048,192]{0,1:T(8,128)} %param.5) | copy-start | bytes 4718596
  11.4 12.4 %collective-permute-start.17 = (f32[256,384]{1,0:T(8,128)S(1)}, f32[256,384]{1,0:T(8,128)S(1)}, u32[]{:S(2)}, u32[]{:S(2)}) collective-permute-start(f32[256,384]{1,0:T(8,128)S(1)} %get-tuple-element.26), channel_id=1, source_target_pairs={{0,2},{2,4},{4,6},{6,0},{1,3},{3,5},{5,7},{7,1},{8,10},{10,12},{12... | collective-permute-start | bytes 1179656 | tf_op jit(solution)/shard_map/ppermute | solution.py:192
  11.5 19.1 %collective-permute-start.18 = (f32[256,384]{1,0:T(8,128)S(1)}, f32[256,384]{1,0:T(8,128)S(1)}, u32[]{:S(2)}, u32[]{:S(2)}) collective-permute-start(f32[256,384]{1,0:T(8,128)S(1)} %get-tuple-element.27), channel_id=1, source_target_pairs={{0,6},{2,0},{4,2},{6,4},{1,7},{3,1},{5,3},{7,5},{8,14},{10,8},{12,... | collective-permute-start | bytes 1179656 | tf_op jit(solution)/shard_map/ppermute | solution.py:192
  14.2 17.2 %collective-permute-start.19 = (f32[256,384]{1,0:T(8,128)S(1)}, f32[256,384]{1,0:T(8,128)S(1)}, u32[]{:S(2)}, u32[]{:S(2)}) collective-permute-start(f32[256,384]{1,0:T(8,128)S(1)} %get-tuple-element.28), channel_id=1, source_target_pairs={{0,4},{2,6},{4,0},{6,2},{1,5},{3,7},{5,1},{7,3},{8,12},{10,14},{12... | collective-permute-start | bytes 1179656 | tf_op jit(solution)/shard_map/ppermute | solution.py:192
  15.6 17.4 %collective-permute-start.24 = (f32[128,768]{1,0:T(8,128)S(1)}, f32[128,768]{1,0:T(8,128)S(1)}, u32[]{:S(2)}, u32[]{:S(2)}) collective-permute-start(f32[128,768]{1,0:T(8,128)S(1)} %get-tuple-element.30), channel_id=1, source_target_pairs={{0,64},{64,0},{128,192},{192,128},{1,65},{65,1},{129,193},{193,129... | collective-permute-start | bytes 1179656 | tf_op jit(solution)/shard_map/ppermute | solution.py:172
  18.3 17.4 %collective-permute-start.26 = (f32[128,768]{1,0:T(8,128)S(1)}, f32[128,768]{1,0:T(8,128)S(1)}, u32[]{:S(2)}, u32[]{:S(2)}) collective-permute-start(f32[128,768]{1,0:T(8,128)S(1)} %get-tuple-element.32), channel_id=1, source_target_pairs={{0,192},{192,0},{64,128},{128,64},{1,193},{193,1},{65,129},{129,65... | collective-permute-start | bytes 1179656 | tf_op jit(solution)/shard_map/ppermute | solution.py:172
  23.8 12.1 %collective-permute-start.2 = (f32[128,768]{1,0:T(8,128)S(1)}, f32[128,768]{1,0:T(8,128)S(1)}, u32[]{:S(2)}, u32[]{:S(2)}) collective-permute-start(f32[128,768]{1,0:T(8,128)S(1)} %get-tuple-element.22), channel_id=1, source_target_pairs={{0,64},{64,0},{128,192},{192,128},{1,65},{65,1},{129,193},{193,129... | collective-permute-start | bytes 1179656 | tf_op jit(solution)/shard_map/ppermute | solution.py:172
  30.6 9.8 %collective-permute-start.4 = (f32[128,768]{1,0:T(8,128)S(1)}, f32[128,768]{1,0:T(8,128)S(1)}, u32[]{:S(2)}, u32[]{:S(2)}) collective-permute-start(f32[128,768]{1,0:T(8,128)S(1)} %get-tuple-element.24), channel_id=1, source_target_pairs={{0,192},{192,0},{64,128},{128,64},{1,193},{193,1},{65,129},{129,65... | collective-permute-start | bytes 1179656 | tf_op jit(solution)/shard_map/ppermute | solution.py:172
  31.4 9.1 %collective-permute-start.20 = (f32[256,384]{1,0:T(8,128)S(1)}, f32[256,384]{1,0:T(8,128)S(1)}, u32[]{:S(2)}, u32[]{:S(2)}) collective-permute-start(f32[256,384]{1,0:T(8,128)S(1)} %add_add_fusion), channel_id=1, source_target_pairs={{0,1},{1,0},{2,3},{3,2},{4,5},{5,4},{6,7},{7,6},{8,9},{9,8},{10,11... | collective-permute-start | bytes 1179656 | tf_op jit(solution)/shard_map/ppermute | solution.py:193
  33.1 12.0 %collective-permute-start.25 = (f32[64,768]{1,0:T(8,128)S(1)}, f32[64,768]{1,0:T(8,128)S(1)}, u32[]{:S(2)}, u32[]{:S(2)}) collective-permute-start(f32[64,768]{1,0:T(8,128)S(1)} %slice.181), channel_id=1, source_target_pairs={{0,192},{192,0},{64,128},{128,64},{1,193},{193,1},{65,129},{129,65... | collective-permute-start | bytes 589832 | tf_op jit(solution)/shard_map/ppermute | solution.py:173
  35.8 9.3 %collective-permute-start.27 = (f32[64,768]{1,0:T(8,128)S(1)}, f32[64,768]{1,0:T(8,128)S(1)}, u32[]{:S(2)}, u32[]{:S(2)}) collective-permute-start(f32[64,768]{1,0:T(8,128)S(1)} %slice.184), channel_id=1, source_target_pairs={{0,64},{64,0},{128,192},{192,128},{1,65},{65,1},{129,193},{193,129... | collective-permute-start | bytes 589832 | tf_op jit(solution)/shard_map/ppermute | solution.py:173
  36.0 12.7 %collective-permute-start.3 = (f32[64,768]{1,0:T(8,128)S(1)}, f32[64,768]{1,0:T(8,128)S(1)}, u32[]{:S(2)}, u32[]{:S(2)}) collective-permute-start(f32[64,768]{1,0:T(8,128)S(1)} %slice.161), channel_id=1, source_target_pairs={{0,192},{192,0},{64,128},{128,64},{1,193},{193,1},{65,129},{129,65... | collective-permute-start | bytes 589832 | tf_op jit(solution)/shard_map/ppermute | solution.py:173
  40.4 10.5 %collective-permute-start.5 = (f32[64,768]{1,0:T(8,128)S(1)}, f32[64,768]{1,0:T(8,128)S(1)}, u32[]{:S(2)}, u32[]{:S(2)}) collective-permute-start(f32[64,768]{1,0:T(8,128)S(1)} %slice.164), channel_id=1, source_target_pairs={{0,64},{64,0},{128,192},{192,128},{1,65},{65,1},{129,193},{193,129... | collective-permute-start | bytes 589832 | tf_op jit(solution)/shard_map/ppermute | solution.py:173
  40.6 67.5 %collective-permute-start.21 = (f32[256,384]{1,0:T(8,128)S(1)}, f32[256,384]{1,0:T(8,128)S(1)}, u32[]{:S(2)}, u32[]{:S(2)}) collective-permute-start(f32[256,384]{1,0:T(8,128)S(1)} %add.71.q0), channel_id=1, source_target_pairs={{0,6},{2,0},{4,2},{6,4},{1,7},{3,1},{5,3},{7,5},{8,14},{10,8},{12,... | collective-permute-start | bytes 1179656 | tf_op jit(solution)/shard_map/ppermute | solution.py:194
  45.1 64.7 %collective-permute-start.22 = (f32[256,384]{1,0:T(8,128)S(1)}, f32[256,384]{1,0:T(8,128)S(1)}, u32[]{:S(2)}, u32[]{:S(2)}) collective-permute-start(f32[256,384]{1,0:T(8,128)S(1)} %add.71.q0), channel_id=1, source_target_pairs={{0,4},{2,6},{4,0},{6,2},{1,5},{3,7},{5,1},{7,3},{8,12},{10,14},{12... | collective-permute-start | bytes 1179656 | tf_op jit(solution)/shard_map/ppermute | solution.py:194
  45.2 9.0 %collective-permute-start.28 = (f32[32,768]{1,0:T(8,128)S(1)}, f32[32,768]{1,0:T(8,128)S(1)}, u32[]{:S(2)}, u32[]{:S(2)}) collective-permute-start(f32[32,768]{1,0:T(8,128)S(1)} %pad_maximum_fusion.7), channel_id=1, source_target_pairs={{0,16},{16,32},{32,48},{48,0},{1,17},{17,33},{33,49},{49,1},{2,18}... | collective-permute-start | bytes 294920 | tf_op jit(solution)/shard_map/ppermute | solution.py:180
  48.8 5.7 %collective-permute-start.29 = (f32[32,768]{1,0:T(8,128)S(1)}, f32[32,768]{1,0:T(8,128)S(1)}, u32[]{:S(2)}, u32[]{:S(2)}) collective-permute-start(f32[32,768]{1,0:T(8,128)S(1)} %pad_maximum_fusion.8), channel_id=1, source_target_pairs={{0,48},{16,0},{32,16},{48,32},{1,49},{17,1},{33,17},{49,33},{2,50}... | collective-permute-start | bytes 294920 | tf_op jit(solution)/shard_map/ppermute | solution.py:180
  50.9 9.9 %collective-permute-start.30 = (f32[32,768]{1,0:T(8,128)S(1)}, f32[32,768]{1,0:T(8,128)S(1)}, u32[]{:S(2)}, u32[]{:S(2)}) collective-permute-start(f32[32,768]{1,0:T(8,128)S(1)} %pad_maximum_fusion.9), channel_id=1, source_target_pairs={{0,32},{16,48},{32,0},{48,16},{1,33},{17,49},{33,1},{49,17},{2,34}... | collective-permute-start | bytes 294920 | tf_op jit(solution)/shard_map/ppermute | solution.py:180
  54.3 8.5 %collective-permute-start.6 = (f32[32,768]{1,0:T(8,128)S(1)}, f32[32,768]{1,0:T(8,128)S(1)}, u32[]{:S(2)}, u32[]{:S(2)}) collective-permute-start(f32[32,768]{1,0:T(8,128)S(1)} %pad_maximum_fusion.4), channel_id=1, source_target_pairs={{0,16},{16,32},{32,48},{48,0},{1,17},{17,33},{33,49},{49,1},{2,18}... | collective-permute-start | bytes 294920 | tf_op jit(solution)/shard_map/ppermute | solution.py:180
  54.5 10.3 %collective-permute-start.7 = (f32[32,768]{1,0:T(8,128)S(1)}, f32[32,768]{1,0:T(8,128)S(1)}, u32[]{:S(2)}, u32[]{:S(2)}) collective-permute-start(f32[32,768]{1,0:T(8,128)S(1)} %pad_maximum_fusion.5), channel_id=1, source_target_pairs={{0,48},{16,0},{32,16},{48,32},{1,49},{17,1},{33,17},{49,33},{2,50}... | collective-permute-start | bytes 294920 | tf_op jit(solution)/shard_map/ppermute | solution.py:180
  60.7 8.5 %collective-permute-start.8 = (f32[32,768]{1,0:T(8,128)S(1)}, f32[32,768]{1,0:T(8,128)S(1)}, u32[]{:S(2)}, u32[]{:S(2)}) collective-permute-start(f32[32,768]{1,0:T(8,128)S(1)} %pad_maximum_fusion.6), channel_id=1, source_target_pairs={{0,32},{16,48},{32,0},{48,16},{1,33},{17,49},{33,1},{49,17},{2,34}... | collective-permute-start | bytes 294920 | tf_op jit(solution)/shard_map/ppermute | solution.py:180
  62.7 47.9 %collective-permute-start.23 = (f32[256,384]{1,0:T(8,128)S(1)}, f32[256,384]{1,0:T(8,128)S(1)}, u32[]{:S(2)}, u32[]{:S(2)}) collective-permute-start(f32[256,384]{1,0:T(8,128)S(1)} %add.71.q0), channel_id=1, source_target_pairs={{0,2},{2,4},{4,6},{6,0},{1,3},{3,5},{5,7},{7,1},{8,10},{10,12},{12... | collective-permute-start | bytes 1179656 | tf_op jit(solution)/shard_map/ppermute | solution.py:194
  64.8 8.4 %collective-permute-start.31 = (f32[32,768]{1,0:T(8,128)S(1)}, f32[32,768]{1,0:T(8,128)S(1)}, u32[]{:S(2)}, u32[]{:S(2)}) collective-permute-start(f32[32,768]{1,0:T(8,128)S(1)} %fusion.3), channel_id=1, source_target_pairs={{0,48},{16,0},{32,16},{48,32},{1,49},{17,1},{33,17},{49,33},{2,50}... | collective-permute-start | bytes 294920 | tf_op jit(solution)/shard_map/ppermute | solution.py:181
  69.2 13.2 %collective-permute-start.32 = (f32[32,768]{1,0:T(8,128)S(1)}, f32[32,768]{1,0:T(8,128)S(1)}, u32[]{:S(2)}, u32[]{:S(2)}) collective-permute-start(f32[32,768]{1,0:T(8,128)S(1)} %fusion.3), channel_id=1, source_target_pairs={{0,32},{16,48},{32,0},{48,16},{1,33},{17,49},{33,1},{49,17},{2,34}... | collective-permute-start | bytes 294920 | tf_op jit(solution)/shard_map/ppermute | solution.py:181
  73.2 10.9 %collective-permute-start.33 = (f32[32,768]{1,0:T(8,128)S(1)}, f32[32,768]{1,0:T(8,128)S(1)}, u32[]{:S(2)}, u32[]{:S(2)}) collective-permute-start(f32[32,768]{1,0:T(8,128)S(1)} %fusion.3), channel_id=1, source_target_pairs={{0,16},{16,32},{32,48},{48,0},{1,17},{17,33},{33,49},{49,1},{2,18}... | collective-permute-start | bytes 294920 | tf_op jit(solution)/shard_map/ppermute | solution.py:181
  82.5 6.4 %collective-permute-start.9 = (f32[32,768]{1,0:T(8,128)S(1)}, f32[32,768]{1,0:T(8,128)S(1)}, u32[]{:S(2)}, u32[]{:S(2)}) collective-permute-start(f32[32,768]{1,0:T(8,128)S(1)} %fusion.1), channel_id=1, source_target_pairs={{0,48},{16,0},{32,16},{48,32},{1,49},{17,1},{33,17},{49,33},{2,50}... | collective-permute-start | bytes 294920 | tf_op jit(solution)/shard_map/ppermute | solution.py:181
  84.1 11.2 %collective-permute-start.10 = (f32[32,768]{1,0:T(8,128)S(1)}, f32[32,768]{1,0:T(8,128)S(1)}, u32[]{:S(2)}, u32[]{:S(2)}) collective-permute-start(f32[32,768]{1,0:T(8,128)S(1)} %fusion.1), channel_id=1, source_target_pairs={{0,32},{16,48},{32,0},{48,16},{1,33},{17,49},{33,1},{49,17},{2,34}... | collective-permute-start | bytes 294920 | tf_op jit(solution)/shard_map/ppermute | solution.py:181
  88.9 7.7 %collective-permute-start.11 = (f32[32,768]{1,0:T(8,128)S(1)}, f32[32,768]{1,0:T(8,128)S(1)}, u32[]{:S(2)}, u32[]{:S(2)}) collective-permute-start(f32[32,768]{1,0:T(8,128)S(1)} %fusion.1), channel_id=1, source_target_pairs={{0,16},{16,32},{32,48},{48,0},{1,17},{17,33},{33,49},{49,1},{2,18}... | collective-permute-start | bytes 294920 | tf_op jit(solution)/shard_map/ppermute | solution.py:181
  95.3 4.5 %collective-permute-start.36 = (f32[64,768]{1,0:T(8,128)S(1)}, f32[64,768]{1,0:T(8,128)S(1)}, u32[]{:S(2)}, u32[]{:S(2)}) collective-permute-start(f32[64,768]{1,0:T(8,128)S(1)} %pad_maximum_fusion.3), channel_id=1, source_target_pairs={{0,64},{64,0},{128,192},{192,128},{1,65},{65,1},{129,193},{193,129... | collective-permute-start | bytes 589832 | tf_op jit(solution)/shard_map/ppermute | solution.py:185
  96.6 5.7 %collective-permute-start.34 = (f32[64,768]{1,0:T(8,128)S(1)}, f32[64,768]{1,0:T(8,128)S(1)}, u32[]{:S(2)}, u32[]{:S(2)}) collective-permute-start(f32[64,768]{1,0:T(8,128)S(1)} %pad_maximum_fusion.2), channel_id=1, source_target_pairs={{0,192},{192,0},{64,128},{128,64},{1,193},{193,1},{65,129},{129,65... | collective-permute-start | bytes 589832 | tf_op jit(solution)/shard_map/ppermute | solution.py:185
  99.8 4.8 %collective-permute-start.14 = (f32[64,768]{1,0:T(8,128)S(1)}, f32[64,768]{1,0:T(8,128)S(1)}, u32[]{:S(2)}, u32[]{:S(2)}) collective-permute-start(f32[64,768]{1,0:T(8,128)S(1)} %pad_maximum_fusion.1), channel_id=1, source_target_pairs={{0,64},{64,0},{128,192},{192,128},{1,65},{65,1},{129,193},{193,129... | collective-permute-start | bytes 589832 | tf_op jit(solution)/shard_map/ppermute | solution.py:185
  102.3 5.7 %collective-permute-start.12 = (f32[64,768]{1,0:T(8,128)S(1)}, f32[64,768]{1,0:T(8,128)S(1)}, u32[]{:S(2)}, u32[]{:S(2)}) collective-permute-start(f32[64,768]{1,0:T(8,128)S(1)} %pad_maximum_fusion), channel_id=1, source_target_pairs={{0,192},{192,0},{64,128},{128,64},{1,193},{193,1},{65,129},{129,65... | collective-permute-start | bytes 589832 | tf_op jit(solution)/shard_map/ppermute | solution.py:185
  104.6 8.2 %collective-permute-start.37 = (f32[128,768]{1,0:T(8,128)S(1)}, f32[128,768]{1,0:T(8,128)S(1)}, u32[]{:S(2)}, u32[]{:S(2)}) collective-permute-start(f32[128,768]{1,0:T(8,128)S(1)} %constant_dynamic-update-slice_fusion.15.w_b), channel_id=1, source_target_pairs={{0,192},{192,0},{64,128},{128,64},{1,193},{193,1},{65,129},{129,65... | collective-permute-start | bytes 1179656 | tf_op jit(solution)/shard_map/ppermute | solution.py:186
  108.0 7.6 %collective-permute-start.35 = (f32[128,768]{1,0:T(8,128)S(1)}, f32[128,768]{1,0:T(8,128)S(1)}, u32[]{:S(2)}, u32[]{:S(2)}) collective-permute-start(f32[128,768]{1,0:T(8,128)S(1)} %constant_dynamic-update-slice_fusion.10.w_a), channel_id=1, source_target_pairs={{0,64},{64,0},{128,192},{192,128},{1,65},{65,1},{129,193},{193,129... | collective-permute-start | bytes 1179656 | tf_op jit(solution)/shard_map/ppermute | solution.py:186
  108.1 10.7 %collective-permute-start.15 = (f32[128,768]{1,0:T(8,128)S(1)}, f32[128,768]{1,0:T(8,128)S(1)}, u32[]{:S(2)}, u32[]{:S(2)}) collective-permute-start(f32[128,768]{1,0:T(8,128)S(1)} %constant_dynamic-update-slice_fusion.5.w_b), channel_id=1, source_target_pairs={{0,192},{192,0},{64,128},{128,64},{1,193},{193,1},{65,129},{129,65... | collective-permute-start | bytes 1179656 | tf_op jit(solution)/shard_map/ppermute | solution.py:186
  109.8 11.4 %collective-permute-start.13 = (f32[128,768]{1,0:T(8,128)S(1)}, f32[128,768]{1,0:T(8,128)S(1)}, u32[]{:S(2)}, u32[]{:S(2)}) collective-permute-start(f32[128,768]{1,0:T(8,128)S(1)} %constant_dynamic-update-slice_fusion.w_a), channel_id=1, source_target_pairs={{0,64},{64,0},{128,192},{192,128},{1,65},{65,1},{129,193},{193,129... | collective-permute-start | bytes 1179656 | tf_op jit(solution)/shard_map/ppermute | solution.py:186
  123.2 16.7 %collective-permute-start.38 = (f32[192,768]{1,0:T(8,128)S(1)}, f32[192,768]{1,0:T(8,128)S(1)}, u32[]{:S(2)}, u32[]{:S(2)}) collective-permute-start(f32[192,768]{1,0:T(8,128)S(1)} %get-tuple-element.36), channel_id=1, source_target_pairs={{0,8},{8,0},{1,9},{9,1},{2,10},{10,2},{3,11},{11,3},{4,12},{12,4},... | collective-permute-start | bytes 1769480 | tf_op jit(solution)/shard_map/ppermute | solution.py:200

commit v2 on v1

v2 whole, which is shorter than its diff:
```python
import functools

import jax
import jax.numpy as jnp
from jax import lax
from jax.experimental import pallas as pl
from jax.experimental.pallas import tpu as pltpu
from jax.sharding import Mesh, PartitionSpec as P

IMAGES = 8
TOK = 256
PIECE = 16
VMEM_LIMIT = 48 * 1024 * 1024
SWAP = [(0, 1), (1, 0)]

CHUNKS = (((0, 1), True), ((2, 3), True))


def partner(i, bit):
    return i ^ 1 if bit else 3 - i


def swap_pairs(step, index):
    return [
        (index(i, c), index(partner(i, (step + c) % 2 == 0), c)) for i in range(4) for c in range(2)
    ]


def split(a):
    hi = a.astype(jnp.bfloat16)
    return hi, (a - hi.astype(jnp.float32)).astype(jnp.bfloat16)


def dot3(a, b, dims):
    a_hi, a_lo = split(a)
    b_hi, b_lo = split(b)
    dot = functools.partial(
        lax.dot_general, dimension_numbers=(dims, ((), ())), preferred_element_type=jnp.float32
    )
    return dot(a_hi, b_hi) + (dot(a_hi, b_lo) + dot(a_lo, b_hi))


def row(at, own, size):
    return pl.multiple_of((own ^ at) * size, size)


def out_kernel(x_first, pos, g_own, g_other, b_own, b_other, keep, send, whole):
    own = pos[1 if x_first else 2]
    g = jnp.concatenate([g_own[...], g_other[...]], axis=0).T
    basis = jnp.concatenate([b_own[...], b_other[...]], axis=0)
    whole[...] = dot3(g, basis, ((1,), (0,)))
    for at in range(16):
        to = keep if at < 8 else send
        to[0, pl.ds(at % 8 * PIECE, PIECE), :] = whole[pl.ds(row(at, own, PIECE), PIECE), :]


def rotate_out(pos, chunk, g_own, g_other, b_own, b_other):
    (images, x_first), (feat, cols) = chunk, b_own.shape
    n, first = len(images), images[0]
    spec = lambda: pl.BlockSpec((feat, cols), lambda i, pos: (0, 0))
    return pl.pallas_call(
        functools.partial(out_kernel, x_first),
        grid_spec=pltpu.PrefetchScalarGridSpec(
            num_scalar_prefetch=1,
            grid=(n,),
            in_specs=[
                pl.BlockSpec((feat, TOK), lambda i, pos: (0, pos[0] * 4 + first + i)),
                pl.BlockSpec((feat, TOK), lambda i, pos: (0, first + i)),
                spec(),
                spec(),
            ],
            out_specs=[pl.BlockSpec((1, TOK // 2, cols), lambda i, pos: (i, 0, 0))] * 2,
            scratch_shapes=[pltpu.VMEM((TOK, cols), jnp.float32)],
        ),
        out_shape=[jax.ShapeDtypeStruct((n, TOK // 2, cols), jnp.float32)] * 2,
        compiler_params=pltpu.CompilerParams(vmem_limit_bytes=VMEM_LIMIT),
        cost_estimate=pl.CostEstimate(
            flops=6 * n * TOK * 2 * feat * cols, bytes_accessed=4000000, transcendentals=0
        ),
    )(pos, g_own, g_other, b_own, b_other)


def in_kernel(pos, acts, b_own, b_other, keep, send, whole):
    own = pos[3]
    basis = jnp.concatenate([b_own[...], b_other[...]], axis=0)
    whole[...] = dot3(acts[...], basis, ((1,), (1,)))
    size = TOK // 4
    for at in range(4):
        to = keep if at < 2 else send
        to[0, pl.ds(at % 2 * size, size), :] = whole[pl.ds(row(at, own, size), size), :]


def rotate_in(pos, acts, b_own, b_other):
    cols, feat = b_own.shape
    spec = lambda: pl.BlockSpec((cols, feat), lambda i, pos: (0, 0))
    return pl.pallas_call(
        in_kernel,
        grid_spec=pltpu.PrefetchScalarGridSpec(
            num_scalar_prefetch=1,
            grid=(4,),
            in_specs=[pl.BlockSpec((TOK, feat), lambda i, pos: (pos[0] * 4 + i, 0)), spec(), spec()],
            out_specs=[pl.BlockSpec((1, TOK // 2, 2 * cols), lambda i, pos: (i, 0, 0))] * 2,
            scratch_shapes=[pltpu.VMEM((TOK, 2 * cols), jnp.float32)],
        ),
        out_shape=[jax.ShapeDtypeStruct((4, TOK // 2, 2 * cols), jnp.float32)] * 2,
        compiler_params=pltpu.CompilerParams(vmem_limit_bytes=VMEM_LIMIT),
        cost_estimate=pl.CostEstimate(flops=24 * TOK * 2 * feat * cols, bytes_accessed=6000000, transcendentals=0),
    )(pos, acts, b_own, b_other)


def tile_kernel(chunk, first, pos, w, v, q, p, *rest):
    images, x_first = chunk
    if first:
        own, other, left, right = rest
    else:
        own_in, other_in, own, other, left, right = rest
    own_out, own_y = pos[1 if x_first else 2], pos[3]
    size = TOK // 4
    total = None
    for i, image in enumerate(images):
        for at in range(16):
            src = w if at < 8 else v
            right[pl.ds(row(at, own_out, PIECE), PIECE), :] = src[i, pl.ds(at % 8 * PIECE, PIECE), :]
        for at in range(4):
            src = q if at < 2 else p
            left[pl.ds(row(at, own_y, size), size), :] = src[image, pl.ds(at % 2 * size, size), :]
        tile = dot3(left[...].T, right[...], ((1,), (0,)))
        total = tile * tile if total is None else total + tile * tile
    cols = own.shape[0]
    if first:
        own[...] = total[:cols]
        other[...] = total[cols:]
    else:
        own[...] = own_in[...] + total[:cols]
        other[...] = other_in[...] + total[cols:]


def tiles(pos, chunk, halves, quarters, running):
    rows, cols = halves[0].shape[2], quarters[0].shape[2] // 2
    full = lambda a: pl.BlockSpec(a.shape, lambda i, pos: (0,) * a.ndim)
    first = running is None
    args = (*halves, *quarters, *(() if first else running))
    out = jax.ShapeDtypeStruct((cols, rows), jnp.float32)
    return pl.pallas_call(
        functools.partial(tile_kernel, chunk, first),
        grid_spec=pltpu.PrefetchScalarGridSpec(
            num_scalar_prefetch=1,
            grid=(1,),
            in_specs=[full(a) for a in args],
            out_specs=[full(out)] * 2,
            scratch_shapes=[pltpu.VMEM((TOK, 2 * cols), jnp.float32), pltpu.VMEM((TOK, rows), jnp.float32)],
        ),
        out_shape=[out] * 2,
        compiler_params=pltpu.CompilerParams(vmem_limit_bytes=VMEM_LIMIT),
        cost_estimate=pl.CostEstimate(
            flops=12 * len(chunk[0]) * TOK * rows * cols, bytes_accessed=6000000, transcendentals=0
        ),
    )(pos, *args)


def exchange(a, axis, step):
    if axis == "y":
        return lax.ppermute(a, ("c", "y"), swap_pairs(step, lambda i, c: 4 * c + i))
    return lax.ppermute(a, (axis, "c"), swap_pairs(step, lambda i, c: 2 * i + c))


def reduced(keep, give, steps):
    for i, (axis, step) in enumerate(steps):
        got = exchange(give, axis, step)
        if i + 1 == len(steps):
            return keep + got
        half = keep.shape[1] // 2
        keep, give = keep[:, :half] + got[:, :half], keep[:, half:] + got[:, half:]


def gathered(a, steps):
    for i, (axis, step) in enumerate(reversed(steps)):
        got = exchange(a, axis, step)
        if i + 1 == len(steps):
            return a, got
        a = jnp.concatenate([a, got], axis=1)


def local(acts, grads, basis_in, basis_out):
    x, zh, c, y = (lax.axis_index(a).astype(jnp.int32) for a in ("x", "zh", "c", "y"))

    def bits(i):
        near, far = ((i == 1) | (i == 2)).astype(jnp.int32), (i >= 2).astype(jnp.int32)
        return jnp.where(c == 0, 2 * near + far, 2 * far + near)

    pos = jnp.stack([c, 4 * bits(x) + bits(zh), 4 * bits(zh) + bits(x), bits(y)])

    grads_t, basis_in_t = grads.T, basis_in.T
    rows = grads.shape[0] // 2
    basis_out_other = lax.ppermute(basis_out, "c", SWAP)
    theirs = lax.dynamic_slice(grads_t, (0, (1 - c) * rows), (grads_t.shape[0], rows))
    grads_other = lax.ppermute(theirs, "c", SWAP)
    basis_in_t, _ = lax.optimization_barrier((basis_in_t, grads_other))
    basis_in_other = lax.ppermute(basis_in_t, "c", SWAP)

    along_x, along_z = (("x", 0), ("x", 1)), (("zh", 0), ("zh", 1))
    whole = []
    for chunk in CHUNKS:
        steps = along_x + along_z if chunk[1] else along_z + along_x
        keep, give = rotate_out(pos, chunk, grads_t, grads_other, basis_out, basis_out_other)
        whole.append(gathered(reduced(keep, give, steps), steps))

    along_y = (("y", 0), ("y", 1))
    keep, give = rotate_in(pos, acts, basis_in_t, basis_in_other)
    total = reduced(keep, give, along_y)
    total = total + lax.ppermute(total, "zl", SWAP)
    quarters = gathered(total, along_y)

    running = None
    for chunk, halves in zip(CHUNKS, whole):
        running = tiles(pos, chunk, halves, quarters, running)
    own, other = running
    return ((own + lax.ppermute(other, "c", SWAP)) * (1.0 / IMAGES)).T


def solution(mesh):
    axes = Mesh(mesh.devices.reshape(4, 4, 2, 4, 2), ("x", "zh", "c", "y", "zl"))
    wide, narrow = ("x", "zh", "c"), ("y", "zl")
    placed = (P(None, narrow), P(None, wide), P(narrow, wide), P(wide, narrow))
    return jax.shard_map(
        local, mesh=axes, in_specs=placed, out_specs=P(narrow, wide), check_vma=False
    )
```

time: 141 us -> 119 us (0.84)
  starting transfers between devices: 75.9 us -> 42.7 us
  waiting for transfers between devices: 45.3 us -> 55.7 us
    ppermute x39 -> x25, starting transfers between devices: 75.9 us -> 42.7 us  [the longest x16 22.6 us: exchange(): lax.ppermute(a, (axis, 'c'), swap_pairs(step, lambda i, c: 2 * i + c))]
    ppermute x39 -> x25, waiting for transfers between devices: 45.3 us -> 55.7 us  [the longest x16 44 us: exchange(): lax.ppermute(a, (axis, 'c'), swap_pairs(step, lambda i, c: 2 * i + c))]
    pallas_call x6 -> x4, Pallas kernels: 9.68 us -> 8.89 us  [the longest x2 4.96 us: rotate_out(): pl.pallas_call(functools.partial(out_kernel, x_first), grid_spec=pltpu.Pr...]
  transfers between devices with their start and end apart: 39 -> 25, of which waited for: 21 -> 16; matrix products, arithmetic and copies ran while one was open for 2% -> 1% of each run, Pallas kernels for 9% -> 8%
where the time goes in v2:
time: 119 us; the launch traced here: 118 us
  waiting for transfers between devices  55.7 us (47%)
  starting transfers between devices  42.7 us (36%)
  Pallas kernels  14.4 us (12%)
  local copies, waits for them, and re-layouts  3.29 us (3%)
  other arithmetic  1.67 us (1%)
    ppermute x16, waiting for transfers between devices, exchange(): lax.ppermute(a, (axis, 'c'), swap_pairs(step, lambda i, c: 2 * i + c))  44 us
    ppermute x16, starting transfers between devices, exchange(): lax.ppermute(a, (axis, 'c'), swap_pairs(step, lambda i, c: 2 * i + c))  22.6 us
    ppermute x4, starting transfers between devices, exchange(): return lax.ppermute(a, ('c', 'y'), swap_pairs(step, lambda i, c: 4 * c + i))  9.47 us
    ppermute x1, starting transfers between devices, local(): return ((own + lax.ppermute(other, 'c', SWAP)) * (1.0 / IMAGES)).T  5.79 us
    pallas_call x1, Pallas kernels, rotate_in(): pl.pallas_call(in_kernel, grid_spec=pltpu.PrefetchScalarGridSpec(num_scal...  5.49 us
    pallas_call x2, Pallas kernels, rotate_out(): pl.pallas_call(functools.partial(out_kernel, x_first), grid_spec=pltpu.Pr...  4.96 us
    ppermute x4, waiting for transfers between devices, exchange(): return lax.ppermute(a, ('c', 'y'), swap_pairs(step, lambda i, c: 4 * c + i))  4.36 us
    pallas_call x2, Pallas kernels, tiles(): pl.pallas_call(functools.partial(tile_kernel, chunk, first), grid_spec=pl...  3.93 us
  transfers between devices with their start and end apart: 25, of which 16 were waited for; matrix products, arithmetic and copies ran while one was open for 1% of the time, Pallas kernels for 8%

profile of v2, /device:TPU:1, one launch (start us, length us, event | category | flops | bytes accessed | tf_op | source)
XLA Modules:
  0.0 117.9 jit_solution(13557437876561155092)
XLA Ops:
  0.0 2.2 %dynamic-slice_bitcast_fusion = f32[192,1024]{1,0:T(8,128)} fusion(f32[2048,192]{0,1:T(8,128)} %param.5, s32[]{:T(128)S(6)} %select_n.18), kind=kLoop, calls=%fused_computation.3 | loop fusion | bytes 1572868 | tf_op jit(solution)/shard_map/dynamic_slice | solution.py:196
  2.2 3.2 %collective-permute-start = (f32[192,1024]{1,0:T(8,128)}, f32[192,1024]{1,0:T(8,128)S(1)}, u32[]{:S(2)}, u32[]{:S(2)}) collective-permute-start(f32[192,1024]{1,0:T(8,128)} %dynamic-slice_bitcast_fusion), channel_id=1, source_target_pairs={{0,8},{8,0},{1,9},{9,1},{2,10},{10,2},{3,11},{11,3},{4,12},{12,4},... | collective-permute-start | bytes 2359304 | tf_op jit(solution)/shard_map/ppermute | solution.py:197
  5.5 0.0 collective-permute-start.1
  5.5 0.1 pad_add_fusion.pos
  5.5 2.9 %collective-permute-done.1.b_other = f32[192,768]{1,0:T(8,128)S(1)} collective-permute-done((f32[192,768]{1,0:T(8,128)}, f32[192,768]{1,0:T(8,128)S(1)}, u32[]{:S(2)}, u32[]{:S(2)}) %collective-permute-start.1) | collective-permute-done | bytes 589856 | tf_op jit(solution)/shard_map/ppermute | solution.py:195
  8.4 0.0 collective-permute-done.g_other
  8.4 1.1 copy-done.1
  9.5 2.5 %shard_map.48 = (f32[2,128,768]{2,1,0:T(8,128)S(1)}, f32[2,128,768]{2,1,0:T(8,128)S(1)}) custom-call(s32[4]{0:T(128)S(1)} %pad_add_fusion.pos, f32[192,2048]{1,0:T(8,128)S(1)} %bitcast.10, f32[192,1024]{1,0:T(8,128)S(1)} %collective-permute-done.g_other, f32[192,768]{1,0:T(8,128)S(1)} %copy-done.1, f32[192,768]{1,0:T(8,128)S(1)} %collective-permute-done.1.b_other), custom_call_target="tpu_custom_call" | custom-call | flops 905969664 | bytes 4000000 | tf_op jit(solution)/shard_map/pallas_call | solution.py:61
  12.0 0.8 collective-permute-start.16
  12.8 0.0 collective-permute-start.10
  12.8 2.5 %shard_map.46 = (f32[2,128,768]{2,1,0:T(8,128)S(1)}, f32[2,128,768]{2,1,0:T(8,128)S(1)}) custom-call(s32[4]{0:T(128)S(1)} %pad_add_fusion.pos, f32[192,2048]{1,0:T(8,128)S(1)} %bitcast.11, f32[192,1024]{1,0:T(8,128)S(1)} %collective-permute-done.g_other, f32[192,768]{1,0:T(8,128)S(1)} %copy-done.1, f32[192,768]{1,0:T(8,128)S(1)} %collective-permute-done.1.b_other), custom_call_target="tpu_custom_call" | custom-call | flops 905969664 | bytes 4000000 | tf_op jit(solution)/shard_map/pallas_call | solution.py:61
  15.3 2.0 %collective-permute-start.2 = (f32[2,128,768]{2,1,0:T(8,128)S(1)}, f32[2,128,768]{2,1,0:T(8,128)S(1)}, u32[]{:S(2)}, u32[]{:S(2)}) collective-permute-start(f32[2,128,768]{2,1,0:T(8,128)S(1)} %get-tuple-element.17), channel_id=1, source_target_pairs={{0,64},{8,200},{64,0},{72,136},{128,192},{136,72},{192,128},{200,8... | collective-permute-start | bytes 2359304 | tf_op jit(solution)/shard_map/ppermute | solution.py:164
  17.3 0.0 collective-permute-done.10.b_other
  17.3 5.5 %shard_map.47 = (f32[4,128,384]{2,1,0:T(8,128)S(1)}, f32[4,128,384]{2,1,0:T(8,128)S(1)}) custom-call(s32[4]{0:T(128)S(1)} %pad_add_fusion.pos, f32[2048,768]{1,0:T(8,128)} %acts.1, f32[192,768]{1,0:T(8,128)S(1)} %bitcast.13, f32[192,768]{1,0:T(8,128)S(1)} %collective-permute-done.10.b_other), custom_call_target="tpu_custom_call" | custom-call | flops 1811939328 | bytes 6000000 | tf_op jit(solution)/shard_map/pallas_call | solution.py:96
  22.8 2.1 %collective-permute-start.11 = (f32[4,128,384]{2,1,0:T(8,128)S(1)}, f32[4,128,384]{2,1,0:T(8,128)S(1)}, u32[]{:S(2)}, u32[]{:S(2)}) collective-permute-start(f32[4,128,384]{2,1,0:T(8,128)S(1)} %get-tuple-element.20), channel_id=1, source_target_pairs={{0,2},{8,14},{2,0},{10,12},{4,6},{12,10},{6,4},{14,8},{1,3},{9,15}... | collective-permute-start | bytes 2359304 | tf_op jit(solution)/shard_map/ppermute | solution.py:163
  24.9 0.0 collective-permute-done.16
  24.9 0.1 slice_add_fusion.1
  25.0 0.4 collective-permute-start.17
  25.4 11.2 %collective-permute-done.2 = f32[2,128,768]{2,1,0:T(8,128)S(1)} collective-permute-done((f32[2,128,768]{2,1,0:T(8,128)S(1)}, f32[2,128,768]{2,1,0:T(8,128)S(1)}, u32[]{:S(2)}, u32[]{:S(2)}) %collective-permute-start.2) | collective-permute-done | bytes 786464 | tf_op jit(solution)/shard_map/ppermute | solution.py:164
  36.6 0.1 slice_add_fusion.5
  36.7 0.1 collective-permute-start.3
  36.8 0.0 collective-permute-done.17
  36.9 4.2 %collective-permute-start.18 = (f32[2,32,768]{2,1,0:T(8,128)S(1)}, f32[2,32,768]{2,1,0:T(8,128)S(1)}, u32[]{:S(2)}, u32[]{:S(2)}) collective-permute-start(f32[2,32,768]{2,1,0:T(8,128)S(1)} %get-tuple-element.32), channel_id=1, source_target_pairs={{0,16},{8,56},{16,0},{24,40},{32,48},{40,24},{48,32},{56,8},{1,17}... | collective-permute-start | bytes 589832 | tf_op jit(solution)/shard_map/ppermute | solution.py:164
  41.1 2.6 %collective-permute-done.3 = f32[2,64,768]{2,1,0:T(8,128)S(1)} collective-permute-done((f32[2,64,768]{2,1,0:T(8,128)S(1)}, f32[2,64,768]{2,1,0:T(8,128)S(1)}, u32[]{:S(2)}, u32[]{:S(2)}) %collective-permute-start.3) | collective-permute-done | bytes 393248 | tf_op jit(solution)/shard_map/ppermute | solution.py:164
  43.8 3.8 %collective-permute-start.4 = (f32[2,32,768]{2,1,0:T(8,128)S(1)}, f32[2,32,768]{2,1,0:T(8,128)S(1)}, u32[]{:S(2)}, u32[]{:S(2)}) collective-permute-start(f32[2,32,768]{2,1,0:T(8,128)S(1)} %get-tuple-element.34), channel_id=1, source_target_pairs={{0,16},{8,56},{16,0},{24,40},{32,48},{40,24},{48,32},{56,8},{1,17}... | collective-permute-start | bytes 589832 | tf_op jit(solution)/shard_map/ppermute | solution.py:164
  47.6 0.0 collective-permute-done.11
  47.6 2.0 %collective-permute-start.12 = (f32[4,64,384]{2,1,0:T(8,128)S(1)}, f32[4,64,384]{2,1,0:T(8,128)S(1)}, u32[]{:S(2)}, u32[]{:S(2)}) collective-permute-start(f32[4,64,384]{2,1,0:T(8,128)S(1)} %slice_add_fusion.2), channel_id=1, source_target_pairs={{0,6},{8,10},{2,4},{10,8},{4,2},{12,14},{6,0},{14,12},{1,7},{9,11}... | collective-permute-start | bytes 1179656 | tf_op jit(solution)/shard_map/ppermute | solution.py:163
  49.6 0.0 collective-permute-done.18
  49.6 1.2 %collective-permute-start.19 = (f32[2,16,768]{2,1,0:T(8,128)S(1)}, f32[2,16,768]{2,1,0:T(8,128)S(1)}, u32[]{:S(2)}, u32[]{:S(2)}) collective-permute-start(f32[2,16,768]{2,1,0:T(8,128)S(1)} %slice_add_fusion.10), channel_id=1, source_target_pairs={{0,48},{8,24},{16,32},{24,8},{32,16},{40,56},{48,0},{56,40},{1,49}... | collective-permute-start | bytes 294920 | tf_op jit(solution)/shard_map/ppermute | solution.py:164
  50.9 1.4 %collective-permute-done.4 = f32[2,32,768]{2,1,0:T(8,128)S(1)} collective-permute-done((f32[2,32,768]{2,1,0:T(8,128)S(1)}, f32[2,32,768]{2,1,0:T(8,128)S(1)}, u32[]{:S(2)}, u32[]{:S(2)}) %collective-permute-start.4) | collective-permute-done | bytes 196640 | tf_op jit(solution)/shard_map/ppermute | solution.py:164
  52.3 0.7 collective-permute-start.5
  53.0 3.4 %collective-permute-done.19 = f32[2,16,768]{2,1,0:T(8,128)S(1)} collective-permute-done((f32[2,16,768]{2,1,0:T(8,128)S(1)}, f32[2,16,768]{2,1,0:T(8,128)S(1)}, u32[]{:S(2)}, u32[]{:S(2)}) %collective-permute-start.19) | collective-permute-done | bytes 98336 | tf_op jit(solution)/shard_map/ppermute | solution.py:164
  56.5 0.1 collective-permute-start.20
  56.6 1.9 %collective-permute-done.5 = f32[2,16,768]{2,1,0:T(8,128)S(1)} collective-permute-done((f32[2,16,768]{2,1,0:T(8,128)S(1)}, f32[2,16,768]{2,1,0:T(8,128)S(1)}, u32[]{:S(2)}, u32[]{:S(2)}) %collective-permute-start.5) | collective-permute-done | bytes 98336 | tf_op jit(solution)/shard_map/ppermute | solution.py:164
  58.5 0.6 collective-permute-start.6
  59.0 3.2 %collective-permute-done.20 = f32[2,16,768]{2,1,0:T(8,128)S(1)} collective-permute-done((f32[2,16,768]{2,1,0:T(8,128)S(1)}, f32[2,16,768]{2,1,0:T(8,128)S(1)}, u32[]{:S(2)}, u32[]{:S(2)}) %collective-permute-start.20) | collective-permute-done | bytes 98336 | tf_op jit(solution)/shard_map/ppermute | solution.py:164
  62.3 0.9 collective-permute-start.21
  63.2 0.0 collective-permute-done.12
  63.2 0.1 fusion
  63.2 1.6 %collective-permute-start.13 = (f32[4,64,384]{2,1,0:T(8,128)S(1)}, f32[4,64,384]{2,1,0:T(8,128)S(1)}, u32[]{:S(2)}, u32[]{:S(2)}) collective-permute-start(f32[4,64,384]{2,1,0:T(8,128)S(1)} %fusion), channel_id=1, source_target_pairs={{0,1},{1,0},{2,3},{3,2},{4,5},{5,4},{6,7},{7,6},{8,9},{9,8},{10,11... | collective-permute-start | bytes 1179656 | tf_op jit(solution)/shard_map/ppermute | solution.py:211
  64.8 0.0 collective-permute-done.6
  64.9 1.8 %collective-permute-start.7 = (f32[2,32,768]{2,1,0:T(8,128)S(1)}, f32[2,32,768]{2,1,0:T(8,128)S(1)}, u32[]{:S(2)}, u32[]{:S(2)}) collective-permute-start(f32[2,32,768]{2,1,0:T(8,128)S(1)} %pad_maximum_fusion.5), channel_id=1, source_target_pairs={{0,16},{8,56},{16,0},{24,40},{32,48},{40,24},{48,32},{56,8},{1,17}... | collective-permute-start | bytes 589832 | tf_op jit(solution)/shard_map/ppermute | solution.py:164
  66.6 4.5 %collective-permute-done.21 = f32[2,32,768]{2,1,0:T(8,128)S(1)} collective-permute-done((f32[2,32,768]{2,1,0:T(8,128)S(1)}, f32[2,32,768]{2,1,0:T(8,128)S(1)}, u32[]{:S(2)}, u32[]{:S(2)}) %collective-permute-start.21) | collective-permute-done | bytes 196640 | tf_op jit(solution)/shard_map/ppermute | solution.py:164
  71.2 1.0 collective-permute-start.22
  72.2 2.8 %collective-permute-done.13 = f32[4,64,384]{2,1,0:T(8,128)S(1)} collective-permute-done((f32[4,64,384]{2,1,0:T(8,128)S(1)}, f32[4,64,384]{2,1,0:T(8,128)S(1)}, u32[]{:S(2)}, u32[]{:S(2)}) %collective-permute-start.13) | collective-permute-done | bytes 393248 | tf_op jit(solution)/shard_map/ppermute | solution.py:211
  75.1 3.4 %collective-permute-start.14 = (f32[4,64,384]{2,1,0:T(8,128)S(1)}, f32[4,64,384]{2,1,0:T(8,128)S(1)}, u32[]{:S(2)}, u32[]{:S(2)}) collective-permute-start(f32[4,64,384]{2,1,0:T(8,128)S(1)} %add.107), channel_id=1, source_target_pairs={{0,6},{8,10},{2,4},{10,8},{4,2},{12,14},{6,0},{14,12},{1,7},{9,11}... | collective-permute-start | bytes 1179656 | tf_op jit(solution)/shard_map/ppermute | solution.py:163
  78.5 0.7 collective-permute-done.7
  79.3 0.1 collective-permute-start.8
  79.4 0.1 pad_maximum_fusion.2.w
  79.5 2.6 %collective-permute-start.23 = (f32[2,128,768]{2,1,0:T(8,128)S(1)}, f32[2,128,768]{2,1,0:T(8,128)S(1)}, u32[]{:S(2)}, u32[]{:S(2)}) collective-permute-start(f32[2,128,768]{2,1,0:T(8,128)S(1)} %pad_maximum_fusion.2.w), channel_id=1, source_target_pairs={{0,64},{8,200},{64,0},{72,136},{128,192},{136,72},{192,128},{200,8... | collective-permute-start | bytes 2359304 | tf_op jit(solution)/shard_map/ppermute | solution.py:164
  82.1 1.9 %collective-permute-done.14 = f32[4,64,384]{2,1,0:T(8,128)S(1)} collective-permute-done((f32[4,64,384]{2,1,0:T(8,128)S(1)}, f32[4,64,384]{2,1,0:T(8,128)S(1)}, u32[]{:S(2)}, u32[]{:S(2)}) %collective-permute-start.14) | collective-permute-done | bytes 393248 | tf_op jit(solution)/shard_map/ppermute | solution.py:163
  84.0 0.1 pad_maximum_fusion.1.q
  84.0 2.0 %collective-permute-start.15 = (f32[4,128,384]{2,1,0:T(8,128)S(1)}, f32[4,128,384]{2,1,0:T(8,128)S(1)}, u32[]{:S(2)}, u32[]{:S(2)}) collective-permute-start(f32[4,128,384]{2,1,0:T(8,128)S(1)} %pad_maximum_fusion.1.q), channel_id=1, source_target_pairs={{0,2},{8,14},{2,0},{10,12},{4,6},{12,10},{6,4},{14,8},{1,3},{9,15}... | collective-permute-start | bytes 2359304 | tf_op jit(solution)/shard_map/ppermute | solution.py:163
  86.0 0.3 collective-permute-done.8
  86.3 0.1 pad_maximum_fusion.w
  86.3 2.2 %collective-permute-start.9 = (f32[2,128,768]{2,1,0:T(8,128)S(1)}, f32[2,128,768]{2,1,0:T(8,128)S(1)}, u32[]{:S(2)}, u32[]{:S(2)}) collective-permute-start(f32[2,128,768]{2,1,0:T(8,128)S(1)} %pad_maximum_fusion.w), channel_id=1, source_target_pairs={{0,64},{8,200},{64,0},{72,136},{128,192},{136,72},{192,128},{200,8... | collective-permute-start | bytes 2359304 | tf_op jit(solution)/shard_map/ppermute | solution.py:164
  88.6 9.6 %collective-permute-done.23.v = f32[2,128,768]{2,1,0:T(8,128)S(1)} collective-permute-done((f32[2,128,768]{2,1,0:T(8,128)S(1)}, f32[2,128,768]{2,1,0:T(8,128)S(1)}, u32[]{:S(2)}, u32[]{:S(2)}) %collective-permute-start.23) | collective-permute-done | bytes 786464 | tf_op jit(solution)/shard_map/ppermute | solution.py:164
  98.2 2.5 %collective-permute-done.15.p = f32[4,128,384]{2,1,0:T(8,128)S(1)} collective-permute-done((f32[4,128,384]{2,1,0:T(8,128)S(1)}, f32[4,128,384]{2,1,0:T(8,128)S(1)}, u32[]{:S(2)}, u32[]{:S(2)}) %collective-permute-start.15) | collective-permute-done | bytes 786464 | tf_op jit(solution)/shard_map/ppermute | solution.py:163
  100.7 2.0 %shard_map.49 = (f32[192,768]{1,0:T(8,128)S(1)}, f32[192,768]{1,0:T(8,128)S(1)}) custom-call(s32[4]{0:T(128)S(1)} %pad_add_fusion.pos, f32[2,128,768]{2,1,0:T(8,128)S(1)} %pad_maximum_fusion.2.w, f32[2,128,768]{2,1,0:T(8,128)S(1)} %collective-permute-done.23.v, f32[4,128,384]{2,1,0:T(8,128)S(1)} %pad_maximum_fusion.1.q, ...), custom_call_target="tpu_custom_call" | custom-call | flops 905969664 | bytes 6000000 | tf_op jit(solution)/shard_map/pallas_call | solution.py:144
  102.6 5.0 %collective-permute-done.9.v = f32[2,128,768]{2,1,0:T(8,128)S(1)} collective-permute-done((f32[2,128,768]{2,1,0:T(8,128)S(1)}, f32[2,128,768]{2,1,0:T(8,128)S(1)}, u32[]{:S(2)}, u32[]{:S(2)}) %collective-permute-start.9) | collective-permute-done | bytes 786464 | tf_op jit(solution)/shard_map/ppermute | solution.py:164
  107.6 2.0 %shard_map.50 = (f32[192,768]{1,0:T(8,128)S(1)}, f32[192,768]{1,0:T(8,128)S(1)}) custom-call(s32[4]{0:T(128)S(1)} %pad_add_fusion.pos, f32[2,128,768]{2,1,0:T(8,128)S(1)} %pad_maximum_fusion.w, f32[2,128,768]{2,1,0:T(8,128)S(1)} %collective-permute-done.9.v, f32[4,128,384]{2,1,0:T(8,128)S(1)} %pad_maximum_fusion.1.q, ...), custom_call_target="tpu_custom_call" | custom-call | flops 905969664 | bytes 6000000 | tf_op jit(solution)/shard_map/pallas_call | solution.py:144
  109.6 5.8 %collective-permute-start.24 = (f32[192,768]{1,0:T(8,128)S(1)}, f32[192,768]{1,0:T(8,128)S(1)}, u32[]{:S(2)}, u32[]{:S(2)}) collective-permute-start(f32[192,768]{1,0:T(8,128)S(1)} %get-tuple-element.26), channel_id=1, source_target_pairs={{0,8},{8,0},{1,9},{9,1},{2,10},{10,2},{3,11},{11,3},{4,12},{12,4},... | collective-permute-start | bytes 1769480 | tf_op jit(solution)/shard_map/ppermute | solution.py:218
  115.4 1.6 %collective-permute-done.24 = f32[192,768]{1,0:T(8,128)S(1)} collective-permute-done((f32[192,768]{1,0:T(8,128)S(1)}, f32[192,768]{1,0:T(8,128)S(1)}, u32[]{:S(2)}, u32[]{:S(2)}) %collective-permute-start.24) | collective-permute-done | bytes 589856 | tf_op jit(solution)/shard_map/ppermute | solution.py:218
  117.0 0.9 multiply_bitcast_fusion
  (18 shorter events, 0.3 us)
Async XLA Ops:
  0.0 8.4 %copy-start = (f32[2048,192]{0,1:T(8,128)S(1)}, f32[2048,192]{0,1:T(8,128)}, u32[]{:S(2)}) copy-start(f32[2048,192]{0,1:T(8,128)} %param.5) | copy-start | bytes 4718596
  2.2 6.2 %collective-permute-start = (f32[192,1024]{1,0:T(8,128)}, f32[192,1024]{1,0:T(8,128)S(1)}, u32[]{:S(2)}, u32[]{:S(2)}) collective-permute-start(f32[192,1024]{1,0:T(8,128)} %dynamic-slice_bitcast_fusion), channel_id=1, source_target_pairs={{0,8},{8,0},{1,9},{9,1},{2,10},{10,2},{3,11},{11,3},{4,12},{12,4},... | collective-permute-start | bytes 2359304 | tf_op jit(solution)/shard_map/ppermute | solution.py:197
  5.5 3.0 %collective-permute-start.1 = (f32[192,768]{1,0:T(8,128)}, f32[192,768]{1,0:T(8,128)S(1)}, u32[]{:S(2)}, u32[]{:S(2)}) collective-permute-start(f32[192,768]{1,0:T(8,128)} %b_own.3), channel_id=1, source_target_pairs={{0,8},{8,0},{1,9},{9,1},{2,10},{10,2},{3,11},{11,3},{4,12},{12,4},... | collective-permute-start | bytes 1769480 | tf_op jit(solution)/shard_map/ppermute | solution.py:195
  8.4 1.1 copy-start.1
  9.5 3.3 %copy-start.2 = (f32[768,192]{0,1:T(8,128)S(1)}, f32[768,192]{0,1:T(8,128)}, u32[]{:S(2)}) copy-start(f32[768,192]{0,1:T(8,128)} %param.6) | copy-start | bytes 1769476
  12.0 12.9 %collective-permute-start.16 = (f32[2,128,768]{2,1,0:T(8,128)S(1)}, f32[2,128,768]{2,1,0:T(8,128)S(1)}, u32[]{:S(2)}, u32[]{:S(2)}) collective-permute-start(f32[2,128,768]{2,1,0:T(8,128)S(1)} %get-tuple-element.22), channel_id=1, source_target_pairs={{0,64},{8,200},{64,0},{72,136},{128,192},{136,72},{192,128},{200,8... | collective-permute-start | bytes 2359304 | tf_op jit(solution)/shard_map/ppermute | solution.py:164
  12.8 4.5 %collective-permute-start.10 = (f32[192,768]{1,0:T(8,128)S(1)}, f32[192,768]{1,0:T(8,128)S(1)}, u32[]{:S(2)}, u32[]{:S(2)}) collective-permute-start(f32[192,768]{1,0:T(8,128)S(1)} %bitcast.12), channel_id=1, source_target_pairs={{0,8},{8,0},{1,9},{9,1},{2,10},{10,2},{3,11},{11,3},{4,12},{12,4},... | collective-permute-start | bytes 1769480 | tf_op jit(solution)/shard_map/ppermute | solution.py:199
  15.3 21.3 %collective-permute-start.2 = (f32[2,128,768]{2,1,0:T(8,128)S(1)}, f32[2,128,768]{2,1,0:T(8,128)S(1)}, u32[]{:S(2)}, u32[]{:S(2)}) collective-permute-start(f32[2,128,768]{2,1,0:T(8,128)S(1)} %get-tuple-element.17), channel_id=1, source_target_pairs={{0,64},{8,200},{64,0},{72,136},{128,192},{136,72},{192,128},{200,8... | collective-permute-start | bytes 2359304 | tf_op jit(solution)/shard_map/ppermute | solution.py:164
  22.8 24.7 %collective-permute-start.11 = (f32[4,128,384]{2,1,0:T(8,128)S(1)}, f32[4,128,384]{2,1,0:T(8,128)S(1)}, u32[]{:S(2)}, u32[]{:S(2)}) collective-permute-start(f32[4,128,384]{2,1,0:T(8,128)S(1)} %get-tuple-element.20), channel_id=1, source_target_pairs={{0,2},{8,14},{2,0},{10,12},{4,6},{12,10},{6,4},{14,8},{1,3},{9,15}... | collective-permute-start | bytes 2359304 | tf_op jit(solution)/shard_map/ppermute | solution.py:163
  25.0 11.8 %collective-permute-start.17 = (f32[2,64,768]{2,1,0:T(8,128)S(1)}, f32[2,64,768]{2,1,0:T(8,128)S(1)}, u32[]{:S(2)}, u32[]{:S(2)}) collective-permute-start(f32[2,64,768]{2,1,0:T(8,128)S(1)} %get-tuple-element.28), channel_id=1, source_target_pairs={{0,192},{8,72},{64,128},{72,8},{128,64},{136,200},{192,0},{200,136... | collective-permute-start | bytes 1179656 | tf_op jit(solution)/shard_map/ppermute | solution.py:164
  36.7 7.0 %collective-permute-start.3 = (f32[2,64,768]{2,1,0:T(8,128)S(1)}, f32[2,64,768]{2,1,0:T(8,128)S(1)}, u32[]{:S(2)}, u32[]{:S(2)}) collective-permute-start(f32[2,64,768]{2,1,0:T(8,128)S(1)} %get-tuple-element.30), channel_id=1, source_target_pairs={{0,192},{8,72},{64,128},{72,8},{128,64},{136,200},{192,0},{200,136... | collective-permute-start | bytes 1179656 | tf_op jit(solution)/shard_map/ppermute | solution.py:164
  36.9 12.7 %collective-permute-start.18 = (f32[2,32,768]{2,1,0:T(8,128)S(1)}, f32[2,32,768]{2,1,0:T(8,128)S(1)}, u32[]{:S(2)}, u32[]{:S(2)}) collective-permute-start(f32[2,32,768]{2,1,0:T(8,128)S(1)} %get-tuple-element.32), channel_id=1, source_target_pairs={{0,16},{8,56},{16,0},{24,40},{32,48},{40,24},{48,32},{56,8},{1,17}... | collective-permute-start | bytes 589832 | tf_op jit(solution)/shard_map/ppermute | solution.py:164
  43.8 8.5 %collective-permute-start.4 = (f32[2,32,768]{2,1,0:T(8,128)S(1)}, f32[2,32,768]{2,1,0:T(8,128)S(1)}, u32[]{:S(2)}, u32[]{:S(2)}) collective-permute-start(f32[2,32,768]{2,1,0:T(8,128)S(1)} %get-tuple-element.34), channel_id=1, source_target_pairs={{0,16},{8,56},{16,0},{24,40},{32,48},{40,24},{48,32},{56,8},{1,17}... | collective-permute-start | bytes 589832 | tf_op jit(solution)/shard_map/ppermute | solution.py:164
  47.6 15.5 %collective-permute-start.12 = (f32[4,64,384]{2,1,0:T(8,128)S(1)}, f32[4,64,384]{2,1,0:T(8,128)S(1)}, u32[]{:S(2)}, u32[]{:S(2)}) collective-permute-start(f32[4,64,384]{2,1,0:T(8,128)S(1)} %slice_add_fusion.2), channel_id=1, source_target_pairs={{0,6},{8,10},{2,4},{10,8},{4,2},{12,14},{6,0},{14,12},{1,7},{9,11}... | collective-permute-start | bytes 1179656 | tf_op jit(solution)/shard_map/ppermute | solution.py:163
  49.6 6.8 %collective-permute-start.19 = (f32[2,16,768]{2,1,0:T(8,128)S(1)}, f32[2,16,768]{2,1,0:T(8,128)S(1)}, u32[]{:S(2)}, u32[]{:S(2)}) collective-permute-start(f32[2,16,768]{2,1,0:T(8,128)S(1)} %slice_add_fusion.10), channel_id=1, source_target_pairs={{0,48},{8,24},{16,32},{24,8},{32,16},{40,56},{48,0},{56,40},{1,49}... | collective-permute-start | bytes 294920 | tf_op jit(solution)/shard_map/ppermute | solution.py:164
  52.3 6.2 %collective-permute-start.5 = (f32[2,16,768]{2,1,0:T(8,128)S(1)}, f32[2,16,768]{2,1,0:T(8,128)S(1)}, u32[]{:S(2)}, u32[]{:S(2)}) collective-permute-start(f32[2,16,768]{2,1,0:T(8,128)S(1)} %slice_add_fusion.12), channel_id=1, source_target_pairs={{0,48},{8,24},{16,32},{24,8},{32,16},{40,56},{48,0},{56,40},{1,49}... | collective-permute-start | bytes 294920 | tf_op jit(solution)/shard_map/ppermute | solution.py:164
  56.5 5.8 %collective-permute-start.20 = (f32[2,16,768]{2,1,0:T(8,128)S(1)}, f32[2,16,768]{2,1,0:T(8,128)S(1)}, u32[]{:S(2)}, u32[]{:S(2)}) collective-permute-start(f32[2,16,768]{2,1,0:T(8,128)S(1)} %fusion.1), channel_id=1, source_target_pairs={{0,48},{8,24},{16,32},{24,8},{32,16},{40,56},{48,0},{56,40},{1,49}... | collective-permute-start | bytes 294920 | tf_op jit(solution)/shard_map/ppermute | solution.py:164
  58.5 6.4 %collective-permute-start.6 = (f32[2,16,768]{2,1,0:T(8,128)S(1)}, f32[2,16,768]{2,1,0:T(8,128)S(1)}, u32[]{:S(2)}, u32[]{:S(2)}) collective-permute-start(f32[2,16,768]{2,1,0:T(8,128)S(1)} %fusion.2), channel_id=1, source_target_pairs={{0,48},{8,24},{16,32},{24,8},{32,16},{40,56},{48,0},{56,40},{1,49}... | collective-permute-start | bytes 294920 | tf_op jit(solution)/shard_map/ppermute | solution.py:164
  62.3 8.9 %collective-permute-start.21 = (f32[2,32,768]{2,1,0:T(8,128)S(1)}, f32[2,32,768]{2,1,0:T(8,128)S(1)}, u32[]{:S(2)}, u32[]{:S(2)}) collective-permute-start(f32[2,32,768]{2,1,0:T(8,128)S(1)} %pad_maximum_fusion.6), channel_id=1, source_target_pairs={{0,16},{8,56},{16,0},{24,40},{32,48},{40,24},{48,32},{56,8},{1,17}... | collective-permute-start | bytes 589832 | tf_op jit(solution)/shard_map/ppermute | solution.py:164
  63.2 11.8 %collective-permute-start.13 = (f32[4,64,384]{2,1,0:T(8,128)S(1)}, f32[4,64,384]{2,1,0:T(8,128)S(1)}, u32[]{:S(2)}, u32[]{:S(2)}) collective-permute-start(f32[4,64,384]{2,1,0:T(8,128)S(1)} %fusion), channel_id=1, source_target_pairs={{0,1},{1,0},{2,3},{3,2},{4,5},{5,4},{6,7},{7,6},{8,9},{9,8},{10,11... | collective-permute-start | bytes 1179656 | tf_op jit(solution)/shard_map/ppermute | solution.py:211
  64.9 14.4 %collective-permute-start.7 = (f32[2,32,768]{2,1,0:T(8,128)S(1)}, f32[2,32,768]{2,1,0:T(8,128)S(1)}, u32[]{:S(2)}, u32[]{:S(2)}) collective-permute-start(f32[2,32,768]{2,1,0:T(8,128)S(1)} %pad_maximum_fusion.5), channel_id=1, source_target_pairs={{0,16},{8,56},{16,0},{24,40},{32,48},{40,24},{48,32},{56,8},{1,17}... | collective-permute-start | bytes 589832 | tf_op jit(solution)/shard_map/ppermute | solution.py:164
  71.2 8.2 %collective-permute-start.22 = (f32[2,64,768]{2,1,0:T(8,128)S(1)}, f32[2,64,768]{2,1,0:T(8,128)S(1)}, u32[]{:S(2)}, u32[]{:S(2)}) collective-permute-start(f32[2,64,768]{2,1,0:T(8,128)S(1)} %pad_maximum_fusion.4), channel_id=1, source_target_pairs={{0,192},{8,72},{64,128},{72,8},{128,64},{136,200},{192,0},{200,136... | collective-permute-start | bytes 1179656 | tf_op jit(solution)/shard_map/ppermute | solution.py:164
  75.1 8.9 %collective-permute-start.14 = (f32[4,64,384]{2,1,0:T(8,128)S(1)}, f32[4,64,384]{2,1,0:T(8,128)S(1)}, u32[]{:S(2)}, u32[]{:S(2)}) collective-permute-start(f32[4,64,384]{2,1,0:T(8,128)S(1)} %add.107), channel_id=1, source_target_pairs={{0,6},{8,10},{2,4},{10,8},{4,2},{12,14},{6,0},{14,12},{1,7},{9,11}... | collective-permute-start | bytes 1179656 | tf_op jit(solution)/shard_map/ppermute | solution.py:163
  79.3 7.0 %collective-permute-start.8 = (f32[2,64,768]{2,1,0:T(8,128)S(1)}, f32[2,64,768]{2,1,0:T(8,128)S(1)}, u32[]{:S(2)}, u32[]{:S(2)}) collective-permute-start(f32[2,64,768]{2,1,0:T(8,128)S(1)} %pad_maximum_fusion.3), channel_id=1, source_target_pairs={{0,192},{8,72},{64,128},{72,8},{128,64},{136,200},{192,0},{200,136... | collective-permute-start | bytes 1179656 | tf_op jit(solution)/shard_map/ppermute | solution.py:164
  79.5 18.8 %collective-permute-start.23 = (f32[2,128,768]{2,1,0:T(8,128)S(1)}, f32[2,128,768]{2,1,0:T(8,128)S(1)}, u32[]{:S(2)}, u32[]{:S(2)}) collective-permute-start(f32[2,128,768]{2,1,0:T(8,128)S(1)} %pad_maximum_fusion.2.w), channel_id=1, source_target_pairs={{0,64},{8,200},{64,0},{72,136},{128,192},{136,72},{192,128},{200,8... | collective-permute-start | bytes 2359304 | tf_op jit(solution)/shard_map/ppermute | solution.py:164
  84.0 16.6 %collective-permute-start.15 = (f32[4,128,384]{2,1,0:T(8,128)S(1)}, f32[4,128,384]{2,1,0:T(8,128)S(1)}, u32[]{:S(2)}, u32[]{:S(2)}) collective-permute-start(f32[4,128,384]{2,1,0:T(8,128)S(1)} %pad_maximum_fusion.1.q), channel_id=1, source_target_pairs={{0,2},{8,14},{2,0},{10,12},{4,6},{12,10},{6,4},{14,8},{1,3},{9,15}... | collective-permute-start | bytes 2359304 | tf_op jit(solution)/shard_map/ppermute | solution.py:163
  86.3 21.3 %collective-permute-start.9 = (f32[2,128,768]{2,1,0:T(8,128)S(1)}, f32[2,128,768]{2,1,0:T(8,128)S(1)}, u32[]{:S(2)}, u32[]{:S(2)}) collective-permute-start(f32[2,128,768]{2,1,0:T(8,128)S(1)} %pad_maximum_fusion.w), channel_id=1, source_target_pairs={{0,64},{8,200},{64,0},{72,136},{128,192},{136,72},{192,128},{200,8... | collective-permute-start | bytes 2359304 | tf_op jit(solution)/shard_map/ppermute | solution.py:164
  109.6 7.4 %collective-permute-start.24 = (f32[192,768]{1,0:T(8,128)S(1)}, f32[192,768]{1,0:T(8,128)S(1)}, u32[]{:S(2)}, u32[]{:S(2)}) collective-permute-start(f32[192,768]{1,0:T(8,128)S(1)} %get-tuple-element.26), channel_id=1, source_target_pairs={{0,8},{8,0},{1,9},{9,1},{2,10},{10,2},{3,11},{11,3},{4,12},{12,4},... | collective-permute-start | bytes 1769480 | tf_op jit(solution)/shard_map/ppermute | solution.py:218

commit v3 on v2

v3 whole, which is shorter than its diff:
```python
import functools

import jax
import jax.numpy as jnp
from jax import lax
from jax.experimental import pallas as pl
from jax.experimental.pallas import tpu as pltpu
from jax.sharding import Mesh, PartitionSpec as P

IMAGES = 8
TOK = 256
PIECE = 32
VMEM_LIMIT = 28 * 1024 * 1024
SWAP = [(0, 1), (1, 0)]
FREE = pl.CostEstimate(flops=0, bytes_accessed=0, transcendentals=0)

CHUNKS = (((0, 1), True), ((2, 3), True))


def partner(i, bit):
    return i ^ 1 if bit else 3 - i


def swap_pairs(step, index):
    return [
        (index(i, c), index(partner(i, (step + c) % 2 == 0), c)) for i in range(4) for c in range(2)
    ]


def split(a):
    hi = a.astype(jnp.bfloat16)
    return hi, (a - hi.astype(jnp.float32)).astype(jnp.bfloat16)


def dot3(a, b, dims):
    a_hi, a_lo = split(a)
    b_hi, b_lo = split(b)
    dot = functools.partial(
        lax.dot_general, dimension_numbers=(dims, ((), ())), preferred_element_type=jnp.float32
    )
    return dot(a_hi, b_hi) + (dot(a_hi, b_lo) + dot(a_lo, b_hi))


def bits(i, c):
    return (i + 1) // 2 % 2 * (2 - c) + i // 2 * (1 + c)


def own_piece(pos, x_first):
    x, zh = bits(pos[1], pos[0]), bits(pos[2], pos[0])
    return 2 * x + zh // 2 if x_first else 2 * zh + x // 2


def row(at, own, size):
    return pl.multiple_of((own ^ at) * size, size)


def out_kernel(x_first, pos, g_own, g_other, b_own, b_other, keep, send, whole):
    own = own_piece(pos, x_first)
    g = jnp.concatenate([g_own[...], g_other[...]], axis=0).T
    basis = jnp.concatenate([b_own[...], b_other[...]], axis=0)
    whole[...] = dot3(g, basis, ((1,), (0,)))
    for at in range(8):
        to = keep if at < 4 else send
        to[0, pl.ds(at % 4 * PIECE, PIECE), :] = whole[pl.ds(row(at, own, PIECE), PIECE), :]


def rotate_out(pos, chunk, base, g_own, g_other, b_own, b_other):
    (images, x_first), (feat, cols) = chunk, b_own.shape
    n, first = len(images), images[0] - base
    spec = lambda: pl.BlockSpec((feat, cols), lambda i, pos: (0, 0))
    return pl.pallas_call(
        functools.partial(out_kernel, x_first),
        grid_spec=pltpu.PrefetchScalarGridSpec(
            num_scalar_prefetch=1,
            grid=(n,),
            in_specs=[
                pl.BlockSpec((feat, TOK), lambda i, pos: (0, first + i)),
                pl.BlockSpec((feat, TOK), lambda i, pos: (0, first + i)),
                spec(),
                spec(),
            ],
            out_specs=[pl.BlockSpec((1, TOK // 2, cols), lambda i, pos: (i, 0, 0))] * 2,
            scratch_shapes=[pltpu.VMEM((TOK, cols), jnp.float32)],
        ),
        out_shape=[jax.ShapeDtypeStruct((n, TOK // 2, cols), jnp.float32)] * 2,
        compiler_params=pltpu.CompilerParams(vmem_limit_bytes=VMEM_LIMIT),
        cost_estimate=FREE,
    )(pos, g_own, g_other, b_own, b_other)


def in_kernel(pos, acts, b_own, b_other, keep, send, whole):
    own = bits(pos[3], pos[0])
    basis = jnp.concatenate([b_own[...], b_other[...]], axis=0)
    whole[...] = dot3(acts[...], basis, ((1,), (1,)))
    size = TOK // 4
    for at in range(4):
        to = keep if at < 2 else send
        to[0, pl.ds(at % 2 * size, size), :] = whole[pl.ds(row(at, own, size), size), :]


def rotate_in(pos, acts, b_own, b_other):
    cols, feat = b_own.shape
    spec = lambda: pl.BlockSpec((cols, feat), lambda i, pos: (0, 0))
    return pl.pallas_call(
        in_kernel,
        grid_spec=pltpu.PrefetchScalarGridSpec(
            num_scalar_prefetch=1,
            grid=(4,),
            in_specs=[pl.BlockSpec((TOK, feat), lambda i, pos: (pos[0] * 4 + i, 0)), spec(), spec()],
            out_specs=[pl.BlockSpec((1, TOK // 2, 2 * cols), lambda i, pos: (i, 0, 0))] * 2,
            scratch_shapes=[pltpu.VMEM((TOK, 2 * cols), jnp.float32)],
        ),
        out_shape=[jax.ShapeDtypeStruct((4, TOK // 2, 2 * cols), jnp.float32)] * 2,
        compiler_params=pltpu.CompilerParams(vmem_limit_bytes=VMEM_LIMIT),
        cost_estimate=FREE,
    )(pos, acts, b_own, b_other)


def tile_kernel(chunk, first, pos, w, v, q, p, *rest):
    images, x_first = chunk
    if first:
        own, other, left, right = rest
    else:
        own_in, other_in, own, other, left, right = rest
    own_out, own_y = own_piece(pos, x_first), bits(pos[3], pos[0])
    size = TOK // 4
    total = None
    for i, image in enumerate(images):
        for at in range(8):
            src = w if at < 4 else v
            right[pl.ds(row(at, own_out, PIECE), PIECE), :] = src[i, pl.ds(at % 4 * PIECE, PIECE), :]
        for at in range(4):
            src = q if at < 2 else p
            left[pl.ds(row(at, own_y, size), size), :] = src[image, pl.ds(at % 2 * size, size), :]
        tile = dot3(left[...].T, right[...], ((1,), (0,)))
        total = tile * tile if total is None else total + tile * tile
    cols = own.shape[0]
    if first:
        own[...] = total[:cols]
        other[...] = total[cols:]
    else:
        own[...] = own_in[...] + total[:cols]
        other[...] = other_in[...] + total[cols:]


def tiles(pos, chunk, halves, quarters, running):
    rows, cols = halves[0].shape[2], quarters[0].shape[2] // 2
    full = lambda a: pl.BlockSpec(a.shape, lambda i, pos: (0,) * a.ndim)
    first = running is None
    args = (*halves, *quarters, *(() if first else running))
    out = jax.ShapeDtypeStruct((cols, rows), jnp.float32)
    return pl.pallas_call(
        functools.partial(tile_kernel, chunk, first),
        grid_spec=pltpu.PrefetchScalarGridSpec(
            num_scalar_prefetch=1,
            grid=(1,),
            in_specs=[full(a) for a in args],
            out_specs=[full(out)] * 2,
            scratch_shapes=[pltpu.VMEM((TOK, 2 * cols), jnp.float32), pltpu.VMEM((TOK, rows), jnp.float32)],
        ),
        out_shape=[out] * 2,
        compiler_params=pltpu.CompilerParams(vmem_limit_bytes=VMEM_LIMIT),
        cost_estimate=FREE,
    )(pos, *args)


def exchange(a, axis, step):
    if axis == "zl":
        return lax.ppermute(a, axis, SWAP)
    if axis == "y":
        return lax.ppermute(a, ("c", "y"), swap_pairs(step, lambda i, c: 4 * c + i))
    return lax.ppermute(a, (axis, "c"), swap_pairs(step, lambda i, c: 2 * i + c))


def after(value, other):
    return value if other is None else lax.optimization_barrier((value, other))[0]


def travel(parts, steps, inner):
    keep, give = parts
    for i, (axis, step) in enumerate(steps):
        got = yield give, axis, step
        if i + 1 == len(steps):
            keep = keep + got
        else:
            half = keep.shape[1] // 2
            keep, give = keep[:, :half] + got[:, :half], keep[:, half:] + got[:, half:]
    keep = keep + (yield keep, *inner)
    for i, (axis, step) in enumerate(reversed(steps)):
        got = yield keep, axis, step
        if i + 1 < len(steps):
            keep = jnp.concatenate([keep, got], axis=1)
    yield keep, got


def local(acts, grads, basis_in, basis_out):
    x, zh, c, y = (lax.axis_index(a).astype(jnp.int32) for a in ("x", "zh", "c", "y"))

    pos = jnp.stack([c, x, zh, y])
    grads_t, basis_in_t = grads.T, basis_in.T

    to_other = lambda a: lax.ppermute(a, "c", SWAP)
    basis_out_other = to_other(basis_out)
    feat, ahead = grads_t.shape[0], len(CHUNKS[0][0])

    def swapped(first, count, token):
        columns = lambda core: lax.dynamic_slice(
            after(grads_t, token), (0, (core * 4 + first) * TOK), (feat, count * TOK)
        )
        return columns(c), to_other(columns(1 - c))

    grads_of = {0: (0, *swapped(0, ahead, None))}

    def output_side(i, token):
        images, x_first = chunk = CHUNKS[i]
        along = [[("x", 0), ("x", 1)], [("zh", 0), ("zh", 1)]][:: 1 if x_first else -1]
        part = 0 if i == 0 else 1
        if part not in grads_of:
            grads_of[1] = (ahead, *swapped(ahead, 4 - ahead, token))
        parts = rotate_out(after(pos, token), chunk, *grads_of[part], basis_out, basis_out_other)
        return travel(parts, along[0] + along[1][:1], along[1][1])

    def input_side(token):
        own = after(basis_in_t, token)
        parts = rotate_in(pos, acts, own, to_other(own))
        return travel(parts, [("y", 0), ("y", 1)], ("zl", 0))

    last = len(CHUNKS)
    chains, flying, results, token = {}, {}, {}, None
    for i in range(last + 1):
        chains[i] = output_side(i, token) if i < last else input_side(token)
        out = next(chains[i])
        flying[i], token = exchange(*out), out[0]
    while len(results) <= last:
        for i in chains:
            if i in results:
                continue
            out = chains[i].send(flying[i])
            if len(out) == 2:
                results[i] = out
            else:
                flying[i] = exchange(*out)

    running = None
    for i in range(last):
        running = tiles(pos, CHUNKS[i], results[i], results[last], running)
    own, other = running
    return ((own + to_other(other)) * (1.0 / IMAGES)).T


def solution(mesh):
    axes = Mesh(mesh.devices.reshape(4, 4, 2, 4, 2), ("x", "zh", "c", "y", "zl"))
    wide, narrow = ("x", "zh", "c"), ("y", "zl")
    placed = (P(None, narrow), P(None, wide), P(narrow, wide), P(wide, narrow))
    return jax.shard_map(
        local, mesh=axes, in_specs=placed, out_specs=P(narrow, wide), check_vma=False
    )
```

time: 119 us -> 112 us (0.941)
  starting transfers between devices: 42.7 us -> 31.8 us
  waiting for transfers between devices: 55.7 us -> 60.3 us
  local copies, waits for them, and re-layouts: 3.29 us -> 5.18 us
  Pallas kernels: 14.4 us -> 12.9 us
    ppermute x5 -> x6, starting transfers between devices: 10.7 us -> 4.92 us  [the longest x5 4.02 us: local(): to_other = lambda a: lax.ppermute(a, 'c', SWAP)]
    ppermute x16 -> x14, waiting for transfers between devices: 44 us -> 48.8 us  [exchange(): lax.ppermute(a, (axis, 'c'), swap_pairs(step, lambda i, c: 2 * i + c))]
    ppermute x4, waiting for transfers between devices: 4.36 us -> 0.01 us  [exchange(): return lax.ppermute(a, ('c', 'y'), swap_pairs(step, lambda i, c: 4 * c + i))]
    ppermute x5 -> x6, waiting for transfers between devices: 7.34 us -> 11.5 us  [the longest x1 6.6 us: exchange(): return lax.ppermute(a, axis, SWAP)]
    ppermute x4, starting transfers between devices: 9.47 us -> 5.9 us  [exchange(): return lax.ppermute(a, ('c', 'y'), swap_pairs(step, lambda i, c: 4 * c + i))]
    unnamed x6, local copies, waits for them, and re-layouts: 1.07 us -> 2.79 us
    ppermute x16 -> x14, starting transfers between devices: 22.6 us -> 21 us  [exchange(): lax.ppermute(a, (axis, 'c'), swap_pairs(step, lambda i, c: 2 * i + c))]
    pallas_call x1, Pallas kernels: 5.49 us -> 3.98 us  [rotate_in(): pl.pallas_call(in_kernel, grid_spec=pltpu.PrefetchScalarGridSpec(num_scal...]
  transfers between devices with their start and end apart: 25 -> 24, of which waited for: 16 -> 15; matrix products, arithmetic and copies ran while one was open for 1% -> 3% of each run, Pallas kernels for 8% -> 8%
where the time goes in v3:
time: 112 us
  waiting for transfers between devices  60.3 us (54%)
  starting transfers between devices  31.8 us (28%)
  Pallas kernels  12.9 us (12%)
  local copies, waits for them, and re-layouts  5.18 us (5%)
  other arithmetic  1.7 us (2%)
    ppermute x14, waiting for transfers between devices, exchange(): lax.ppermute(a, (axis, 'c'), swap_pairs(step, lambda i, c: 2 * i + c))  48.8 us
    ppermute x14, starting transfers between devices, exchange(): lax.ppermute(a, (axis, 'c'), swap_pairs(step, lambda i, c: 2 * i + c))  21 us
    ppermute x1, waiting for transfers between devices, exchange(): return lax.ppermute(a, axis, SWAP)  6.6 us
    ppermute x4, starting transfers between devices, exchange(): return lax.ppermute(a, ('c', 'y'), swap_pairs(step, lambda i, c: 4 * c + i))  5.9 us
    pallas_call x2, Pallas kernels, rotate_out(): pl.pallas_call(functools.partial(out_kernel, x_first), grid_spec=pltpu.Pr...  4.96 us
    ppermute x5, waiting for transfers between devices, local(): to_other = lambda a: lax.ppermute(a, 'c', SWAP)  4.93 us
    ppermute x5, starting transfers between devices, local(): to_other = lambda a: lax.ppermute(a, 'c', SWAP)  4.02 us
    pallas_call x1, Pallas kernels, rotate_in(): pl.pallas_call(in_kernel, grid_spec=pltpu.PrefetchScalarGridSpec(num_scal...  3.98 us
  transfers between devices with their start and end apart: 24, of which 15 were waited for; matrix products, arithmetic and copies ran while one was open for 3% of the time, Pallas kernels for 8%

profile of v3, /device:TPU:1, one launch (start us, length us, event | category | flops | bytes accessed | tf_op | source)
XLA Modules:
  0.0 112.1 jit_solution(6926495237479642044)
XLA Ops:
  0.0 3.2 %collective-permute-start.1 = (f32[192,768]{1,0:T(8,128)}, f32[192,768]{1,0:T(8,128)S(1)}, u32[]{:S(2)}, u32[]{:S(2)}) collective-permute-start(f32[192,768]{1,0:T(8,128)} %b_own.3), channel_id=1, source_target_pairs={{0,8},{8,0},{1,9},{9,1},{2,10},{10,2},{3,11},{11,3},{4,12},{12,4},... | collective-permute-start | bytes 1769480 | tf_op jit(solution)/shard_map/ppermute | solution.py:202
  3.2 1.2 %dynamic-slice_bitcast_fusion = (f32[192,512]{1,0:T(8,128)S(1)}, f32[192,512]{1,0:T(8,128)S(1)}) fusion(f32[2048,192]{0,1:T(8,128)} %param.5, s32[]{:T(128)S(6)} %select_n.13, s32[]{:T(128)S(6)} %select_n.12), kind=kLoop, calls=%fused_computation.13 | loop fusion | bytes 1572872 | tf_op jit(solution)/shard_map/dynamic_slice | solution.py:207
  4.4 0.2 collective-permute-start
  4.6 0.1 pad_add_fusion.pos
  4.6 1.6 %collective-permute-done.g_other = f32[192,512]{1,0:T(8,128)S(1)} collective-permute-done((f32[192,512]{1,0:T(8,128)S(1)}, f32[192,512]{1,0:T(8,128)S(1)}, u32[]{:S(2)}, u32[]{:S(2)}) %collective-permute-start) | collective-permute-done | bytes 393248 | tf_op jit(solution)/shard_map/ppermute | solution.py:202
  6.2 0.0 collective-permute-done.1.b_other
  6.2 2.5 %shard_map.46 = (f32[2,128,768]{2,1,0:T(8,128)S(1)}, f32[2,128,768]{2,1,0:T(8,128)S(1)}) custom-call(s32[4]{0:T(128)S(1)} %pad_add_fusion.pos, f32[192,512]{1,0:T(8,128)S(1)} %get-tuple-element.38.g_own, f32[192,512]{1,0:T(8,128)S(1)} %collective-permute-done.g_other, f32[192,768]{1,0:T(8,128)S(1)} %copy-done.1, f32[192,768]{1,0:T(8,128)S(1)} %collective-permute-done.1.b_other), custom_call_target="tpu_custom_call" | custom-call | tf_op jit(solution)/shard_map/pallas_call | solution.py:71
  8.7 0.8 collective-permute-start.16
  9.6 1.2 %constant_dynamic-slice_fusion = (f32[192,512]{1,0:T(8,128)S(1)}, f32[192,512]{1,0:T(8,128)S(1)}) fusion(f32[192,2048]{1,0:T(8,128)} %bitcast.14, s32[]{:T(128)S(6)} %select_n.15, s32[]{:T(128)S(6)} %select_n.14), kind=kLoop, calls=%fused_computation.21 | loop fusion | bytes 1572872 | tf_op jit(solution)/shard_map/dynamic_slice | solution.py:207
  10.8 0.1 collective-permute-start.2
  10.9 1.7 %collective-permute-done.2.g_other = f32[192,512]{1,0:T(8,128)S(1)} collective-permute-done((f32[192,512]{1,0:T(8,128)S(1)}, f32[192,512]{1,0:T(8,128)S(1)}, u32[]{:S(2)}, u32[]{:S(2)}) %collective-permute-start.2) | collective-permute-done | bytes 393248 | tf_op jit(solution)/shard_map/ppermute | solution.py:202
  12.6 2.5 %shard_map.47 = (f32[2,128,768]{2,1,0:T(8,128)S(1)}, f32[2,128,768]{2,1,0:T(8,128)S(1)}) custom-call(s32[4]{0:T(128)S(1)} %pad_add_fusion.pos, f32[192,512]{1,0:T(8,128)S(1)} %get-tuple-element.36.g_own, f32[192,512]{1,0:T(8,128)S(1)} %collective-permute-done.2.g_other, f32[192,768]{1,0:T(8,128)S(1)} %copy-done.1, f32[192,768]{1,0:T(8,128)S(1)} %collective-permute-done.1.b_other), custom_call_target="tpu_custom_call" | custom-call | tf_op jit(solution)/shard_map/pallas_call | solution.py:71
  15.1 2.0 %collective-permute-start.3 = (f32[2,128,768]{2,1,0:T(8,128)S(1)}, f32[2,128,768]{2,1,0:T(8,128)S(1)}, u32[]{:S(2)}, u32[]{:S(2)}) collective-permute-start(f32[2,128,768]{2,1,0:T(8,128)S(1)} %get-tuple-element.22), channel_id=1, source_target_pairs={{0,64},{8,200},{64,0},{72,136},{128,192},{136,72},{192,128},{200,8... | collective-permute-start | bytes 2359304 | tf_op jit(solution)/shard_map/ppermute | solution.py:172
  17.1 0.0 collective-permute-start.10
  17.1 3.8 %collective-permute-done.16 = f32[2,128,768]{2,1,0:T(8,128)S(1)} collective-permute-done((f32[2,128,768]{2,1,0:T(8,128)S(1)}, f32[2,128,768]{2,1,0:T(8,128)S(1)}, u32[]{:S(2)}, u32[]{:S(2)}) %collective-permute-start.16) | collective-permute-done | bytes 786464 | tf_op jit(solution)/shard_map/ppermute | solution.py:172
  20.9 0.1 slice_add_fusion.1
  20.9 0.1 collective-permute-start.17
  21.0 0.0 collective-permute-done.10.b_other
  21.1 0.0 copy-start
  21.1 2.8 %copy-done = f32[2048,768]{1,0:T(8,128)S(1)} copy-done((f32[2048,768]{1,0:T(8,128)S(1)}, f32[2048,768]{1,0:T(8,128)}, u32[]{:S(2)}) %copy-start) | copy-done | bytes 6291480
  23.8 4.0 %shard_map.48 = (f32[4,128,384]{2,1,0:T(8,128)S(1)}, f32[4,128,384]{2,1,0:T(8,128)S(1)}) custom-call(s32[4]{0:T(128)S(1)} %pad_add_fusion.pos, f32[2048,768]{1,0:T(8,128)S(1)} %copy-done, f32[192,768]{1,0:T(8,128)S(1)} %bitcast.13, f32[192,768]{1,0:T(8,128)S(1)} %collective-permute-done.10.b_other), custom_call_target="tpu_custom_call" | custom-call | tf_op jit(solution)/shard_map/pallas_call | solution.py:104
  27.8 1.4 %collective-permute-start.11 = (f32[4,128,384]{2,1,0:T(8,128)S(1)}, f32[4,128,384]{2,1,0:T(8,128)S(1)}, u32[]{:S(2)}, u32[]{:S(2)}) collective-permute-start(f32[4,128,384]{2,1,0:T(8,128)S(1)} %get-tuple-element.25), channel_id=1, source_target_pairs={{0,2},{8,14},{2,0},{10,12},{4,6},{12,10},{6,4},{14,8},{1,3},{9,15}... | collective-permute-start | bytes 2359304 | tf_op jit(solution)/shard_map/ppermute | solution.py:171
  29.2 3.0 %collective-permute-done.17 = f32[2,64,768]{2,1,0:T(8,128)S(1)} collective-permute-done((f32[2,64,768]{2,1,0:T(8,128)S(1)}, f32[2,64,768]{2,1,0:T(8,128)S(1)}, u32[]{:S(2)}, u32[]{:S(2)}) %collective-permute-start.17) | collective-permute-done | bytes 393248 | tf_op jit(solution)/shard_map/ppermute | solution.py:172
  32.3 4.4 %collective-permute-start.18 = (f32[2,32,768]{2,1,0:T(8,128)S(1)}, f32[2,32,768]{2,1,0:T(8,128)S(1)}, u32[]{:S(2)}, u32[]{:S(2)}) collective-permute-start(f32[2,32,768]{2,1,0:T(8,128)S(1)} %slice_add_fusion.6), channel_id=1, source_target_pairs={{0,16},{8,56},{16,0},{24,40},{32,48},{40,24},{48,32},{56,8},{1,17}... | collective-permute-start | bytes 589832 | tf_op jit(solution)/shard_map/ppermute | solution.py:172
  36.6 0.0 collective-permute-done.3
  36.6 0.1 slice_add_fusion.5
  36.7 0.4 collective-permute-start.4
  37.1 4.1 %collective-permute-done.18 = f32[2,32,768]{2,1,0:T(8,128)S(1)} collective-permute-done((f32[2,32,768]{2,1,0:T(8,128)S(1)}, f32[2,32,768]{2,1,0:T(8,128)S(1)}, u32[]{:S(2)}, u32[]{:S(2)}) %collective-permute-start.18) | collective-permute-done | bytes 196640 | tf_op jit(solution)/shard_map/ppermute | solution.py:172
  41.2 1.9 %collective-permute-start.19 = (f32[2,32,768]{2,1,0:T(8,128)S(1)}, f32[2,32,768]{2,1,0:T(8,128)S(1)}, u32[]{:S(2)}, u32[]{:S(2)}) collective-permute-start(f32[2,32,768]{2,1,0:T(8,128)S(1)} %fusion.1), channel_id=1, source_target_pairs={{0,48},{8,24},{16,32},{24,8},{32,16},{40,56},{48,0},{56,40},{1,49}... | collective-permute-start | bytes 589832 | tf_op jit(solution)/shard_map/ppermute | solution.py:172
  43.1 0.6 collective-permute-done.4
  43.8 1.7 %collective-permute-start.5 = (f32[2,32,768]{2,1,0:T(8,128)S(1)}, f32[2,32,768]{2,1,0:T(8,128)S(1)}, u32[]{:S(2)}, u32[]{:S(2)}) collective-permute-start(f32[2,32,768]{2,1,0:T(8,128)S(1)} %slice_add_fusion.8), channel_id=1, source_target_pairs={{0,16},{8,56},{16,0},{24,40},{32,48},{40,24},{48,32},{56,8},{1,17}... | collective-permute-start | bytes 589832 | tf_op jit(solution)/shard_map/ppermute | solution.py:172
  45.5 0.0 collective-permute-done.11
  45.5 1.6 %collective-permute-start.12 = (f32[4,64,384]{2,1,0:T(8,128)S(1)}, f32[4,64,384]{2,1,0:T(8,128)S(1)}, u32[]{:S(2)}, u32[]{:S(2)}) collective-permute-start(f32[4,64,384]{2,1,0:T(8,128)S(1)} %slice_add_fusion.2), channel_id=1, source_target_pairs={{0,6},{8,10},{2,4},{10,8},{4,2},{12,14},{6,0},{14,12},{1,7},{9,11}... | collective-permute-start | bytes 1179656 | tf_op jit(solution)/shard_map/ppermute | solution.py:171
  47.2 2.0 %collective-permute-done.19 = f32[2,32,768]{2,1,0:T(8,128)S(1)} collective-permute-done((f32[2,32,768]{2,1,0:T(8,128)S(1)}, f32[2,32,768]{2,1,0:T(8,128)S(1)}, u32[]{:S(2)}, u32[]{:S(2)}) %collective-permute-start.19) | collective-permute-done | bytes 196640 | tf_op jit(solution)/shard_map/ppermute | solution.py:172
  49.2 1.8 %collective-permute-start.20 = (f32[2,32,768]{2,1,0:T(8,128)S(1)}, f32[2,32,768]{2,1,0:T(8,128)S(1)}, u32[]{:S(2)}, u32[]{:S(2)}) collective-permute-start(f32[2,32,768]{2,1,0:T(8,128)S(1)} %add.90), channel_id=1, source_target_pairs={{0,16},{8,56},{16,0},{24,40},{32,48},{40,24},{48,32},{56,8},{1,17}... | collective-permute-start | bytes 589832 | tf_op jit(solution)/shard_map/ppermute | solution.py:172
  51.0 4.9 %collective-permute-done.5 = f32[2,32,768]{2,1,0:T(8,128)S(1)} collective-permute-done((f32[2,32,768]{2,1,0:T(8,128)S(1)}, f32[2,32,768]{2,1,0:T(8,128)S(1)}, u32[]{:S(2)}, u32[]{:S(2)}) %collective-permute-start.5) | collective-permute-done | bytes 196640 | tf_op jit(solution)/shard_map/ppermute | solution.py:172
  55.9 2.4 %collective-permute-start.6 = (f32[2,32,768]{2,1,0:T(8,128)S(1)}, f32[2,32,768]{2,1,0:T(8,128)S(1)}, u32[]{:S(2)}, u32[]{:S(2)}) collective-permute-start(f32[2,32,768]{2,1,0:T(8,128)S(1)} %fusion.2), channel_id=1, source_target_pairs={{0,48},{8,24},{16,32},{24,8},{32,16},{40,56},{48,0},{56,40},{1,49}... | collective-permute-start | bytes 589832 | tf_op jit(solution)/shard_map/ppermute | solution.py:172
  58.4 0.0 collective-permute-done.12
  58.4 0.1 fusion
  58.5 0.9 collective-permute-start.13
  59.4 4.7 %collective-permute-done.6 = f32[2,32,768]{2,1,0:T(8,128)S(1)} collective-permute-done((f32[2,32,768]{2,1,0:T(8,128)S(1)}, f32[2,32,768]{2,1,0:T(8,128)S(1)}, u32[]{:S(2)}, u32[]{:S(2)}) %collective-permute-start.6) | collective-permute-done | bytes 196640 | tf_op jit(solution)/shard_map/ppermute | solution.py:172
  64.1 2.2 %collective-permute-start.7 = (f32[2,32,768]{2,1,0:T(8,128)S(1)}, f32[2,32,768]{2,1,0:T(8,128)S(1)}, u32[]{:S(2)}, u32[]{:S(2)}) collective-permute-start(f32[2,32,768]{2,1,0:T(8,128)S(1)} %add.80), channel_id=1, source_target_pairs={{0,16},{8,56},{16,0},{24,40},{32,48},{40,24},{48,32},{56,8},{1,17}... | collective-permute-start | bytes 589832 | tf_op jit(solution)/shard_map/ppermute | solution.py:172
  66.3 0.0 collective-permute-done.20
  66.3 2.6 %collective-permute-start.21 = (f32[2,64,768]{2,1,0:T(8,128)S(1)}, f32[2,64,768]{2,1,0:T(8,128)S(1)}, u32[]{:S(2)}, u32[]{:S(2)}) collective-permute-start(f32[2,64,768]{2,1,0:T(8,128)S(1)} %pad_maximum_fusion.4), channel_id=1, source_target_pairs={{0,192},{8,72},{64,128},{72,8},{128,64},{136,200},{192,0},{200,136... | collective-permute-start | bytes 1179656 | tf_op jit(solution)/shard_map/ppermute | solution.py:172
  68.9 6.6 %collective-permute-done.13 = f32[4,64,384]{2,1,0:T(8,128)S(1)} collective-permute-done((f32[4,64,384]{2,1,0:T(8,128)S(1)}, f32[4,64,384]{2,1,0:T(8,128)S(1)}, u32[]{:S(2)}, u32[]{:S(2)}) %collective-permute-start.13) | collective-permute-done | bytes 393248 | tf_op jit(solution)/shard_map/ppermute | solution.py:169
  75.5 0.1 add.84
  75.5 0.1 collective-permute-start.14
  75.6 6.5 %collective-permute-done.7 = f32[2,32,768]{2,1,0:T(8,128)S(1)} collective-permute-done((f32[2,32,768]{2,1,0:T(8,128)S(1)}, f32[2,32,768]{2,1,0:T(8,128)S(1)}, u32[]{:S(2)}, u32[]{:S(2)}) %collective-permute-start.7) | collective-permute-done | bytes 196640 | tf_op jit(solution)/shard_map/ppermute | solution.py:172
  82.1 0.1 collective-permute-start.8
  82.2 0.0 collective-permute-done.21
  82.2 0.1 pad_maximum_fusion.2.w
  82.3 0.5 collective-permute-start.22
  82.8 0.1 pad_maximum_fusion.1.q
  82.9 2.8 %collective-permute-start.15 = (f32[4,128,384]{2,1,0:T(8,128)S(1)}, f32[4,128,384]{2,1,0:T(8,128)S(1)}, u32[]{:S(2)}, u32[]{:S(2)}) collective-permute-start(f32[4,128,384]{2,1,0:T(8,128)S(1)} %pad_maximum_fusion.1.q), channel_id=1, source_target_pairs={{0,2},{8,14},{2,0},{10,12},{4,6},{12,10},{6,4},{14,8},{1,3},{9,15}... | collective-permute-start | bytes 2359304 | tf_op jit(solution)/shard_map/ppermute | solution.py:171
  85.7 4.2 %collective-permute-done.8 = f32[2,64,768]{2,1,0:T(8,128)S(1)} collective-permute-done((f32[2,64,768]{2,1,0:T(8,128)S(1)}, f32[2,64,768]{2,1,0:T(8,128)S(1)}, u32[]{:S(2)}, u32[]{:S(2)}) %collective-permute-start.8) | collective-permute-done | bytes 393248 | tf_op jit(solution)/shard_map/ppermute | solution.py:172
  89.8 0.1 pad_maximum_fusion.w
  89.9 0.1 collective-permute-start.9
  90.0 8.6 %collective-permute-done.22.v = f32[2,128,768]{2,1,0:T(8,128)S(1)} collective-permute-done((f32[2,128,768]{2,1,0:T(8,128)S(1)}, f32[2,128,768]{2,1,0:T(8,128)S(1)}, u32[]{:S(2)}, u32[]{:S(2)}) %collective-permute-start.22) | collective-permute-done | bytes 786464 | tf_op jit(solution)/shard_map/ppermute | solution.py:172
  98.6 2.0 %shard_map.49 = (f32[192,768]{1,0:T(8,128)S(1)}, f32[192,768]{1,0:T(8,128)S(1)}) custom-call(s32[4]{0:T(128)S(1)} %pad_add_fusion.pos, f32[2,128,768]{2,1,0:T(8,128)S(1)} %pad_maximum_fusion.2.w, f32[2,128,768]{2,1,0:T(8,128)S(1)} %collective-permute-done.22.v, f32[4,128,384]{2,1,0:T(8,128)S(1)} %pad_maximum_fusion.1.q, ...), custom_call_target="tpu_custom_call" | custom-call | tf_op jit(solution)/shard_map/pallas_call | solution.py:152
  100.6 6.4 %collective-permute-done.9.v = f32[2,128,768]{2,1,0:T(8,128)S(1)} collective-permute-done((f32[2,128,768]{2,1,0:T(8,128)S(1)}, f32[2,128,768]{2,1,0:T(8,128)S(1)}, u32[]{:S(2)}, u32[]{:S(2)}) %collective-permute-start.9) | collective-permute-done | bytes 786464 | tf_op jit(solution)/shard_map/ppermute | solution.py:172
  107.1 2.0 %shard_map.50 = (f32[192,768]{1,0:T(8,128)S(1)}, f32[192,768]{1,0:T(8,128)S(1)}) custom-call(s32[4]{0:T(128)S(1)} %pad_add_fusion.pos, f32[2,128,768]{2,1,0:T(8,128)S(1)} %pad_maximum_fusion.w, f32[2,128,768]{2,1,0:T(8,128)S(1)} %collective-permute-done.9.v, f32[4,128,384]{2,1,0:T(8,128)S(1)} %pad_maximum_fusion.1.q, ...), custom_call_target="tpu_custom_call" | custom-call | tf_op jit(solution)/shard_map/pallas_call | solution.py:152
  109.1 0.5 collective-permute-start.23
  109.6 1.6 %collective-permute-done.23 = f32[192,768]{1,0:T(8,128)S(1)} collective-permute-done((f32[192,768]{1,0:T(8,128)S(1)}, f32[192,768]{1,0:T(8,128)S(1)}, u32[]{:S(2)}, u32[]{:S(2)}) %collective-permute-start.23) | collective-permute-done | bytes 589856 | tf_op jit(solution)/shard_map/ppermute | solution.py:202
  111.2 0.9 multiply_bitcast_fusion
  (15 shorter events, 0.3 us)
Async XLA Ops:
  0.0 6.2 %copy-start.1 = (f32[192,768]{1,0:T(8,128)S(1)}, f32[192,768]{1,0:T(8,128)}, u32[]{:S(2)}) copy-start(f32[192,768]{1,0:T(8,128)} %b_own.3) | copy-start | bytes 1769476
  0.0 6.2 %collective-permute-start.1 = (f32[192,768]{1,0:T(8,128)}, f32[192,768]{1,0:T(8,128)S(1)}, u32[]{:S(2)}, u32[]{:S(2)}) collective-permute-start(f32[192,768]{1,0:T(8,128)} %b_own.3), channel_id=1, source_target_pairs={{0,8},{8,0},{1,9},{9,1},{2,10},{10,2},{3,11},{11,3},{4,12},{12,4},... | collective-permute-start | bytes 1769480 | tf_op jit(solution)/shard_map/ppermute | solution.py:202
  4.4 1.8 %collective-permute-start = (f32[192,512]{1,0:T(8,128)S(1)}, f32[192,512]{1,0:T(8,128)S(1)}, u32[]{:S(2)}, u32[]{:S(2)}) collective-permute-start(f32[192,512]{1,0:T(8,128)S(1)} %get-tuple-element.37), channel_id=1, source_target_pairs={{0,8},{8,0},{1,9},{9,1},{2,10},{10,2},{3,11},{11,3},{4,12},{12,4},... | collective-permute-start | bytes 1179656 | tf_op jit(solution)/shard_map/ppermute | solution.py:202
  8.7 12.1 %collective-permute-start.16 = (f32[2,128,768]{2,1,0:T(8,128)S(1)}, f32[2,128,768]{2,1,0:T(8,128)S(1)}, u32[]{:S(2)}, u32[]{:S(2)}) collective-permute-start(f32[2,128,768]{2,1,0:T(8,128)S(1)} %get-tuple-element.18), channel_id=1, source_target_pairs={{0,64},{8,200},{64,0},{72,136},{128,192},{136,72},{192,128},{200,8... | collective-permute-start | bytes 2359304 | tf_op jit(solution)/shard_map/ppermute | solution.py:172
  9.5 7.5 %copy-start.2 = (f32[768,192]{0,1:T(8,128)S(1)}, f32[768,192]{0,1:T(8,128)}, u32[]{:S(2)}) copy-start(f32[768,192]{0,1:T(8,128)} %param.6) | copy-start | bytes 1769476
  10.8 1.8 %collective-permute-start.2 = (f32[192,512]{1,0:T(8,128)S(1)}, f32[192,512]{1,0:T(8,128)S(1)}, u32[]{:S(2)}, u32[]{:S(2)}) collective-permute-start(f32[192,512]{1,0:T(8,128)S(1)} %get-tuple-element.35), channel_id=1, source_target_pairs={{0,8},{8,0},{1,9},{9,1},{2,10},{10,2},{3,11},{11,3},{4,12},{12,4},... | collective-permute-start | bytes 1179656 | tf_op jit(solution)/shard_map/ppermute | solution.py:202
  15.1 21.6 %collective-permute-start.3 = (f32[2,128,768]{2,1,0:T(8,128)S(1)}, f32[2,128,768]{2,1,0:T(8,128)S(1)}, u32[]{:S(2)}, u32[]{:S(2)}) collective-permute-start(f32[2,128,768]{2,1,0:T(8,128)S(1)} %get-tuple-element.22), channel_id=1, source_target_pairs={{0,64},{8,200},{64,0},{72,136},{128,192},{136,72},{192,128},{200,8... | collective-permute-start | bytes 2359304 | tf_op jit(solution)/shard_map/ppermute | solution.py:172
  17.1 4.0 %collective-permute-start.10 = (f32[192,768]{1,0:T(8,128)S(1)}, f32[192,768]{1,0:T(8,128)S(1)}, u32[]{:S(2)}, u32[]{:S(2)}) collective-permute-start(f32[192,768]{1,0:T(8,128)S(1)} %bitcast.12), channel_id=1, source_target_pairs={{0,8},{8,0},{1,9},{9,1},{2,10},{10,2},{3,11},{11,3},{4,12},{12,4},... | collective-permute-start | bytes 1769480 | tf_op jit(solution)/shard_map/ppermute | solution.py:202
  20.9 11.3 %collective-permute-start.17 = (f32[2,64,768]{2,1,0:T(8,128)S(1)}, f32[2,64,768]{2,1,0:T(8,128)S(1)}, u32[]{:S(2)}, u32[]{:S(2)}) collective-permute-start(f32[2,64,768]{2,1,0:T(8,128)S(1)} %get-tuple-element.32), channel_id=1, source_target_pairs={{0,192},{8,72},{64,128},{72,8},{128,64},{136,200},{192,0},{200,136... | collective-permute-start | bytes 1179656 | tf_op jit(solution)/shard_map/ppermute | solution.py:172
  21.1 2.8 %copy-start = (f32[2048,768]{1,0:T(8,128)S(1)}, f32[2048,768]{1,0:T(8,128)}, u32[]{:S(2)}) copy-start(f32[2048,768]{1,0:T(8,128)} %acts.1) | copy-start | bytes 18874372
  27.8 17.7 %collective-permute-start.11 = (f32[4,128,384]{2,1,0:T(8,128)S(1)}, f32[4,128,384]{2,1,0:T(8,128)S(1)}, u32[]{:S(2)}, u32[]{:S(2)}) collective-permute-start(f32[4,128,384]{2,1,0:T(8,128)S(1)} %get-tuple-element.25), channel_id=1, source_target_pairs={{0,2},{8,14},{2,0},{10,12},{4,6},{12,10},{6,4},{14,8},{1,3},{9,15}... | collective-permute-start | bytes 2359304 | tf_op jit(solution)/shard_map/ppermute | solution.py:171
  32.3 8.9 %collective-permute-start.18 = (f32[2,32,768]{2,1,0:T(8,128)S(1)}, f32[2,32,768]{2,1,0:T(8,128)S(1)}, u32[]{:S(2)}, u32[]{:S(2)}) collective-permute-start(f32[2,32,768]{2,1,0:T(8,128)S(1)} %slice_add_fusion.6), channel_id=1, source_target_pairs={{0,16},{8,56},{16,0},{24,40},{32,48},{40,24},{48,32},{56,8},{1,17}... | collective-permute-start | bytes 589832 | tf_op jit(solution)/shard_map/ppermute | solution.py:172
  36.7 7.0 %collective-permute-start.4 = (f32[2,64,768]{2,1,0:T(8,128)S(1)}, f32[2,64,768]{2,1,0:T(8,128)S(1)}, u32[]{:S(2)}, u32[]{:S(2)}) collective-permute-start(f32[2,64,768]{2,1,0:T(8,128)S(1)} %get-tuple-element.34), channel_id=1, source_target_pairs={{0,192},{8,72},{64,128},{72,8},{128,64},{136,200},{192,0},{200,136... | collective-permute-start | bytes 1179656 | tf_op jit(solution)/shard_map/ppermute | solution.py:172
  41.2 7.9 %collective-permute-start.19 = (f32[2,32,768]{2,1,0:T(8,128)S(1)}, f32[2,32,768]{2,1,0:T(8,128)S(1)}, u32[]{:S(2)}, u32[]{:S(2)}) collective-permute-start(f32[2,32,768]{2,1,0:T(8,128)S(1)} %fusion.1), channel_id=1, source_target_pairs={{0,48},{8,24},{16,32},{24,8},{32,16},{40,56},{48,0},{56,40},{1,49}... | collective-permute-start | bytes 589832 | tf_op jit(solution)/shard_map/ppermute | solution.py:172
  43.8 12.1 %collective-permute-start.5 = (f32[2,32,768]{2,1,0:T(8,128)S(1)}, f32[2,32,768]{2,1,0:T(8,128)S(1)}, u32[]{:S(2)}, u32[]{:S(2)}) collective-permute-start(f32[2,32,768]{2,1,0:T(8,128)S(1)} %slice_add_fusion.8), channel_id=1, source_target_pairs={{0,16},{8,56},{16,0},{24,40},{32,48},{40,24},{48,32},{56,8},{1,17}... | collective-permute-start | bytes 589832 | tf_op jit(solution)/shard_map/ppermute | solution.py:172
  45.5 12.8 %collective-permute-start.12 = (f32[4,64,384]{2,1,0:T(8,128)S(1)}, f32[4,64,384]{2,1,0:T(8,128)S(1)}, u32[]{:S(2)}, u32[]{:S(2)}) collective-permute-start(f32[4,64,384]{2,1,0:T(8,128)S(1)} %slice_add_fusion.2), channel_id=1, source_target_pairs={{0,6},{8,10},{2,4},{10,8},{4,2},{12,14},{6,0},{14,12},{1,7},{9,11}... | collective-permute-start | bytes 1179656 | tf_op jit(solution)/shard_map/ppermute | solution.py:171
  49.2 17.1 %collective-permute-start.20 = (f32[2,32,768]{2,1,0:T(8,128)S(1)}, f32[2,32,768]{2,1,0:T(8,128)S(1)}, u32[]{:S(2)}, u32[]{:S(2)}) collective-permute-start(f32[2,32,768]{2,1,0:T(8,128)S(1)} %add.90), channel_id=1, source_target_pairs={{0,16},{8,56},{16,0},{24,40},{32,48},{40,24},{48,32},{56,8},{1,17}... | collective-permute-start | bytes 589832 | tf_op jit(solution)/shard_map/ppermute | solution.py:172
  55.9 8.1 %collective-permute-start.6 = (f32[2,32,768]{2,1,0:T(8,128)S(1)}, f32[2,32,768]{2,1,0:T(8,128)S(1)}, u32[]{:S(2)}, u32[]{:S(2)}) collective-permute-start(f32[2,32,768]{2,1,0:T(8,128)S(1)} %fusion.2), channel_id=1, source_target_pairs={{0,48},{8,24},{16,32},{24,8},{32,16},{40,56},{48,0},{56,40},{1,49}... | collective-permute-start | bytes 589832 | tf_op jit(solution)/shard_map/ppermute | solution.py:172
  58.5 17.0 %collective-permute-start.13 = (f32[4,64,384]{2,1,0:T(8,128)S(1)}, f32[4,64,384]{2,1,0:T(8,128)S(1)}, u32[]{:S(2)}, u32[]{:S(2)}) collective-permute-start(f32[4,64,384]{2,1,0:T(8,128)S(1)} %fusion), channel_id=1, source_target_pairs={{0,1},{1,0},{2,3},{3,2},{4,5},{5,4},{6,7},{7,6},{8,9},{9,8},{10,11... | collective-permute-start | bytes 1179656 | tf_op jit(solution)/shard_map/ppermute | solution.py:169
  64.1 18.0 %collective-permute-start.7 = (f32[2,32,768]{2,1,0:T(8,128)S(1)}, f32[2,32,768]{2,1,0:T(8,128)S(1)}, u32[]{:S(2)}, u32[]{:S(2)}) collective-permute-start(f32[2,32,768]{2,1,0:T(8,128)S(1)} %add.80), channel_id=1, source_target_pairs={{0,16},{8,56},{16,0},{24,40},{32,48},{40,24},{48,32},{56,8},{1,17}... | collective-permute-start | bytes 589832 | tf_op jit(solution)/shard_map/ppermute | solution.py:172
  66.3 15.9 %collective-permute-start.21 = (f32[2,64,768]{2,1,0:T(8,128)S(1)}, f32[2,64,768]{2,1,0:T(8,128)S(1)}, u32[]{:S(2)}, u32[]{:S(2)}) collective-permute-start(f32[2,64,768]{2,1,0:T(8,128)S(1)} %pad_maximum_fusion.4), channel_id=1, source_target_pairs={{0,192},{8,72},{64,128},{72,8},{128,64},{136,200},{192,0},{200,136... | collective-permute-start | bytes 1179656 | tf_op jit(solution)/shard_map/ppermute | solution.py:172
  75.5 7.3 %collective-permute-start.14 = (f32[4,64,384]{2,1,0:T(8,128)S(1)}, f32[4,64,384]{2,1,0:T(8,128)S(1)}, u32[]{:S(2)}, u32[]{:S(2)}) collective-permute-start(f32[4,64,384]{2,1,0:T(8,128)S(1)} %add.84), channel_id=1, source_target_pairs={{0,6},{8,10},{2,4},{10,8},{4,2},{12,14},{6,0},{14,12},{1,7},{9,11}... | collective-permute-start | bytes 1179656 | tf_op jit(solution)/shard_map/ppermute | solution.py:171
  82.1 7.7 %collective-permute-start.8 = (f32[2,64,768]{2,1,0:T(8,128)S(1)}, f32[2,64,768]{2,1,0:T(8,128)S(1)}, u32[]{:S(2)}, u32[]{:S(2)}) collective-permute-start(f32[2,64,768]{2,1,0:T(8,128)S(1)} %pad_maximum_fusion.3), channel_id=1, source_target_pairs={{0,192},{8,72},{64,128},{72,8},{128,64},{136,200},{192,0},{200,136... | collective-permute-start | bytes 1179656 | tf_op jit(solution)/shard_map/ppermute | solution.py:172
  82.3 16.4 %collective-permute-start.22 = (f32[2,128,768]{2,1,0:T(8,128)S(1)}, f32[2,128,768]{2,1,0:T(8,128)S(1)}, u32[]{:S(2)}, u32[]{:S(2)}) collective-permute-start(f32[2,128,768]{2,1,0:T(8,128)S(1)} %pad_maximum_fusion.2.w), channel_id=1, source_target_pairs={{0,64},{8,200},{64,0},{72,136},{128,192},{136,72},{192,128},{200,8... | collective-permute-start | bytes 2359304 | tf_op jit(solution)/shard_map/ppermute | solution.py:172
  82.9 15.8 %collective-permute-start.15 = (f32[4,128,384]{2,1,0:T(8,128)S(1)}, f32[4,128,384]{2,1,0:T(8,128)S(1)}, u32[]{:S(2)}, u32[]{:S(2)}) collective-permute-start(f32[4,128,384]{2,1,0:T(8,128)S(1)} %pad_maximum_fusion.1.q), channel_id=1, source_target_pairs={{0,2},{8,14},{2,0},{10,12},{4,6},{12,10},{6,4},{14,8},{1,3},{9,15}... | collective-permute-start | bytes 2359304 | tf_op jit(solution)/shard_map/ppermute | solution.py:171
  89.9 17.2 %collective-permute-start.9 = (f32[2,128,768]{2,1,0:T(8,128)S(1)}, f32[2,128,768]{2,1,0:T(8,128)S(1)}, u32[]{:S(2)}, u32[]{:S(2)}) collective-permute-start(f32[2,128,768]{2,1,0:T(8,128)S(1)} %pad_maximum_fusion.w), channel_id=1, source_target_pairs={{0,64},{8,200},{64,0},{72,136},{128,192},{136,72},{192,128},{200,8... | collective-permute-start | bytes 2359304 | tf_op jit(solution)/shard_map/ppermute | solution.py:172
  109.1 2.2 %collective-permute-start.23 = (f32[192,768]{1,0:T(8,128)S(1)}, f32[192,768]{1,0:T(8,128)S(1)}, u32[]{:S(2)}, u32[]{:S(2)}) collective-permute-start(f32[192,768]{1,0:T(8,128)S(1)} %get-tuple-element.30), channel_id=1, source_target_pairs={{0,8},{8,0},{1,9},{9,1},{2,10},{10,2},{3,11},{11,3},{4,12},{12,4},... | collective-permute-start | bytes 1769480 | tf_op jit(solution)/shard_map/ppermute | solution.py:202

commit v4 on v3

--- a/solution.py
+++ b/solution.py
@@ -14,7 +14,7 @@
 SWAP = [(0, 1), (1, 0)]
 FREE = pl.CostEstimate(flops=0, bytes_accessed=0, transcendentals=0)
 
-CHUNKS = (((0, 1), True), ((2, 3), True))
+CHUNKS = (((0, 1), 'xxz'), ((2,), 'xxz'), ((3,), 'xzz'))
 
 
 def partner(i, bit):
@@ -45,17 +45,17 @@
     return (i + 1) // 2 % 2 * (2 - c) + i // 2 * (1 + c)
 
 
-def own_piece(pos, x_first):
+def own_piece(pos, order):
     x, zh = bits(pos[1], pos[0]), bits(pos[2], pos[0])
-    return 2 * x + zh // 2 if x_first else 2 * zh + x // 2
+    return {"xxz": 2 * x + zh // 2, "xzz": x // 2 * 4 + zh, "zzx": 2 * zh + x // 2}[order]
 
 
 def row(at, own, size):
     return pl.multiple_of((own ^ at) * size, size)
 
 
-def out_kernel(x_first, pos, g_own, g_other, b_own, b_other, keep, send, whole):
-    own = own_piece(pos, x_first)
+def out_kernel(order, pos, g_own, g_other, b_own, b_other, keep, send, whole):
+    own = own_piece(pos, order)
     g = jnp.concatenate([g_own[...], g_other[...]], axis=0).T
     basis = jnp.concatenate([b_own[...], b_other[...]], axis=0)
     whole[...] = dot3(g, basis, ((1,), (0,)))
@@ -65,11 +65,11 @@
 
 
 def rotate_out(pos, chunk, base, g_own, g_other, b_own, b_other):
-    (images, x_first), (feat, cols) = chunk, b_own.shape
+    (images, order), (feat, cols) = chunk, b_own.shape
     n, first = len(images), images[0] - base
     spec = lambda: pl.BlockSpec((feat, cols), lambda i, pos: (0, 0))
     return pl.pallas_call(
-        functools.partial(out_kernel, x_first),
+        functools.partial(out_kernel, order),
         grid_spec=pltpu.PrefetchScalarGridSpec(
             num_scalar_prefetch=1,
             grid=(n,),
@@ -117,12 +117,12 @@
 
 
 def tile_kernel(chunk, first, pos, w, v, q, p, *rest):
-    images, x_first = chunk
+    images, order = chunk
     if first:
         own, other, left, right = rest
     else:
         own_in, other_in, own, other, left, right = rest
-    own_out, own_y = own_piece(pos, x_first), bits(pos[3], pos[0])
+    own_out, own_y = own_piece(pos, order), bits(pos[3], pos[0])
     size = TOK // 4
     total = None
     for i, image in enumerate(images):
@@ -212,13 +212,14 @@
     grads_of = {0: (0, *swapped(0, ahead, None))}
 
     def output_side(i, token):
-        images, x_first = chunk = CHUNKS[i]
-        along = [[("x", 0), ("x", 1)], [("zh", 0), ("zh", 1)]][:: 1 if x_first else -1]
+        images, order = chunk = CHUNKS[i]
+        left = {"x": [("x", 0), ("x", 1)], "z": [("zh", 0), ("zh", 1)]}
+        steps = [left[axis].pop(0) for axis in order]
         part = 0 if i == 0 else 1
         if part not in grads_of:
             grads_of[1] = (ahead, *swapped(ahead, 4 - ahead, token))
         parts = rotate_out(after(pos, token), chunk, *grads_of[part], basis_out, basis_out_other)
-        return travel(parts, along[0] + along[1][:1], along[1][1])
+        return travel(parts, steps, (left["x"] + left["z"])[0])
 
     def input_side(token):
         own = after(basis_in_t, token)

time: 112 us -> 112 us (level)
  starting transfers between devices: 31.8 us -> 48.3 us
  waiting for transfers between devices: 60.3 us -> 45.3 us
  local copies, waits for them, and re-layouts: 5.18 us -> 2.12 us
    ppermute x14 -> x21, starting transfers between devices: 21 us -> 32.4 us  [exchange(): lax.ppermute(a, (axis, 'c'), swap_pairs(step, lambda i, c: 2 * i + c))]
    ppermute x14 -> x21, waiting for transfers between devices: 48.8 us -> 39.8 us  [exchange(): lax.ppermute(a, (axis, 'c'), swap_pairs(step, lambda i, c: 2 * i + c))]
    ppermute x1, waiting for transfers between devices: 6.6 us -> 0.01 us  [exchange(): return lax.ppermute(a, axis, SWAP)]
    ppermute x5, starting transfers between devices: 4.02 us -> 8.61 us  [local(): to_other = lambda a: lax.ppermute(a, 'c', SWAP)]
    unnamed x6 -> x8, local copies, waits for them, and re-layouts: 2.79 us -> 0.01 us
    ppermute x4, waiting for transfers between devices: 0.01 us -> 1.21 us  [exchange(): return lax.ppermute(a, ('c', 'y'), swap_pairs(step, lambda i, c: 4 * c + i))]
    pallas_call x2 -> x3, Pallas kernels: 3.96 us -> 4.65 us  [tiles(): pl.pallas_call(functools.partial(tile_kernel, chunk, first), grid_spec=pl...]
    pallas_call x2 -> x3, Pallas kernels: 4.96 us -> 5.32 us  [rotate_out(): pl.pallas_call(functools.partial(out_kernel, order), grid_spec=pltpu.Pref...]
  transfers between devices with their start and end apart: 24 -> 31, of which waited for: 15 -> 15; matrix products, arithmetic and copies ran while one was open for 3% -> 3% of each run, Pallas kernels for 8% -> 9%
where the time goes in v4:
time: 112 us
  starting transfers between devices  48.3 us (43%)
  waiting for transfers between devices  45.3 us (40%)
  Pallas kernels  13.9 us (12%)
  local copies, waits for them, and re-layouts  2.12 us (2%)
  other arithmetic  1.66 us (1%)
    ppermute x21, waiting for transfers between devices, exchange(): lax.ppermute(a, (axis, 'c'), swap_pairs(step, lambda i, c: 2 * i + c))  39.8 us
    ppermute x21, starting transfers between devices, exchange(): lax.ppermute(a, (axis, 'c'), swap_pairs(step, lambda i, c: 2 * i + c))  32.4 us
    ppermute x5, starting transfers between devices, local(): to_other = lambda a: lax.ppermute(a, 'c', SWAP)  8.61 us
    ppermute x4, starting transfers between devices, exchange(): return lax.ppermute(a, ('c', 'y'), swap_pairs(step, lambda i, c: 4 * c + i))  6.32 us
    pallas_call x3, Pallas kernels, rotate_out(): pl.pallas_call(functools.partial(out_kernel, order), grid_spec=pltpu.Pref...  5.32 us
    pallas_call x3, Pallas kernels, tiles(): pl.pallas_call(functools.partial(tile_kernel, chunk, first), grid_spec=pl...  4.65 us
    ppermute x5, waiting for transfers between devices, local(): to_other = lambda a: lax.ppermute(a, 'c', SWAP)  4.31 us
    pallas_call x1, Pallas kernels, rotate_in(): pl.pallas_call(in_kernel, grid_spec=pltpu.PrefetchScalarGridSpec(num_scal...  3.96 us
  transfers between devices with their start and end apart: 31, of which 15 were waited for; matrix products, arithmetic and copies ran while one was open for 3% of the time, Pallas kernels for 9%

profile of v4, /device:TPU:1, one launch (start us, length us, event | category | flops | bytes accessed | tf_op | source)
XLA Modules:
  0.0 111.6 jit_solution(10538732021479441910)
XLA Ops:
  0.0 3.2 %collective-permute-start.1 = (f32[192,768]{1,0:T(8,128)}, f32[192,768]{1,0:T(8,128)S(1)}, u32[]{:S(2)}, u32[]{:S(2)}) collective-permute-start(f32[192,768]{1,0:T(8,128)} %b_own.5), channel_id=1, source_target_pairs={{0,8},{8,0},{1,9},{9,1},{2,10},{10,2},{3,11},{11,3},{4,12},{12,4},... | collective-permute-start | bytes 1769480 | tf_op jit(solution)/shard_map/ppermute | solution.py:202
  3.2 2.0 %dynamic-slice_bitcast_fusion = (f32[192,512]{1,0:T(8,128)}, f32[192,512]{1,0:T(8,128)S(1)}) fusion(f32[2048,192]{0,1:T(8,128)} %param.5, s32[]{:T(128)S(6)} %select_n.13, s32[]{:T(128)S(6)} %select_n.12), kind=kLoop, calls=%fused_computation.11 | loop fusion | bytes 1572872 | tf_op jit(solution)/shard_map/dynamic_slice | solution.py:207
  5.3 0.0 collective-permute-start
  5.3 0.1 pad_add_fusion.pos
  5.4 1.8 %collective-permute-done.g_other = f32[192,512]{1,0:T(8,128)S(1)} collective-permute-done((f32[192,512]{1,0:T(8,128)}, f32[192,512]{1,0:T(8,128)S(1)}, u32[]{:S(2)}, u32[]{:S(2)}) %collective-permute-start) | collective-permute-done | bytes 393248 | tf_op jit(solution)/shard_map/ppermute | solution.py:202
  7.2 0.0 collective-permute-done.1.b_other
  7.2 2.4 %shard_map.46 = (f32[2,128,768]{2,1,0:T(8,128)S(1)}, f32[2,128,768]{2,1,0:T(8,128)S(1)}) custom-call(s32[4]{0:T(128)S(1)} %pad_add_fusion.pos, f32[192,512]{1,0:T(8,128)S(1)} %get-tuple-element.46.g_own, f32[192,512]{1,0:T(8,128)S(1)} %collective-permute-done.g_other, f32[192,768]{1,0:T(8,128)S(1)} %copy-done.1, f32[192,768]{1,0:T(8,128)S(1)} %collective-permute-done.1.b_other), custom_call_target="tpu_custom_call" | custom-call | tf_op jit(solution)/shard_map/pallas_call | solution.py:71
  9.7 0.1 constant_dynamic-slice_fusion
  9.8 0.2 collective-permute-start.2
  10.0 0.7 collective-permute-start.23
  10.7 0.8 collective-permute-done.2.g_other
  11.6 1.4 %shard_map.47 = (f32[1,128,768]{2,1,0:T(8,128)S(1)}, f32[1,128,768]{2,1,0:T(8,128)S(1)}) custom-call(s32[4]{0:T(128)S(1)} %pad_add_fusion.pos, f32[192,512]{1,0:T(8,128)S(1)} %get-tuple-element.44.g_own, f32[192,512]{1,0:T(8,128)S(1)} %collective-permute-done.2.g_other, f32[192,768]{1,0:T(8,128)S(1)} %copy-done.1, f32[192,768]{1,0:T(8,128)S(1)} %collective-permute-done.1.b_other), custom_call_target="tpu_custom_call" | custom-call | tf_op jit(solution)/shard_map/pallas_call | solution.py:71
  13.0 1.4 %shard_map.48 = (f32[1,128,768]{2,1,0:T(8,128)S(1)}, f32[1,128,768]{2,1,0:T(8,128)S(1)}) custom-call(s32[4]{0:T(128)S(1)} %pad_add_fusion.pos, f32[192,512]{1,0:T(8,128)S(1)} %get-tuple-element.44.g_own, f32[192,512]{1,0:T(8,128)S(1)} %collective-permute-done.2.g_other, f32[192,768]{1,0:T(8,128)S(1)} %copy-done.1, f32[192,768]{1,0:T(8,128)S(1)} %collective-permute-done.1.b_other), custom_call_target="tpu_custom_call" | custom-call | tf_op jit(solution)/shard_map/pallas_call | solution.py:71
  14.5 0.2 collective-permute-start.10
  14.7 1.0 collective-permute-start.3
  15.7 1.6 %collective-permute-start.16 = (f32[1,128,768]{2,1,0:T(8,128)S(1)}, f32[1,128,768]{2,1,0:T(8,128)S(1)}, u32[]{:S(2)}, u32[]{:S(2)}) collective-permute-start(f32[1,128,768]{2,1,0:T(8,128)S(1)} %get-tuple-element.26), channel_id=1, source_target_pairs={{0,64},{8,200},{64,0},{72,136},{128,192},{136,72},{192,128},{200,8... | collective-permute-start | bytes 1179656 | tf_op jit(solution)/shard_map/ppermute | solution.py:172
  17.4 4.0 %shard_map.49 = (f32[4,128,384]{2,1,0:T(8,128)S(1)}, f32[4,128,384]{2,1,0:T(8,128)S(1)}) custom-call(s32[4]{0:T(128)S(1)} %pad_add_fusion.pos, f32[2048,768]{1,0:T(8,128)S(1)} %copy-done, f32[192,768]{1,0:T(8,128)S(1)} %bitcast.13, f32[192,768]{1,0:T(8,128)S(1)} %collective-permute-done.10.b_other), custom_call_target="tpu_custom_call" | custom-call | tf_op jit(solution)/shard_map/pallas_call | solution.py:104
  21.4 1.9 %collective-permute-start.11 = (f32[4,128,384]{2,1,0:T(8,128)S(1)}, f32[4,128,384]{2,1,0:T(8,128)S(1)}, u32[]{:S(2)}, u32[]{:S(2)}) collective-permute-start(f32[4,128,384]{2,1,0:T(8,128)S(1)} %get-tuple-element.32), channel_id=1, source_target_pairs={{0,2},{8,14},{2,0},{10,12},{4,6},{12,10},{6,4},{14,8},{1,3},{9,15}... | collective-permute-start | bytes 2359304 | tf_op jit(solution)/shard_map/ppermute | solution.py:171
  23.3 0.1 slice_add_fusion.1
  23.4 0.1 collective-permute-start.24
  23.5 2.8 %collective-permute-done.3 = f32[1,128,768]{2,1,0:T(8,128)S(1)} collective-permute-done((f32[1,128,768]{2,1,0:T(8,128)S(1)}, f32[1,128,768]{2,1,0:T(8,128)S(1)}, u32[]{:S(2)}, u32[]{:S(2)}) %collective-permute-start.3) | collective-permute-done | bytes 393248 | tf_op jit(solution)/shard_map/ppermute | solution.py:172
  26.3 4.4 %collective-permute-start.4 = (f32[1,64,768]{2,1,0:T(8,128)S(1)}, f32[1,64,768]{2,1,0:T(8,128)S(1)}, u32[]{:S(2)}, u32[]{:S(2)}) collective-permute-start(f32[1,64,768]{2,1,0:T(8,128)S(1)} %get-tuple-element.50), channel_id=1, source_target_pairs={{0,16},{8,56},{16,0},{24,40},{32,48},{40,24},{48,32},{56,8},{1,17}... | collective-permute-start | bytes 589832 | tf_op jit(solution)/shard_map/ppermute | solution.py:172
  30.7 3.9 %collective-permute-done.16 = f32[1,128,768]{2,1,0:T(8,128)S(1)} collective-permute-done((f32[1,128,768]{2,1,0:T(8,128)S(1)}, f32[1,128,768]{2,1,0:T(8,128)S(1)}, u32[]{:S(2)}, u32[]{:S(2)}) %collective-permute-start.16) | collective-permute-done | bytes 393248 | tf_op jit(solution)/shard_map/ppermute | solution.py:172
  34.6 0.1 collective-permute-start.17
  34.7 0.0 collective-permute-done.24
  34.7 4.3 %collective-permute-start.25 = (f32[2,32,768]{2,1,0:T(8,128)S(1)}, f32[2,32,768]{2,1,0:T(8,128)S(1)}, u32[]{:S(2)}, u32[]{:S(2)}) collective-permute-start(f32[2,32,768]{2,1,0:T(8,128)S(1)} %slice_add_fusion.4), channel_id=1, source_target_pairs={{0,16},{8,56},{16,0},{24,40},{32,48},{40,24},{48,32},{56,8},{1,17}... | collective-permute-start | bytes 589832 | tf_op jit(solution)/shard_map/ppermute | solution.py:172
  39.0 1.5 %collective-permute-start.12 = (f32[4,64,384]{2,1,0:T(8,128)S(1)}, f32[4,64,384]{2,1,0:T(8,128)S(1)}, u32[]{:S(2)}, u32[]{:S(2)}) collective-permute-start(f32[4,64,384]{2,1,0:T(8,128)S(1)} %slice_add_fusion.2), channel_id=1, source_target_pairs={{0,6},{8,10},{2,4},{10,8},{4,2},{12,14},{6,0},{14,12},{1,7},{9,11}... | collective-permute-start | bytes 1179656 | tf_op jit(solution)/shard_map/ppermute | solution.py:171
  40.5 2.1 %collective-permute-start.18 = (f32[1,32,768]{2,1,0:T(8,128)S(1)}, f32[1,32,768]{2,1,0:T(8,128)S(1)}, u32[]{:S(2)}, u32[]{:S(2)}) collective-permute-start(f32[1,32,768]{2,1,0:T(8,128)S(1)} %slice_add_fusion.10), channel_id=1, source_target_pairs={{0,16},{8,56},{16,0},{24,40},{32,48},{40,24},{48,32},{56,8},{1,17}... | collective-permute-start | bytes 294920 | tf_op jit(solution)/shard_map/ppermute | solution.py:172
  42.6 1.1 %collective-permute-done.25 = f32[2,32,768]{2,1,0:T(8,128)S(1)} collective-permute-done((f32[2,32,768]{2,1,0:T(8,128)S(1)}, f32[2,32,768]{2,1,0:T(8,128)S(1)}, u32[]{:S(2)}, u32[]{:S(2)}) %collective-permute-start.25) | collective-permute-done | bytes 196640 | tf_op jit(solution)/shard_map/ppermute | solution.py:172
  43.7 1.7 %collective-permute-start.26 = (f32[2,32,768]{2,1,0:T(8,128)S(1)}, f32[2,32,768]{2,1,0:T(8,128)S(1)}, u32[]{:S(2)}, u32[]{:S(2)}) collective-permute-start(f32[2,32,768]{2,1,0:T(8,128)S(1)} %fusion.1), channel_id=1, source_target_pairs={{0,48},{8,24},{16,32},{24,8},{32,16},{40,56},{48,0},{56,40},{1,49}... | collective-permute-start | bytes 589832 | tf_op jit(solution)/shard_map/ppermute | solution.py:172
  45.5 0.6 collective-permute-done.12
  46.0 0.1 fusion
  46.1 1.0 collective-permute-start.13
  47.1 0.0 collective-permute-done.4
  47.1 1.3 %collective-permute-start.5 = (f32[1,32,768]{2,1,0:T(8,128)S(1)}, f32[1,32,768]{2,1,0:T(8,128)S(1)}, u32[]{:S(2)}, u32[]{:S(2)}) collective-permute-start(f32[1,32,768]{2,1,0:T(8,128)S(1)} %slice_add_fusion.12), channel_id=1, source_target_pairs={{0,48},{8,24},{16,32},{24,8},{32,16},{40,56},{48,0},{56,40},{1,49}... | collective-permute-start | bytes 294920 | tf_op jit(solution)/shard_map/ppermute | solution.py:172
  48.4 4.8 %collective-permute-done.26 = f32[2,32,768]{2,1,0:T(8,128)S(1)} collective-permute-done((f32[2,32,768]{2,1,0:T(8,128)S(1)}, f32[2,32,768]{2,1,0:T(8,128)S(1)}, u32[]{:S(2)}, u32[]{:S(2)}) %collective-permute-start.26) | collective-permute-done | bytes 196640 | tf_op jit(solution)/shard_map/ppermute | solution.py:172
  53.3 2.4 %collective-permute-start.27 = (f32[2,32,768]{2,1,0:T(8,128)S(1)}, f32[2,32,768]{2,1,0:T(8,128)S(1)}, u32[]{:S(2)}, u32[]{:S(2)}) collective-permute-start(f32[2,32,768]{2,1,0:T(8,128)S(1)} %add.114), channel_id=1, source_target_pairs={{0,16},{8,56},{16,0},{24,40},{32,48},{40,24},{48,32},{56,8},{1,17}... | collective-permute-start | bytes 589832 | tf_op jit(solution)/shard_map/ppermute | solution.py:172
  55.7 3.2 %collective-permute-start.19 = (f32[1,32,768]{2,1,0:T(8,128)S(1)}, f32[1,32,768]{2,1,0:T(8,128)S(1)}, u32[]{:S(2)}, u32[]{:S(2)}) collective-permute-start(f32[1,32,768]{2,1,0:T(8,128)S(1)} %fusion.2), channel_id=1, source_target_pairs={{0,48},{8,24},{16,32},{24,8},{32,16},{40,56},{48,0},{56,40},{1,49}... | collective-permute-start | bytes 294920 | tf_op jit(solution)/shard_map/ppermute | solution.py:172
  58.8 10.7 %collective-permute-done.27 = f32[2,32,768]{2,1,0:T(8,128)S(1)} collective-permute-done((f32[2,32,768]{2,1,0:T(8,128)S(1)}, f32[2,32,768]{2,1,0:T(8,128)S(1)}, u32[]{:S(2)}, u32[]{:S(2)}) %collective-permute-start.27) | collective-permute-done | bytes 196640 | tf_op jit(solution)/shard_map/ppermute | solution.py:172
  69.6 2.0 %collective-permute-start.28 = (f32[2,64,768]{2,1,0:T(8,128)S(1)}, f32[2,64,768]{2,1,0:T(8,128)S(1)}, u32[]{:S(2)}, u32[]{:S(2)}) collective-permute-start(f32[2,64,768]{2,1,0:T(8,128)S(1)} %pad_maximum_fusion.4), channel_id=1, source_target_pairs={{0,192},{8,72},{64,128},{72,8},{128,64},{136,200},{192,0},{200,136... | collective-permute-start | bytes 1179656 | tf_op jit(solution)/shard_map/ppermute | solution.py:172
  71.7 0.3 collective-permute-start.14
  72.0 0.5 collective-permute-start.6
  72.5 1.1 %collective-permute-start.20 = (f32[1,32,768]{2,1,0:T(8,128)S(1)}, f32[1,32,768]{2,1,0:T(8,128)S(1)}, u32[]{:S(2)}, u32[]{:S(2)}) collective-permute-start(f32[1,32,768]{2,1,0:T(8,128)S(1)} %add.108), channel_id=1, source_target_pairs={{0,16},{8,56},{16,0},{24,40},{32,48},{40,24},{48,32},{56,8},{1,17}... | collective-permute-start | bytes 294920 | tf_op jit(solution)/shard_map/ppermute | solution.py:172
  73.6 4.5 %collective-permute-done.6 = f32[1,32,768]{2,1,0:T(8,128)S(1)} collective-permute-done((f32[1,32,768]{2,1,0:T(8,128)S(1)}, f32[1,32,768]{2,1,0:T(8,128)S(1)}, u32[]{:S(2)}, u32[]{:S(2)}) %collective-permute-start.6) | collective-permute-done | bytes 98336 | tf_op jit(solution)/shard_map/ppermute | solution.py:172
  78.1 0.1 collective-permute-start.7
  78.3 1.5 %collective-permute-start.21 = (f32[1,64,768]{2,1,0:T(8,128)S(1)}, f32[1,64,768]{2,1,0:T(8,128)S(1)}, u32[]{:S(2)}, u32[]{:S(2)}) collective-permute-start(f32[1,64,768]{2,1,0:T(8,128)S(1)} %pad_maximum_fusion.6), channel_id=1, source_target_pairs={{0,192},{8,72},{64,128},{72,8},{128,64},{136,200},{192,0},{200,136... | collective-permute-start | bytes 589832 | tf_op jit(solution)/shard_map/ppermute | solution.py:172
  79.8 0.1 pad_maximum_fusion.1.w
  79.9 3.1 %collective-permute-start.29 = (f32[2,128,768]{2,1,0:T(8,128)S(1)}, f32[2,128,768]{2,1,0:T(8,128)S(1)}, u32[]{:S(2)}, u32[]{:S(2)}) collective-permute-start(f32[2,128,768]{2,1,0:T(8,128)S(1)} %pad_maximum_fusion.1.w), channel_id=1, source_target_pairs={{0,64},{8,200},{64,0},{72,136},{128,192},{136,72},{192,128},{200,8... | collective-permute-start | bytes 2359304 | tf_op jit(solution)/shard_map/ppermute | solution.py:172
  83.0 0.1 pad_maximum_fusion.q
  83.0 2.6 %collective-permute-start.15 = (f32[4,128,384]{2,1,0:T(8,128)S(1)}, f32[4,128,384]{2,1,0:T(8,128)S(1)}, u32[]{:S(2)}, u32[]{:S(2)}) collective-permute-start(f32[4,128,384]{2,1,0:T(8,128)S(1)} %pad_maximum_fusion.q), channel_id=1, source_target_pairs={{0,2},{8,14},{2,0},{10,12},{4,6},{12,10},{6,4},{14,8},{1,3},{9,15}... | collective-permute-start | bytes 2359304 | tf_op jit(solution)/shard_map/ppermute | solution.py:171
  85.6 0.1 collective-permute-start.8
  85.8 0.6 collective-permute-start.22
  86.4 6.1 %collective-permute-done.8 = f32[1,64,768]{2,1,0:T(8,128)S(1)} collective-permute-done((f32[1,64,768]{2,1,0:T(8,128)S(1)}, f32[1,64,768]{2,1,0:T(8,128)S(1)}, u32[]{:S(2)}, u32[]{:S(2)}) %collective-permute-start.8) | collective-permute-done | bytes 196640 | tf_op jit(solution)/shard_map/ppermute | solution.py:172
  92.5 0.6 collective-permute-start.9
  93.1 1.6 %collective-permute-done.29.v = f32[2,128,768]{2,1,0:T(8,128)S(1)} collective-permute-done((f32[2,128,768]{2,1,0:T(8,128)S(1)}, f32[2,128,768]{2,1,0:T(8,128)S(1)}, u32[]{:S(2)}, u32[]{:S(2)}) %collective-permute-start.29) | collective-permute-done | bytes 786464 | tf_op jit(solution)/shard_map/ppermute | solution.py:172
  94.7 0.6 collective-permute-done.15.p
  95.3 2.0 %shard_map.50 = (f32[192,768]{1,0:T(8,128)S(1)}, f32[192,768]{1,0:T(8,128)S(1)}) custom-call(s32[4]{0:T(128)S(1)} %pad_add_fusion.pos, f32[2,128,768]{2,1,0:T(8,128)S(1)} %pad_maximum_fusion.1.w, f32[2,128,768]{2,1,0:T(8,128)S(1)} %collective-permute-done.29.v, f32[4,128,384]{2,1,0:T(8,128)S(1)} %pad_maximum_fusion.q, ...), custom_call_target="tpu_custom_call" | custom-call | tf_op jit(solution)/shard_map/pallas_call | solution.py:152
  97.3 1.5 %collective-permute-done.22.v = f32[1,128,768]{2,1,0:T(8,128)S(1)} collective-permute-done((f32[1,128,768]{2,1,0:T(8,128)S(1)}, f32[1,128,768]{2,1,0:T(8,128)S(1)}, u32[]{:S(2)}, u32[]{:S(2)}) %collective-permute-start.22) | collective-permute-done | bytes 393248 | tf_op jit(solution)/shard_map/ppermute | solution.py:172
  98.8 1.3 %shard_map.51 = (f32[192,768]{1,0:T(8,128)S(1)}, f32[192,768]{1,0:T(8,128)S(1)}) custom-call(s32[4]{0:T(128)S(1)} %pad_add_fusion.pos, f32[1,128,768]{2,1,0:T(8,128)S(1)} %pad_maximum_fusion.3.w, f32[1,128,768]{2,1,0:T(8,128)S(1)} %collective-permute-done.22.v, f32[4,128,384]{2,1,0:T(8,128)S(1)} %pad_maximum_fusion.q, ...), custom_call_target="tpu_custom_call" | custom-call | tf_op jit(solution)/shard_map/pallas_call | solution.py:152
  100.1 2.7 %collective-permute-done.9.v = f32[1,128,768]{2,1,0:T(8,128)S(1)} collective-permute-done((f32[1,128,768]{2,1,0:T(8,128)S(1)}, f32[1,128,768]{2,1,0:T(8,128)S(1)}, u32[]{:S(2)}, u32[]{:S(2)}) %collective-permute-start.9) | collective-permute-done | bytes 393248 | tf_op jit(solution)/shard_map/ppermute | solution.py:172
  102.9 1.3 %shard_map.52 = (f32[192,768]{1,0:T(8,128)S(1)}, f32[192,768]{1,0:T(8,128)S(1)}) custom-call(s32[4]{0:T(128)S(1)} %pad_add_fusion.pos, f32[1,128,768]{2,1,0:T(8,128)S(1)} %pad_maximum_fusion.2.w, f32[1,128,768]{2,1,0:T(8,128)S(1)} %collective-permute-done.9.v, f32[4,128,384]{2,1,0:T(8,128)S(1)} %pad_maximum_fusion.q, ...), custom_call_target="tpu_custom_call" | custom-call | tf_op jit(solution)/shard_map/pallas_call | solution.py:152
  104.2 4.9 %collective-permute-start.30 = (f32[192,768]{1,0:T(8,128)S(1)}, f32[192,768]{1,0:T(8,128)S(1)}, u32[]{:S(2)}, u32[]{:S(2)}) collective-permute-start(f32[192,768]{1,0:T(8,128)S(1)} %get-tuple-element.40), channel_id=1, source_target_pairs={{0,8},{8,0},{1,9},{9,1},{2,10},{10,2},{3,11},{11,3},{4,12},{12,4},... | collective-permute-start | bytes 1769480 | tf_op jit(solution)/shard_map/ppermute | solution.py:202
  109.1 1.6 %collective-permute-done.30 = f32[192,768]{1,0:T(8,128)S(1)} collective-permute-done((f32[192,768]{1,0:T(8,128)S(1)}, f32[192,768]{1,0:T(8,128)S(1)}, u32[]{:S(2)}, u32[]{:S(2)}) %collective-permute-start.30) | collective-permute-done | bytes 589856 | tf_op jit(solution)/shard_map/ppermute | solution.py:202
  110.7 0.9 multiply_bitcast_fusion
  (39 shorter events, 0.5 us)
Async XLA Ops:
  0.0 7.2 %copy-start.1 = (f32[192,768]{1,0:T(8,128)S(1)}, f32[192,768]{1,0:T(8,128)}, u32[]{:S(2)}) copy-start(f32[192,768]{1,0:T(8,128)} %b_own.5) | copy-start | bytes 1769476
  0.0 7.2 %collective-permute-start.1 = (f32[192,768]{1,0:T(8,128)}, f32[192,768]{1,0:T(8,128)S(1)}, u32[]{:S(2)}, u32[]{:S(2)}) collective-permute-start(f32[192,768]{1,0:T(8,128)} %b_own.5), channel_id=1, source_target_pairs={{0,8},{8,0},{1,9},{9,1},{2,10},{10,2},{3,11},{11,3},{4,12},{12,4},... | collective-permute-start | bytes 1769480 | tf_op jit(solution)/shard_map/ppermute | solution.py:202
  3.2 6.4 %copy-start.3 = (f32[2048,192]{0,1:T(8,128)S(1)}, f32[2048,192]{0,1:T(8,128)}, u32[]{:S(2)}) copy-start(f32[2048,192]{0,1:T(8,128)} %param.5) | copy-start | bytes 4718596
  5.3 1.9 %collective-permute-start = (f32[192,512]{1,0:T(8,128)}, f32[192,512]{1,0:T(8,128)S(1)}, u32[]{:S(2)}, u32[]{:S(2)}) collective-permute-start(f32[192,512]{1,0:T(8,128)} %get-tuple-element.45), channel_id=1, source_target_pairs={{0,8},{8,0},{1,9},{9,1},{2,10},{10,2},{3,11},{11,3},{4,12},{12,4},... | collective-permute-start | bytes 1179656 | tf_op jit(solution)/shard_map/ppermute | solution.py:202
  7.2 10.2 %copy-start = (f32[2048,768]{1,0:T(8,128)S(1)}, f32[2048,768]{1,0:T(8,128)}, u32[]{:S(2)}) copy-start(f32[2048,768]{1,0:T(8,128)} %acts.1) | copy-start | bytes 18874372
  9.8 1.8 %collective-permute-start.2 = (f32[192,512]{1,0:T(8,128)S(1)}, f32[192,512]{1,0:T(8,128)S(1)}, u32[]{:S(2)}, u32[]{:S(2)}) collective-permute-start(f32[192,512]{1,0:T(8,128)S(1)} %get-tuple-element.43), channel_id=1, source_target_pairs={{0,8},{8,0},{1,9},{9,1},{2,10},{10,2},{3,11},{11,3},{4,12},{12,4},... | collective-permute-start | bytes 1179656 | tf_op jit(solution)/shard_map/ppermute | solution.py:202
  10.0 13.3 %collective-permute-start.23 = (f32[2,128,768]{2,1,0:T(8,128)S(1)}, f32[2,128,768]{2,1,0:T(8,128)S(1)}, u32[]{:S(2)}, u32[]{:S(2)}) collective-permute-start(f32[2,128,768]{2,1,0:T(8,128)S(1)} %get-tuple-element.23), channel_id=1, source_target_pairs={{0,64},{8,200},{64,0},{72,136},{128,192},{136,72},{192,128},{200,8... | collective-permute-start | bytes 2359304 | tf_op jit(solution)/shard_map/ppermute | solution.py:172
  11.6 2.9 %copy-start.2 = (f32[768,192]{0,1:T(8,128)S(1)}, f32[768,192]{0,1:T(8,128)}, u32[]{:S(2)}) copy-start(f32[768,192]{0,1:T(8,128)} %param.6) | copy-start | bytes 1769476
  14.5 2.9 %collective-permute-start.10 = (f32[192,768]{1,0:T(8,128)S(1)}, f32[192,768]{1,0:T(8,128)S(1)}, u32[]{:S(2)}, u32[]{:S(2)}) collective-permute-start(f32[192,768]{1,0:T(8,128)S(1)} %bitcast.12), channel_id=1, source_target_pairs={{0,8},{8,0},{1,9},{9,1},{2,10},{10,2},{3,11},{11,3},{4,12},{12,4},... | collective-permute-start | bytes 1769480 | tf_op jit(solution)/shard_map/ppermute | solution.py:202
  14.7 11.5 %collective-permute-start.3 = (f32[1,128,768]{2,1,0:T(8,128)S(1)}, f32[1,128,768]{2,1,0:T(8,128)S(1)}, u32[]{:S(2)}, u32[]{:S(2)}) collective-permute-start(f32[1,128,768]{2,1,0:T(8,128)S(1)} %get-tuple-element.29), channel_id=1, source_target_pairs={{0,64},{8,200},{64,0},{72,136},{128,192},{136,72},{192,128},{200,8... | collective-permute-start | bytes 1179656 | tf_op jit(solution)/shard_map/ppermute | solution.py:172
  15.7 18.8 %collective-permute-start.16 = (f32[1,128,768]{2,1,0:T(8,128)S(1)}, f32[1,128,768]{2,1,0:T(8,128)S(1)}, u32[]{:S(2)}, u32[]{:S(2)}) collective-permute-start(f32[1,128,768]{2,1,0:T(8,128)S(1)} %get-tuple-element.26), channel_id=1, source_target_pairs={{0,64},{8,200},{64,0},{72,136},{128,192},{136,72},{192,128},{200,8... | collective-permute-start | bytes 1179656 | tf_op jit(solution)/shard_map/ppermute | solution.py:172
  21.4 17.6 %collective-permute-start.11 = (f32[4,128,384]{2,1,0:T(8,128)S(1)}, f32[4,128,384]{2,1,0:T(8,128)S(1)}, u32[]{:S(2)}, u32[]{:S(2)}) collective-permute-start(f32[4,128,384]{2,1,0:T(8,128)S(1)} %get-tuple-element.32), channel_id=1, source_target_pairs={{0,2},{8,14},{2,0},{10,12},{4,6},{12,10},{6,4},{14,8},{1,3},{9,15}... | collective-permute-start | bytes 2359304 | tf_op jit(solution)/shard_map/ppermute | solution.py:171
  23.4 11.3 %collective-permute-start.24 = (f32[2,64,768]{2,1,0:T(8,128)S(1)}, f32[2,64,768]{2,1,0:T(8,128)S(1)}, u32[]{:S(2)}, u32[]{:S(2)}) collective-permute-start(f32[2,64,768]{2,1,0:T(8,128)S(1)} %get-tuple-element.42), channel_id=1, source_target_pairs={{0,192},{8,72},{64,128},{72,8},{128,64},{136,200},{192,0},{200,136... | collective-permute-start | bytes 1179656 | tf_op jit(solution)/shard_map/ppermute | solution.py:172
  26.3 20.8 %collective-permute-start.4 = (f32[1,64,768]{2,1,0:T(8,128)S(1)}, f32[1,64,768]{2,1,0:T(8,128)S(1)}, u32[]{:S(2)}, u32[]{:S(2)}) collective-permute-start(f32[1,64,768]{2,1,0:T(8,128)S(1)} %get-tuple-element.50), channel_id=1, source_target_pairs={{0,16},{8,56},{16,0},{24,40},{32,48},{40,24},{48,32},{56,8},{1,17}... | collective-permute-start | bytes 589832 | tf_op jit(solution)/shard_map/ppermute | solution.py:172
  34.6 5.9 %collective-permute-start.17 = (f32[1,64,768]{2,1,0:T(8,128)S(1)}, f32[1,64,768]{2,1,0:T(8,128)S(1)}, u32[]{:S(2)}, u32[]{:S(2)}) collective-permute-start(f32[1,64,768]{2,1,0:T(8,128)S(1)} %get-tuple-element.48), channel_id=1, source_target_pairs={{0,192},{8,72},{64,128},{72,8},{128,64},{136,200},{192,0},{200,136... | collective-permute-start | bytes 589832 | tf_op jit(solution)/shard_map/ppermute | solution.py:172
  34.7 9.0 %collective-permute-start.25 = (f32[2,32,768]{2,1,0:T(8,128)S(1)}, f32[2,32,768]{2,1,0:T(8,128)S(1)}, u32[]{:S(2)}, u32[]{:S(2)}) collective-permute-start(f32[2,32,768]{2,1,0:T(8,128)S(1)} %slice_add_fusion.4), channel_id=1, source_target_pairs={{0,16},{8,56},{16,0},{24,40},{32,48},{40,24},{48,32},{56,8},{1,17}... | collective-permute-start | bytes 589832 | tf_op jit(solution)/shard_map/ppermute | solution.py:172
  39.0 7.0 %collective-permute-start.12 = (f32[4,64,384]{2,1,0:T(8,128)S(1)}, f32[4,64,384]{2,1,0:T(8,128)S(1)}, u32[]{:S(2)}, u32[]{:S(2)}) collective-permute-start(f32[4,64,384]{2,1,0:T(8,128)S(1)} %slice_add_fusion.2), channel_id=1, source_target_pairs={{0,6},{8,10},{2,4},{10,8},{4,2},{12,14},{6,0},{14,12},{1,7},{9,11}... | collective-permute-start | bytes 1179656 | tf_op jit(solution)/shard_map/ppermute | solution.py:171
  40.5 15.1 %collective-permute-start.18 = (f32[1,32,768]{2,1,0:T(8,128)S(1)}, f32[1,32,768]{2,1,0:T(8,128)S(1)}, u32[]{:S(2)}, u32[]{:S(2)}) collective-permute-start(f32[1,32,768]{2,1,0:T(8,128)S(1)} %slice_add_fusion.10), channel_id=1, source_target_pairs={{0,16},{8,56},{16,0},{24,40},{32,48},{40,24},{48,32},{56,8},{1,17}... | collective-permute-start | bytes 294920 | tf_op jit(solution)/shard_map/ppermute | solution.py:172
  43.7 9.5 %collective-permute-start.26 = (f32[2,32,768]{2,1,0:T(8,128)S(1)}, f32[2,32,768]{2,1,0:T(8,128)S(1)}, u32[]{:S(2)}, u32[]{:S(2)}) collective-permute-start(f32[2,32,768]{2,1,0:T(8,128)S(1)} %fusion.1), channel_id=1, source_target_pairs={{0,48},{8,24},{16,32},{24,8},{32,16},{40,56},{48,0},{56,40},{1,49}... | collective-permute-start | bytes 589832 | tf_op jit(solution)/shard_map/ppermute | solution.py:172
  46.1 25.5 %collective-permute-start.13 = (f32[4,64,384]{2,1,0:T(8,128)S(1)}, f32[4,64,384]{2,1,0:T(8,128)S(1)}, u32[]{:S(2)}, u32[]{:S(2)}) collective-permute-start(f32[4,64,384]{2,1,0:T(8,128)S(1)} %fusion), channel_id=1, source_target_pairs={{0,1},{1,0},{2,3},{3,2},{4,5},{5,4},{6,7},{7,6},{8,9},{9,8},{10,11... | collective-permute-start | bytes 1179656 | tf_op jit(solution)/shard_map/ppermute | solution.py:169
  47.1 24.9 %collective-permute-start.5 = (f32[1,32,768]{2,1,0:T(8,128)S(1)}, f32[1,32,768]{2,1,0:T(8,128)S(1)}, u32[]{:S(2)}, u32[]{:S(2)}) collective-permute-start(f32[1,32,768]{2,1,0:T(8,128)S(1)} %slice_add_fusion.12), channel_id=1, source_target_pairs={{0,48},{8,24},{16,32},{24,8},{32,16},{40,56},{48,0},{56,40},{1,49}... | collective-permute-start | bytes 294920 | tf_op jit(solution)/shard_map/ppermute | solution.py:172
  53.3 16.3 %collective-permute-start.27 = (f32[2,32,768]{2,1,0:T(8,128)S(1)}, f32[2,32,768]{2,1,0:T(8,128)S(1)}, u32[]{:S(2)}, u32[]{:S(2)}) collective-permute-start(f32[2,32,768]{2,1,0:T(8,128)S(1)} %add.114), channel_id=1, source_target_pairs={{0,16},{8,56},{16,0},{24,40},{32,48},{40,24},{48,32},{56,8},{1,17}... | collective-permute-start | bytes 589832 | tf_op jit(solution)/shard_map/ppermute | solution.py:172
  55.7 16.8 %collective-permute-start.19 = (f32[1,32,768]{2,1,0:T(8,128)S(1)}, f32[1,32,768]{2,1,0:T(8,128)S(1)}, u32[]{:S(2)}, u32[]{:S(2)}) collective-permute-start(f32[1,32,768]{2,1,0:T(8,128)S(1)} %fusion.2), channel_id=1, source_target_pairs={{0,48},{8,24},{16,32},{24,8},{32,16},{40,56},{48,0},{56,40},{1,49}... | collective-permute-start | bytes 294920 | tf_op jit(solution)/shard_map/ppermute | solution.py:172
  69.6 10.2 %collective-permute-start.28 = (f32[2,64,768]{2,1,0:T(8,128)S(1)}, f32[2,64,768]{2,1,0:T(8,128)S(1)}, u32[]{:S(2)}, u32[]{:S(2)}) collective-permute-start(f32[2,64,768]{2,1,0:T(8,128)S(1)} %pad_maximum_fusion.4), channel_id=1, source_target_pairs={{0,192},{8,72},{64,128},{72,8},{128,64},{136,200},{192,0},{200,136... | collective-permute-start | bytes 1179656 | tf_op jit(solution)/shard_map/ppermute | solution.py:172
  71.7 11.3 %collective-permute-start.14 = (f32[4,64,384]{2,1,0:T(8,128)S(1)}, f32[4,64,384]{2,1,0:T(8,128)S(1)}, u32[]{:S(2)}, u32[]{:S(2)}) collective-permute-start(f32[4,64,384]{2,1,0:T(8,128)S(1)} %add.102), channel_id=1, source_target_pairs={{0,6},{8,10},{2,4},{10,8},{4,2},{12,14},{6,0},{14,12},{1,7},{9,11}... | collective-permute-start | bytes 1179656 | tf_op jit(solution)/shard_map/ppermute | solution.py:171
  72.0 6.1 %collective-permute-start.6 = (f32[1,32,768]{2,1,0:T(8,128)S(1)}, f32[1,32,768]{2,1,0:T(8,128)S(1)}, u32[]{:S(2)}, u32[]{:S(2)}) collective-permute-start(f32[1,32,768]{2,1,0:T(8,128)S(1)} %fusion.3), channel_id=1, source_target_pairs={{0,192},{8,72},{64,128},{72,8},{128,64},{136,200},{192,0},{200,136... | collective-permute-start | bytes 294920 | tf_op jit(solution)/shard_map/ppermute | solution.py:172
  72.5 5.8 %collective-permute-start.20 = (f32[1,32,768]{2,1,0:T(8,128)S(1)}, f32[1,32,768]{2,1,0:T(8,128)S(1)}, u32[]{:S(2)}, u32[]{:S(2)}) collective-permute-start(f32[1,32,768]{2,1,0:T(8,128)S(1)} %add.108), channel_id=1, source_target_pairs={{0,16},{8,56},{16,0},{24,40},{32,48},{40,24},{48,32},{56,8},{1,17}... | collective-permute-start | bytes 294920 | tf_op jit(solution)/shard_map/ppermute | solution.py:172
  78.1 7.5 %collective-permute-start.7 = (f32[1,32,768]{2,1,0:T(8,128)S(1)}, f32[1,32,768]{2,1,0:T(8,128)S(1)}, u32[]{:S(2)}, u32[]{:S(2)}) collective-permute-start(f32[1,32,768]{2,1,0:T(8,128)S(1)} %add.98), channel_id=1, source_target_pairs={{0,48},{8,24},{16,32},{24,8},{32,16},{40,56},{48,0},{56,40},{1,49}... | collective-permute-start | bytes 294920 | tf_op jit(solution)/shard_map/ppermute | solution.py:172
  78.3 7.5 %collective-permute-start.21 = (f32[1,64,768]{2,1,0:T(8,128)S(1)}, f32[1,64,768]{2,1,0:T(8,128)S(1)}, u32[]{:S(2)}, u32[]{:S(2)}) collective-permute-start(f32[1,64,768]{2,1,0:T(8,128)S(1)} %pad_maximum_fusion.6), channel_id=1, source_target_pairs={{0,192},{8,72},{64,128},{72,8},{128,64},{136,200},{192,0},{200,136... | collective-permute-start | bytes 589832 | tf_op jit(solution)/shard_map/ppermute | solution.py:172
  79.9 14.8 %collective-permute-start.29 = (f32[2,128,768]{2,1,0:T(8,128)S(1)}, f32[2,128,768]{2,1,0:T(8,128)S(1)}, u32[]{:S(2)}, u32[]{:S(2)}) collective-permute-start(f32[2,128,768]{2,1,0:T(8,128)S(1)} %pad_maximum_fusion.1.w), channel_id=1, source_target_pairs={{0,64},{8,200},{64,0},{72,136},{128,192},{136,72},{192,128},{200,8... | collective-permute-start | bytes 2359304 | tf_op jit(solution)/shard_map/ppermute | solution.py:172
  83.0 12.3 %collective-permute-start.15 = (f32[4,128,384]{2,1,0:T(8,128)S(1)}, f32[4,128,384]{2,1,0:T(8,128)S(1)}, u32[]{:S(2)}, u32[]{:S(2)}) collective-permute-start(f32[4,128,384]{2,1,0:T(8,128)S(1)} %pad_maximum_fusion.q), channel_id=1, source_target_pairs={{0,2},{8,14},{2,0},{10,12},{4,6},{12,10},{6,4},{14,8},{1,3},{9,15}... | collective-permute-start | bytes 2359304 | tf_op jit(solution)/shard_map/ppermute | solution.py:171
  85.6 6.8 %collective-permute-start.8 = (f32[1,64,768]{2,1,0:T(8,128)S(1)}, f32[1,64,768]{2,1,0:T(8,128)S(1)}, u32[]{:S(2)}, u32[]{:S(2)}) collective-permute-start(f32[1,64,768]{2,1,0:T(8,128)S(1)} %pad_maximum_fusion.5), channel_id=1, source_target_pairs={{0,16},{8,56},{16,0},{24,40},{32,48},{40,24},{48,32},{56,8},{1,17}... | collective-permute-start | bytes 589832 | tf_op jit(solution)/shard_map/ppermute | solution.py:172
  85.8 13.0 %collective-permute-start.22 = (f32[1,128,768]{2,1,0:T(8,128)S(1)}, f32[1,128,768]{2,1,0:T(8,128)S(1)}, u32[]{:S(2)}, u32[]{:S(2)}) collective-permute-start(f32[1,128,768]{2,1,0:T(8,128)S(1)} %pad_maximum_fusion.3.w), channel_id=1, source_target_pairs={{0,64},{8,200},{64,0},{72,136},{128,192},{136,72},{192,128},{200,8... | collective-permute-start | bytes 1179656 | tf_op jit(solution)/shard_map/ppermute | solution.py:172
  92.5 10.4 %collective-permute-start.9 = (f32[1,128,768]{2,1,0:T(8,128)S(1)}, f32[1,128,768]{2,1,0:T(8,128)S(1)}, u32[]{:S(2)}, u32[]{:S(2)}) collective-permute-start(f32[1,128,768]{2,1,0:T(8,128)S(1)} %pad_maximum_fusion.2.w), channel_id=1, source_target_pairs={{0,64},{8,200},{64,0},{72,136},{128,192},{136,72},{192,128},{200,8... | collective-permute-start | bytes 1179656 | tf_op jit(solution)/shard_map/ppermute | solution.py:172
  104.2 6.5 %collective-permute-start.30 = (f32[192,768]{1,0:T(8,128)S(1)}, f32[192,768]{1,0:T(8,128)S(1)}, u32[]{:S(2)}, u32[]{:S(2)}) collective-permute-start(f32[192,768]{1,0:T(8,128)S(1)} %get-tuple-element.40), channel_id=1, source_target_pairs={{0,8},{8,0},{1,9},{9,1},{2,10},{10,2},{3,11},{11,3},{4,12},{12,4},... | collective-permute-start | bytes 1769480 | tf_op jit(solution)/shard_map/ppermute | solution.py:202
